TPU v7x, 256 devices: a whole 4x4x8 slice. The times are simulated.
256 devices in a mesh: blk: 32 (over x, z), head: 8 (over y, core).
Axes of the slice: x: 4, y: 4, z: 8, core: 2. Of those that a mesh axis runs over, the one named last changes fastest.
Arguments:
- queries: bfloat16 [8192, 3072], P('blk', 'head'), may hold values from -5 to 5
- keys: bfloat16 [8192, 3072], P('blk', 'head'), may hold values from -5 to 5
- values: bfloat16 [8192, 3072], P('blk', 'head'), may hold values from -5 to 5
- query_tangent: bfloat16 [8192, 3072], P('blk', 'head'), may hold values from -5 to 5
- key_tangent: bfloat16 [8192, 3072], P('blk', 'head'), may hold values from -5 to 5
- value_tangent: bfloat16 [8192, 3072], P('blk', 'head'), may hold values from -5 to 5
- tile_mask: int32 [24, 64, 64], P('head'), may hold values from 0 to 1, as said below
- block_frame: int32 [32], replicated, may hold values from 0 to 31, each once
- out_weight: bfloat16 [3072, 3072], P('head'), may hold values from -1.25 to 1.25
Outputs:
- attn_out: bfloat16 [8192, 3072], P(('blk', 'head'))
- tangent_out: bfloat16 [8192, 3072], P(('blk', 'head'))
Inputs may be any that keep to these rules, and one draw needn't show every extreme that they name: tile_mask[h, a, a] is 1 for every head and tile. `block_frame`: each frame block is held by exactly one index of blk.
All inputs are finite; a program needn't handle non-finite values.
Results may differ from a plain program's by a relative error of at most 0.02.
Values may be sent and summed in bfloat16 or wider, within the bound.
No kernel may reach another device: no remote copies, remote signals or barrier semaphores. Data moves between devices by JAX's collectives and lax.ppermute only.
A program may use at most 128 MiB of HBM per device.

v0:
```python
import jax
import jax.numpy as jnp
from jax import lax
from jax.sharding import PartitionSpec as P

TILE = 128


VERY_LOW = -1e30


def passed_along(block, axis, distance):
    devices = range(lax.axis_size(axis))
    route = [((i - distance) % len(devices), i) for i in devices]
    return lax.ppermute(block, axis, route)


def frame_lookup(block_frame, owners):
    matches = owners[:, None] == jnp.arange(block_frame.shape[0], dtype=jnp.int32)[None, :]
    return jnp.sum(jnp.where(matches, block_frame[None, :], 0), axis=1)


def body(
    queries,
    keys,
    values,
    query_tangent,
    key_tangent,
    value_tangent,
    tile_mask,
    block_frame,
    out_weight,
):
    tok_rows = queries.shape[0]
    heads_here = tile_mask.shape[0]
    head_width = queries.shape[1] // heads_here
    tile_count = tile_mask.shape[2]
    tiles_here = tok_rows // TILE
    scaling = head_width ** (-0.5)
    blocks = lax.axis_size("blk")
    position = lax.axis_index("blk")
    my_frame = frame_lookup(block_frame, jnp.reshape(position, (1,)))[0]
    row_mask = lax.dynamic_slice_in_dim(tile_mask, my_frame * tiles_here, tiles_here, 1).astype(
        jnp.float32
    )
    query_heads = queries.reshape(tok_rows, heads_here, head_width)
    qtan_heads = query_tangent.reshape(tok_rows, heads_here, head_width)

    def live_tiles_for(offset, count):
        places = offset + jnp.arange(count, dtype=jnp.int32)
        frames = frame_lookup(block_frame, places // tok_rows)
        key_tiles = frames * tiles_here + places % tok_rows // TILE
        one_hot = (key_tiles[:, None] == jnp.arange(tile_count, dtype=jnp.int32)[None, :]).astype(
            jnp.float32
        )
        return jnp.einsum("hrt,kt->hrk", row_mask, one_hot) > 0.5

    def accumulate(carried, pieces, live_tiles):
        count = pieces.shape[1]
        key_heads = pieces[0].reshape(count, heads_here, head_width)
        value_heads = pieces[1].reshape(count, heads_here, head_width)
        ktan_heads = pieces[2].reshape(count, heads_here, head_width)
        vtan_heads = pieces[3].reshape(count, heads_here, head_width)
        is_live = jnp.repeat(live_tiles, TILE, axis=1)
        scores = scaling * jnp.einsum(
            "qhd,khd->hqk", query_heads, key_heads, preferred_element_type=jnp.float32
        )
        tangent_scores = scaling * (
            jnp.einsum("qhd,khd->hqk", qtan_heads, key_heads, preferred_element_type=jnp.float32)
            + jnp.einsum(
                "qhd,khd->hqk", query_heads, ktan_heads, preferred_element_type=jnp.float32
            )
        )
        row_max, totals, drifts, sum_attn, sum_tangent = carried
        masked = jnp.where(is_live, scores, VERY_LOW)
        new_max = jnp.maximum(row_max, jnp.max(masked, axis=2))
        fading = jnp.exp(row_max - new_max)
        weights = jnp.where(is_live, jnp.exp(masked - new_max[:, :, None]), 0.0)
        scaled = weights * tangent_scores
        weights_low = weights.astype(jnp.bfloat16)
        scaled_low = scaled.astype(jnp.bfloat16)
        fading_rows = fading.T[:, :, None]
        sum_attn = sum_attn * fading_rows + jnp.einsum(
            "hqk,khd->qhd", weights_low, value_heads, preferred_element_type=jnp.float32
        )
        sum_tangent = (
            sum_tangent * fading_rows
            + jnp.einsum(
                "hqk,khd->qhd", scaled_low, value_heads, preferred_element_type=jnp.float32
            )
            + jnp.einsum(
                "hqk,khd->qhd", weights_low, vtan_heads, preferred_element_type=jnp.float32
            )
        )
        totals = totals * fading + jnp.sum(weights, axis=2)
        drifts = drifts * fading + jnp.sum(scaled, axis=2)
        return (new_max, totals, drifts, sum_attn, sum_tangent)

    def attend(carried, pieces, offset):
        live_tiles = live_tiles_for(offset, pieces.shape[1])
        return accumulate(carried, pieces, live_tiles)

    zero_rows = jnp.zeros((heads_here, tok_rows), jnp.float32)
    zero_sums = jnp.zeros((tok_rows, heads_here, head_width), jnp.float32)
    start_state = (
        jnp.full((heads_here, tok_rows), VERY_LOW, jnp.float32),
        zero_rows,
        zero_rows,
        zero_sums,
        zero_sums,
    )
    stacked = jnp.stack((keys, values, key_tangent, value_tangent))
    carried = attend(start_state, stacked, position * tok_rows)

    def onward(step_index, holding):
        current, pieces = holding
        pieces = passed_along(pieces, "blk", 1)
        source = (position - step_index) % blocks
        return (attend(current, pieces, source * tok_rows), pieces)

    carried, stacked_after = lax.fori_loop(1, blocks, onward, (carried, stacked))
    row_max, totals, drifts, sum_attn, sum_tangent = carried
    total_rows = totals.T[:, :, None]
    attn = sum_attn / total_rows
    attn_tangent = sum_tangent / total_rows - drifts.T[:, :, None] / total_rows * attn
    mixed = attn.reshape(tok_rows, heads_here * head_width).astype(jnp.bfloat16)
    mixed_tangent = attn_tangent.reshape(tok_rows, heads_here * head_width).astype(jnp.bfloat16)
    summed = lax.psum_scatter(
        jnp.concatenate(
            (
                jnp.dot(mixed, out_weight, preferred_element_type=jnp.float32),
                jnp.dot(mixed_tangent, out_weight, preferred_element_type=jnp.float32),
            ),
            axis=1,
        ).astype(jnp.bfloat16),
        "head",
        scatter_dimension=0,
        tiled=True,
    ).astype(jnp.float32)
    width_out = out_weight.shape[1]
    return (summed[:, :width_out].astype(jnp.bfloat16), summed[:, width_out:].astype(jnp.bfloat16))


def solution(mesh):
    in_specs = (
        P("blk", "head"),
        P("blk", "head"),
        P("blk", "head"),
        P("blk", "head"),
        P("blk", "head"),
        P("blk", "head"),
        P("head", None, None),
        P(),
        P("head", None),
    )
    out_specs = (P(("blk", "head"), None), P(("blk", "head"), None))
    return jax.shard_map(body, mesh=mesh, in_specs=in_specs, out_specs=out_specs, check_vma=False)
```

profile of v0, /device:TPU:1, one launch (start us, length us, event | category | flops | bytes accessed | tf_op | source)
XLA Modules:
  0.0 784.1 jit_solution(2852807309217203881)
XLA Ops:
  7.2 1.5 fusion.36
  12.0 1.1 copy.83
  13.0 1.1 copy.94
  14.1 1.7 copy.91
  15.8 1.7 copy.99
  17.9 1.7 copy.88
  19.6 1.1 copy.107
  20.7 1.3 fusion.46
  23.1 1.2 fusion.21
  24.6 1.1 fusion.23
  25.7 1.0 pad_maximum_fusion.1
  26.7 682.2 %while.26 = (s32[]{:T(128)}, f32[3,256]{1,0:T(4,128)S(1)}, f32[3,256]{1,0:T(4,128)S(1)}, f32[3,256]{1,0:T(4,128)S(1)}, f32[256,3,128]{2,0,1:T(8,128)}, /*index=5...) while((s32[]{:T(128)}, f32[3,256]{1,0:T(4,128)S(1)}, ...), condition=%wide.region_10.11_spmd, body=%wide.region_5.10_spmd.sunk | while | flops 306470400 | bytes 24660288 | solution.py:121
  26.7 2.5 collective-permute-start
  30.5 22.4 %collective-permute-done = bf16[4,256,384]{1,2,0:T(8,128)(2,1)S(1)} collective-permute-done((bf16[4,256,384]{1,2,0:T(8,128)(2,1)}, bf16[4,256,384]{1,2,0:T(8,128)(2,1)S(1)}, u32[]{:S(2)}, u32[]{:S(2)}) %collective-permute-start) | collective-permute-done | bytes 786464 | tf_op jit(solution)/shard_map/while/body/eval_jaxpr/ppermute | solution.py:15
  55.8 0.9 copy.158
  58.1 20.1 %collective-permute-done = bf16[4,256,384]{1,2,0:T(8,128)(2,1)S(1)} collective-permute-done((bf16[4,256,384]{1,2,0:T(8,128)(2,1)}, bf16[4,256,384]{1,2,0:T(8,128)(2,1)S(1)}, u32[]{:S(2)}, u32[]{:S(2)}) %collective-permute-start) | collective-permute-done | bytes 786464 | tf_op jit(solution)/shard_map/while/body/eval_jaxpr/ppermute | solution.py:15
  81.0 0.9 copy.158
  83.3 19.1 %collective-permute-done = bf16[4,256,384]{1,2,0:T(8,128)(2,1)S(1)} collective-permute-done((bf16[4,256,384]{1,2,0:T(8,128)(2,1)}, bf16[4,256,384]{1,2,0:T(8,128)(2,1)S(1)}, u32[]{:S(2)}, u32[]{:S(2)}) %collective-permute-start) | collective-permute-done | bytes 786464 | tf_op jit(solution)/shard_map/while/body/eval_jaxpr/ppermute | solution.py:15
  105.4 0.9 copy.158
  107.7 18.2 %collective-permute-done = bf16[4,256,384]{1,2,0:T(8,128)(2,1)S(1)} collective-permute-done((bf16[4,256,384]{1,2,0:T(8,128)(2,1)}, bf16[4,256,384]{1,2,0:T(8,128)(2,1)S(1)}, u32[]{:S(2)}, u32[]{:S(2)}) %collective-permute-start) | collective-permute-done | bytes 786464 | tf_op jit(solution)/shard_map/while/body/eval_jaxpr/ppermute | solution.py:15
  128.9 0.9 copy.158
  131.1 17.3 %collective-permute-done = bf16[4,256,384]{1,2,0:T(8,128)(2,1)S(1)} collective-permute-done((bf16[4,256,384]{1,2,0:T(8,128)(2,1)}, bf16[4,256,384]{1,2,0:T(8,128)(2,1)S(1)}, u32[]{:S(2)}, u32[]{:S(2)}) %collective-permute-start) | collective-permute-done | bytes 786464 | tf_op jit(solution)/shard_map/while/body/eval_jaxpr/ppermute | solution.py:15
  151.4 0.9 copy.158
  153.7 16.4 %collective-permute-done = bf16[4,256,384]{1,2,0:T(8,128)(2,1)S(1)} collective-permute-done((bf16[4,256,384]{1,2,0:T(8,128)(2,1)}, bf16[4,256,384]{1,2,0:T(8,128)(2,1)S(1)}, u32[]{:S(2)}, u32[]{:S(2)}) %collective-permute-start) | collective-permute-done | bytes 786464 | tf_op jit(solution)/shard_map/while/body/eval_jaxpr/ppermute | solution.py:15
  173.0 0.9 copy.158
  175.3 15.4 %collective-permute-done = bf16[4,256,384]{1,2,0:T(8,128)(2,1)S(1)} collective-permute-done((bf16[4,256,384]{1,2,0:T(8,128)(2,1)}, bf16[4,256,384]{1,2,0:T(8,128)(2,1)S(1)}, u32[]{:S(2)}, u32[]{:S(2)}) %collective-permute-start) | collective-permute-done | bytes 786464 | tf_op jit(solution)/shard_map/while/body/eval_jaxpr/ppermute | solution.py:15
  193.6 0.9 copy.158
  195.9 14.5 %collective-permute-done = bf16[4,256,384]{1,2,0:T(8,128)(2,1)S(1)} collective-permute-done((bf16[4,256,384]{1,2,0:T(8,128)(2,1)}, bf16[4,256,384]{1,2,0:T(8,128)(2,1)S(1)}, u32[]{:S(2)}, u32[]{:S(2)}) %collective-permute-start) | collective-permute-done | bytes 786464 | tf_op jit(solution)/shard_map/while/body/eval_jaxpr/ppermute | solution.py:15
  213.4 0.9 copy.158
  215.7 13.6 %collective-permute-done = bf16[4,256,384]{1,2,0:T(8,128)(2,1)S(1)} collective-permute-done((bf16[4,256,384]{1,2,0:T(8,128)(2,1)}, bf16[4,256,384]{1,2,0:T(8,128)(2,1)S(1)}, u32[]{:S(2)}, u32[]{:S(2)}) %collective-permute-start) | collective-permute-done | bytes 786464 | tf_op jit(solution)/shard_map/while/body/eval_jaxpr/ppermute | solution.py:15
  232.2 0.9 copy.158
  234.5 13.1 %collective-permute-done = bf16[4,256,384]{1,2,0:T(8,128)(2,1)S(1)} collective-permute-done((bf16[4,256,384]{1,2,0:T(8,128)(2,1)}, bf16[4,256,384]{1,2,0:T(8,128)(2,1)S(1)}, u32[]{:S(2)}, u32[]{:S(2)}) %collective-permute-start) | collective-permute-done | bytes 786464 | tf_op jit(solution)/shard_map/while/body/eval_jaxpr/ppermute | solution.py:15
  250.5 0.9 copy.158
  252.8 13.1 %collective-permute-done = bf16[4,256,384]{1,2,0:T(8,128)(2,1)S(1)} collective-permute-done((bf16[4,256,384]{1,2,0:T(8,128)(2,1)}, bf16[4,256,384]{1,2,0:T(8,128)(2,1)S(1)}, u32[]{:S(2)}, u32[]{:S(2)}) %collective-permute-start) | collective-permute-done | bytes 786464 | tf_op jit(solution)/shard_map/while/body/eval_jaxpr/ppermute | solution.py:15
  271.2 13.4 %collective-permute-done = bf16[4,256,384]{1,2,0:T(8,128)(2,1)S(1)} collective-permute-done((bf16[4,256,384]{1,2,0:T(8,128)(2,1)}, bf16[4,256,384]{1,2,0:T(8,128)(2,1)S(1)}, u32[]{:S(2)}, u32[]{:S(2)}) %collective-permute-start) | collective-permute-done | bytes 786464 | tf_op jit(solution)/shard_map/while/body/eval_jaxpr/ppermute | solution.py:15
  289.8 14.5 %collective-permute-done = bf16[4,256,384]{1,2,0:T(8,128)(2,1)S(1)} collective-permute-done((bf16[4,256,384]{1,2,0:T(8,128)(2,1)}, bf16[4,256,384]{1,2,0:T(8,128)(2,1)S(1)}, u32[]{:S(2)}, u32[]{:S(2)}) %collective-permute-start) | collective-permute-done | bytes 786464 | tf_op jit(solution)/shard_map/while/body/eval_jaxpr/ppermute | solution.py:15
  309.5 15.6 %collective-permute-done = bf16[4,256,384]{1,2,0:T(8,128)(2,1)S(1)} collective-permute-done((bf16[4,256,384]{1,2,0:T(8,128)(2,1)}, bf16[4,256,384]{1,2,0:T(8,128)(2,1)S(1)}, u32[]{:S(2)}, u32[]{:S(2)}) %collective-permute-start) | collective-permute-done | bytes 786464 | tf_op jit(solution)/shard_map/while/body/eval_jaxpr/ppermute | solution.py:15
  330.3 16.7 %collective-permute-done = bf16[4,256,384]{1,2,0:T(8,128)(2,1)S(1)} collective-permute-done((bf16[4,256,384]{1,2,0:T(8,128)(2,1)}, bf16[4,256,384]{1,2,0:T(8,128)(2,1)S(1)}, u32[]{:S(2)}, u32[]{:S(2)}) %collective-permute-start) | collective-permute-done | bytes 786464 | tf_op jit(solution)/shard_map/while/body/eval_jaxpr/ppermute | solution.py:15
  349.9 0.9 copy.158
  352.2 17.7 %collective-permute-done = bf16[4,256,384]{1,2,0:T(8,128)(2,1)S(1)} collective-permute-done((bf16[4,256,384]{1,2,0:T(8,128)(2,1)}, bf16[4,256,384]{1,2,0:T(8,128)(2,1)S(1)}, u32[]{:S(2)}, u32[]{:S(2)}) %collective-permute-start) | collective-permute-done | bytes 786464 | tf_op jit(solution)/shard_map/while/body/eval_jaxpr/ppermute | solution.py:15
  375.2 18.8 %collective-permute-done = bf16[4,256,384]{1,2,0:T(8,128)(2,1)S(1)} collective-permute-done((bf16[4,256,384]{1,2,0:T(8,128)(2,1)}, bf16[4,256,384]{1,2,0:T(8,128)(2,1)S(1)}, u32[]{:S(2)}, u32[]{:S(2)}) %collective-permute-start) | collective-permute-done | bytes 786464 | tf_op jit(solution)/shard_map/while/body/eval_jaxpr/ppermute | solution.py:15
  399.3 19.9 %collective-permute-done = bf16[4,256,384]{1,2,0:T(8,128)(2,1)S(1)} collective-permute-done((bf16[4,256,384]{1,2,0:T(8,128)(2,1)}, bf16[4,256,384]{1,2,0:T(8,128)(2,1)S(1)}, u32[]{:S(2)}, u32[]{:S(2)}) %collective-permute-start) | collective-permute-done | bytes 786464 | tf_op jit(solution)/shard_map/while/body/eval_jaxpr/ppermute | solution.py:15
  424.4 21.0 %collective-permute-done = bf16[4,256,384]{1,2,0:T(8,128)(2,1)S(1)} collective-permute-done((bf16[4,256,384]{1,2,0:T(8,128)(2,1)}, bf16[4,256,384]{1,2,0:T(8,128)(2,1)S(1)}, u32[]{:S(2)}, u32[]{:S(2)}) %collective-permute-start) | collective-permute-done | bytes 786464 | tf_op jit(solution)/shard_map/while/body/eval_jaxpr/ppermute | solution.py:15
  448.3 0.9 copy.158
  450.6 21.2 %collective-permute-done = bf16[4,256,384]{1,2,0:T(8,128)(2,1)S(1)} collective-permute-done((bf16[4,256,384]{1,2,0:T(8,128)(2,1)}, bf16[4,256,384]{1,2,0:T(8,128)(2,1)S(1)}, u32[]{:S(2)}, u32[]{:S(2)}) %collective-permute-start) | collective-permute-done | bytes 786464 | tf_op jit(solution)/shard_map/while/body/eval_jaxpr/ppermute | solution.py:15
  477.0 20.3 %collective-permute-done = bf16[4,256,384]{1,2,0:T(8,128)(2,1)S(1)} collective-permute-done((bf16[4,256,384]{1,2,0:T(8,128)(2,1)}, bf16[4,256,384]{1,2,0:T(8,128)(2,1)S(1)}, u32[]{:S(2)}, u32[]{:S(2)}) %collective-permute-start) | collective-permute-done | bytes 786464 | tf_op jit(solution)/shard_map/while/body/eval_jaxpr/ppermute | solution.py:15
  502.5 19.3 %collective-permute-done = bf16[4,256,384]{1,2,0:T(8,128)(2,1)S(1)} collective-permute-done((bf16[4,256,384]{1,2,0:T(8,128)(2,1)}, bf16[4,256,384]{1,2,0:T(8,128)(2,1)S(1)}, u32[]{:S(2)}, u32[]{:S(2)}) %collective-permute-start) | collective-permute-done | bytes 786464 | tf_op jit(solution)/shard_map/while/body/eval_jaxpr/ppermute | solution.py:15
  527.1 18.4 %collective-permute-done = bf16[4,256,384]{1,2,0:T(8,128)(2,1)S(1)} collective-permute-done((bf16[4,256,384]{1,2,0:T(8,128)(2,1)}, bf16[4,256,384]{1,2,0:T(8,128)(2,1)S(1)}, u32[]{:S(2)}, u32[]{:S(2)}) %collective-permute-start) | collective-permute-done | bytes 786464 | tf_op jit(solution)/shard_map/while/body/eval_jaxpr/ppermute | solution.py:15
  550.7 17.5 %collective-permute-done = bf16[4,256,384]{1,2,0:T(8,128)(2,1)S(1)} collective-permute-done((bf16[4,256,384]{1,2,0:T(8,128)(2,1)}, bf16[4,256,384]{1,2,0:T(8,128)(2,1)S(1)}, u32[]{:S(2)}, u32[]{:S(2)}) %collective-permute-start) | collective-permute-done | bytes 786464 | tf_op jit(solution)/shard_map/while/body/eval_jaxpr/ppermute | solution.py:15
  573.4 16.6 %collective-permute-done = bf16[4,256,384]{1,2,0:T(8,128)(2,1)S(1)} collective-permute-done((bf16[4,256,384]{1,2,0:T(8,128)(2,1)}, bf16[4,256,384]{1,2,0:T(8,128)(2,1)S(1)}, u32[]{:S(2)}, u32[]{:S(2)}) %collective-permute-start) | collective-permute-done | bytes 786464 | tf_op jit(solution)/shard_map/while/body/eval_jaxpr/ppermute | solution.py:15
  595.2 15.6 %collective-permute-done = bf16[4,256,384]{1,2,0:T(8,128)(2,1)S(1)} collective-permute-done((bf16[4,256,384]{1,2,0:T(8,128)(2,1)}, bf16[4,256,384]{1,2,0:T(8,128)(2,1)S(1)}, u32[]{:S(2)}, u32[]{:S(2)}) %collective-permute-start) | collective-permute-done | bytes 786464 | tf_op jit(solution)/shard_map/while/body/eval_jaxpr/ppermute | solution.py:15
  616.1 14.7 %collective-permute-done = bf16[4,256,384]{1,2,0:T(8,128)(2,1)S(1)} collective-permute-done((bf16[4,256,384]{1,2,0:T(8,128)(2,1)}, bf16[4,256,384]{1,2,0:T(8,128)(2,1)S(1)}, u32[]{:S(2)}, u32[]{:S(2)}) %collective-permute-start) | collective-permute-done | bytes 786464 | tf_op jit(solution)/shard_map/while/body/eval_jaxpr/ppermute | solution.py:15
  633.7 0.9 copy.158
  636.0 13.8 %collective-permute-done = bf16[4,256,384]{1,2,0:T(8,128)(2,1)S(1)} collective-permute-done((bf16[4,256,384]{1,2,0:T(8,128)(2,1)}, bf16[4,256,384]{1,2,0:T(8,128)(2,1)S(1)}, u32[]{:S(2)}, u32[]{:S(2)}) %collective-permute-start) | collective-permute-done | bytes 786464 | tf_op jit(solution)/shard_map/while/body/eval_jaxpr/ppermute | solution.py:15
  655.1 13.1 %collective-permute-done = bf16[4,256,384]{1,2,0:T(8,128)(2,1)S(1)} collective-permute-done((bf16[4,256,384]{1,2,0:T(8,128)(2,1)}, bf16[4,256,384]{1,2,0:T(8,128)(2,1)S(1)}, u32[]{:S(2)}, u32[]{:S(2)}) %collective-permute-start) | collective-permute-done | bytes 786464 | tf_op jit(solution)/shard_map/while/body/eval_jaxpr/ppermute | solution.py:15
  673.4 13.1 %collective-permute-done = bf16[4,256,384]{1,2,0:T(8,128)(2,1)S(1)} collective-permute-done((bf16[4,256,384]{1,2,0:T(8,128)(2,1)}, bf16[4,256,384]{1,2,0:T(8,128)(2,1)S(1)}, u32[]{:S(2)}, u32[]{:S(2)}) %collective-permute-start) | collective-permute-done | bytes 786464 | tf_op jit(solution)/shard_map/while/body/eval_jaxpr/ppermute | solution.py:15
  691.7 13.2 %collective-permute-done = bf16[4,256,384]{1,2,0:T(8,128)(2,1)S(1)} collective-permute-done((bf16[4,256,384]{1,2,0:T(8,128)(2,1)}, bf16[4,256,384]{1,2,0:T(8,128)(2,1)S(1)}, u32[]{:S(2)}, u32[]{:S(2)}) %collective-permute-start) | collective-permute-done | bytes 786464 | tf_op jit(solution)/shard_map/while/body/eval_jaxpr/ppermute | solution.py:15
  708.9 1.2 copy.108
  710.0 1.2 copy.109
  711.3 1.0 convolution_convert_fusion
  712.3 1.0 convolution_convert_fusion.1
  713.3 1.9 pad_maximum_fusion
  715.3 60.2 %reduce-scatter.2.cloned.1.call-done = bf16[32,6144]{1,0:T(8,128)(2,1)} async-done(((bf16[256,6144]{1,0:T(8,128)(2,1)}), bf16[32,6144]{1,0:T(8,128)(2,1)}) %reduce-scatter.2.cloned.1.call-update) | async-done | bytes 393232 | tf_op jit(solution)/shard_map/reduce_scatter | solution.py:128
  775.5 1.8 fusion.42
  (885 shorter events, 151.4 us)
Async XLA Ops:
  7.2 704.2 %copy-start = (bf16[384,3072]{1,0:T(8,128)(2,1)S(1)}, bf16[384,3072]{1,0:T(8,128)(2,1)}, u32[]{:S(2)}) copy-start(bf16[384,3072]{1,0:T(8,128)(2,1)} %param.19) | copy-start | bytes 7077892
  7.2 10.4 %copy-start.7 = (bf16[256,384]{1,0:T(8,128)(2,1)S(1)}, bf16[256,384]{1,0:T(8,128)(2,1)}, u32[]{:S(2)}) copy-start(bf16[256,384]{1,0:T(8,128)(2,1)} %param.11) | copy-start | bytes 589828
  7.2 768.3 %reduce-scatter.2.cloned.1.call-start = ((), (), s32[]{:S(2)}) async-start(), calls=%async_computation.1 | async-start | bytes 3538944 | tf_op jit(solution)/shard_map/reduce_scatter | solution.py:128
  20.7 1.8 copy-start.5
  22.6 2.0 copy-start.6
  24.2 2.5 copy-start.8
  26.7 26.1 %collective-permute-start = (bf16[4,256,384]{1,2,0:T(8,128)(2,1)}, bf16[4,256,384]{1,2,0:T(8,128)(2,1)S(1)}, u32[]{:S(2)}, u32[]{:S(2)}) collective-permute-start(bf16[4,256,384]{1,2,0:T(8,128)(2,1)} %get-tuple-element.538), channel_id=1, source_target_pairs={{248,0},{0,8},{8,16},{16,24},{24,32},{32,40},{40,48},{48,56},{56,6... | collective-permute-start | bytes 2359304 | tf_op jit(solution)/shard_map/while/body/eval_jaxpr/ppermute | solution.py:15
  55.1 1.5 copy-start.4
  56.8 21.3 %collective-permute-start = (bf16[4,256,384]{1,2,0:T(8,128)(2,1)}, bf16[4,256,384]{1,2,0:T(8,128)(2,1)S(1)}, u32[]{:S(2)}, u32[]{:S(2)}) collective-permute-start(bf16[4,256,384]{1,2,0:T(8,128)(2,1)} %get-tuple-element.538), channel_id=1, source_target_pairs={{248,0},{0,8},{8,16},{16,24},{24,32},{32,40},{40,48},{48,56},{56,6... | collective-permute-start | bytes 2359304 | tf_op jit(solution)/shard_map/while/body/eval_jaxpr/ppermute | solution.py:15
  80.4 1.5 copy-start.4
  82.1 20.4 %collective-permute-start = (bf16[4,256,384]{1,2,0:T(8,128)(2,1)}, bf16[4,256,384]{1,2,0:T(8,128)(2,1)S(1)}, u32[]{:S(2)}, u32[]{:S(2)}) collective-permute-start(bf16[4,256,384]{1,2,0:T(8,128)(2,1)} %get-tuple-element.538), channel_id=1, source_target_pairs={{248,0},{0,8},{8,16},{16,24},{24,32},{32,40},{40,48},{48,56},{56,6... | collective-permute-start | bytes 2359304 | tf_op jit(solution)/shard_map/while/body/eval_jaxpr/ppermute | solution.py:15
  104.8 1.5 copy-start.4
  106.4 19.5 %collective-permute-start = (bf16[4,256,384]{1,2,0:T(8,128)(2,1)}, bf16[4,256,384]{1,2,0:T(8,128)(2,1)S(1)}, u32[]{:S(2)}, u32[]{:S(2)}) collective-permute-start(bf16[4,256,384]{1,2,0:T(8,128)(2,1)} %get-tuple-element.538), channel_id=1, source_target_pairs={{248,0},{0,8},{8,16},{16,24},{24,32},{32,40},{40,48},{48,56},{56,6... | collective-permute-start | bytes 2359304 | tf_op jit(solution)/shard_map/while/body/eval_jaxpr/ppermute | solution.py:15
  129.9 18.6 %collective-permute-start = (bf16[4,256,384]{1,2,0:T(8,128)(2,1)}, bf16[4,256,384]{1,2,0:T(8,128)(2,1)S(1)}, u32[]{:S(2)}, u32[]{:S(2)}) collective-permute-start(bf16[4,256,384]{1,2,0:T(8,128)(2,1)} %get-tuple-element.538), channel_id=1, source_target_pairs={{248,0},{0,8},{8,16},{16,24},{24,32},{32,40},{40,48},{48,56},{56,6... | collective-permute-start | bytes 2359304 | tf_op jit(solution)/shard_map/while/body/eval_jaxpr/ppermute | solution.py:15
  150.8 1.5 copy-start.4
  152.4 17.6 %collective-permute-start = (bf16[4,256,384]{1,2,0:T(8,128)(2,1)}, bf16[4,256,384]{1,2,0:T(8,128)(2,1)S(1)}, u32[]{:S(2)}, u32[]{:S(2)}) collective-permute-start(bf16[4,256,384]{1,2,0:T(8,128)(2,1)} %get-tuple-element.538), channel_id=1, source_target_pairs={{248,0},{0,8},{8,16},{16,24},{24,32},{32,40},{40,48},{48,56},{56,6... | collective-permute-start | bytes 2359304 | tf_op jit(solution)/shard_map/while/body/eval_jaxpr/ppermute | solution.py:15
  172.3 1.5 copy-start.4
  174.0 16.7 %collective-permute-start = (bf16[4,256,384]{1,2,0:T(8,128)(2,1)}, bf16[4,256,384]{1,2,0:T(8,128)(2,1)S(1)}, u32[]{:S(2)}, u32[]{:S(2)}) collective-permute-start(bf16[4,256,384]{1,2,0:T(8,128)(2,1)} %get-tuple-element.538), channel_id=1, source_target_pairs={{248,0},{0,8},{8,16},{16,24},{24,32},{32,40},{40,48},{48,56},{56,6... | collective-permute-start | bytes 2359304 | tf_op jit(solution)/shard_map/while/body/eval_jaxpr/ppermute | solution.py:15
  194.7 15.8 %collective-permute-start = (bf16[4,256,384]{1,2,0:T(8,128)(2,1)}, bf16[4,256,384]{1,2,0:T(8,128)(2,1)S(1)}, u32[]{:S(2)}, u32[]{:S(2)}) collective-permute-start(bf16[4,256,384]{1,2,0:T(8,128)(2,1)} %get-tuple-element.538), channel_id=1, source_target_pairs={{248,0},{0,8},{8,16},{16,24},{24,32},{32,40},{40,48},{48,56},{56,6... | collective-permute-start | bytes 2359304 | tf_op jit(solution)/shard_map/while/body/eval_jaxpr/ppermute | solution.py:15
  212.8 1.5 copy-start.4
  214.4 14.9 %collective-permute-start = (bf16[4,256,384]{1,2,0:T(8,128)(2,1)}, bf16[4,256,384]{1,2,0:T(8,128)(2,1)S(1)}, u32[]{:S(2)}, u32[]{:S(2)}) collective-permute-start(bf16[4,256,384]{1,2,0:T(8,128)(2,1)} %get-tuple-element.538), channel_id=1, source_target_pairs={{248,0},{0,8},{8,16},{16,24},{24,32},{32,40},{40,48},{48,56},{56,6... | collective-permute-start | bytes 2359304 | tf_op jit(solution)/shard_map/while/body/eval_jaxpr/ppermute | solution.py:15
  231.6 1.5 copy-start.4
  233.2 14.4 %collective-permute-start = (bf16[4,256,384]{1,2,0:T(8,128)(2,1)}, bf16[4,256,384]{1,2,0:T(8,128)(2,1)S(1)}, u32[]{:S(2)}, u32[]{:S(2)}) collective-permute-start(bf16[4,256,384]{1,2,0:T(8,128)(2,1)} %get-tuple-element.538), channel_id=1, source_target_pairs={{248,0},{0,8},{8,16},{16,24},{24,32},{32,40},{40,48},{48,56},{56,6... | collective-permute-start | bytes 2359304 | tf_op jit(solution)/shard_map/while/body/eval_jaxpr/ppermute | solution.py:15
  249.9 1.5 copy-start.4
  251.5 14.4 %collective-permute-start = (bf16[4,256,384]{1,2,0:T(8,128)(2,1)}, bf16[4,256,384]{1,2,0:T(8,128)(2,1)S(1)}, u32[]{:S(2)}, u32[]{:S(2)}) collective-permute-start(bf16[4,256,384]{1,2,0:T(8,128)(2,1)} %get-tuple-element.538), channel_id=1, source_target_pairs={{248,0},{0,8},{8,16},{16,24},{24,32},{32,40},{40,48},{48,56},{56,6... | collective-permute-start | bytes 2359304 | tf_op jit(solution)/shard_map/while/body/eval_jaxpr/ppermute | solution.py:15
  268.2 1.5 copy-start.4
  269.9 14.7 %collective-permute-start = (bf16[4,256,384]{1,2,0:T(8,128)(2,1)}, bf16[4,256,384]{1,2,0:T(8,128)(2,1)S(1)}, u32[]{:S(2)}, u32[]{:S(2)}) collective-permute-start(bf16[4,256,384]{1,2,0:T(8,128)(2,1)} %get-tuple-element.538), channel_id=1, source_target_pairs={{248,0},{0,8},{8,16},{16,24},{24,32},{32,40},{40,48},{48,56},{56,6... | collective-permute-start | bytes 2359304 | tf_op jit(solution)/shard_map/while/body/eval_jaxpr/ppermute | solution.py:15
  286.9 1.5 copy-start.4
  288.5 15.8 %collective-permute-start = (bf16[4,256,384]{1,2,0:T(8,128)(2,1)}, bf16[4,256,384]{1,2,0:T(8,128)(2,1)S(1)}, u32[]{:S(2)}, u32[]{:S(2)}) collective-permute-start(bf16[4,256,384]{1,2,0:T(8,128)(2,1)} %get-tuple-element.538), channel_id=1, source_target_pairs={{248,0},{0,8},{8,16},{16,24},{24,32},{32,40},{40,48},{48,56},{56,6... | collective-permute-start | bytes 2359304 | tf_op jit(solution)/shard_map/while/body/eval_jaxpr/ppermute | solution.py:15
  306.6 1.5 copy-start.4
  308.2 16.9 %collective-permute-start = (bf16[4,256,384]{1,2,0:T(8,128)(2,1)}, bf16[4,256,384]{1,2,0:T(8,128)(2,1)S(1)}, u32[]{:S(2)}, u32[]{:S(2)}) collective-permute-start(bf16[4,256,384]{1,2,0:T(8,128)(2,1)} %get-tuple-element.538), channel_id=1, source_target_pairs={{248,0},{0,8},{8,16},{16,24},{24,32},{32,40},{40,48},{48,56},{56,6... | collective-permute-start | bytes 2359304 | tf_op jit(solution)/shard_map/while/body/eval_jaxpr/ppermute | solution.py:15
  327.4 1.5 copy-start.4
  329.1 17.9 %collective-permute-start = (bf16[4,256,384]{1,2,0:T(8,128)(2,1)}, bf16[4,256,384]{1,2,0:T(8,128)(2,1)S(1)}, u32[]{:S(2)}, u32[]{:S(2)}) collective-permute-start(bf16[4,256,384]{1,2,0:T(8,128)(2,1)} %get-tuple-element.538), channel_id=1, source_target_pairs={{248,0},{0,8},{8,16},{16,24},{24,32},{32,40},{40,48},{48,56},{56,6... | collective-permute-start | bytes 2359304 | tf_op jit(solution)/shard_map/while/body/eval_jaxpr/ppermute | solution.py:15
  349.3 1.5 copy-start.4
  350.9 19.0 %collective-permute-start = (bf16[4,256,384]{1,2,0:T(8,128)(2,1)}, bf16[4,256,384]{1,2,0:T(8,128)(2,1)S(1)}, u32[]{:S(2)}, u32[]{:S(2)}) collective-permute-start(bf16[4,256,384]{1,2,0:T(8,128)(2,1)} %get-tuple-element.538), channel_id=1, source_target_pairs={{248,0},{0,8},{8,16},{16,24},{24,32},{32,40},{40,48},{48,56},{56,6... | collective-permute-start | bytes 2359304 | tf_op jit(solution)/shard_map/while/body/eval_jaxpr/ppermute | solution.py:15
  372.3 1.5 copy-start.4
  373.9 20.1 %collective-permute-start = (bf16[4,256,384]{1,2,0:T(8,128)(2,1)}, bf16[4,256,384]{1,2,0:T(8,128)(2,1)S(1)}, u32[]{:S(2)}, u32[]{:S(2)}) collective-permute-start(bf16[4,256,384]{1,2,0:T(8,128)(2,1)} %get-tuple-element.538), channel_id=1, source_target_pairs={{248,0},{0,8},{8,16},{16,24},{24,32},{32,40},{40,48},{48,56},{56,6... | collective-permute-start | bytes 2359304 | tf_op jit(solution)/shard_map/while/body/eval_jaxpr/ppermute | solution.py:15
  398.0 21.2 %collective-permute-start = (bf16[4,256,384]{1,2,0:T(8,128)(2,1)}, bf16[4,256,384]{1,2,0:T(8,128)(2,1)S(1)}, u32[]{:S(2)}, u32[]{:S(2)}) collective-permute-start(bf16[4,256,384]{1,2,0:T(8,128)(2,1)} %get-tuple-element.538), channel_id=1, source_target_pairs={{248,0},{0,8},{8,16},{16,24},{24,32},{32,40},{40,48},{48,56},{56,6... | collective-permute-start | bytes 2359304 | tf_op jit(solution)/shard_map/while/body/eval_jaxpr/ppermute | solution.py:15
  421.5 1.5 copy-start.4
  423.1 22.3 %collective-permute-start = (bf16[4,256,384]{1,2,0:T(8,128)(2,1)}, bf16[4,256,384]{1,2,0:T(8,128)(2,1)S(1)}, u32[]{:S(2)}, u32[]{:S(2)}) collective-permute-start(bf16[4,256,384]{1,2,0:T(8,128)(2,1)} %get-tuple-element.538), channel_id=1, source_target_pairs={{248,0},{0,8},{8,16},{16,24},{24,32},{32,40},{40,48},{48,56},{56,6... | collective-permute-start | bytes 2359304 | tf_op jit(solution)/shard_map/while/body/eval_jaxpr/ppermute | solution.py:15
  447.7 1.5 copy-start.4
  449.3 22.5 %collective-permute-start = (bf16[4,256,384]{1,2,0:T(8,128)(2,1)}, bf16[4,256,384]{1,2,0:T(8,128)(2,1)S(1)}, u32[]{:S(2)}, u32[]{:S(2)}) collective-permute-start(bf16[4,256,384]{1,2,0:T(8,128)(2,1)} %get-tuple-element.538), channel_id=1, source_target_pairs={{248,0},{0,8},{8,16},{16,24},{24,32},{32,40},{40,48},{48,56},{56,6... | collective-permute-start | bytes 2359304 | tf_op jit(solution)/shard_map/while/body/eval_jaxpr/ppermute | solution.py:15
  474.1 1.5 copy-start.4
  475.7 21.5 %collective-permute-start = (bf16[4,256,384]{1,2,0:T(8,128)(2,1)}, bf16[4,256,384]{1,2,0:T(8,128)(2,1)S(1)}, u32[]{:S(2)}, u32[]{:S(2)}) collective-permute-start(bf16[4,256,384]{1,2,0:T(8,128)(2,1)} %get-tuple-element.538), channel_id=1, source_target_pairs={{248,0},{0,8},{8,16},{16,24},{24,32},{32,40},{40,48},{48,56},{56,6... | collective-permute-start | bytes 2359304 | tf_op jit(solution)/shard_map/while/body/eval_jaxpr/ppermute | solution.py:15
  499.6 1.5 copy-start.4
  501.2 20.6 %collective-permute-start = (bf16[4,256,384]{1,2,0:T(8,128)(2,1)}, bf16[4,256,384]{1,2,0:T(8,128)(2,1)S(1)}, u32[]{:S(2)}, u32[]{:S(2)}) collective-permute-start(bf16[4,256,384]{1,2,0:T(8,128)(2,1)} %get-tuple-element.538), channel_id=1, source_target_pairs={{248,0},{0,8},{8,16},{16,24},{24,32},{32,40},{40,48},{48,56},{56,6... | collective-permute-start | bytes 2359304 | tf_op jit(solution)/shard_map/while/body/eval_jaxpr/ppermute | solution.py:15
  524.2 1.5 copy-start.4
  525.8 19.7 %collective-permute-start = (bf16[4,256,384]{1,2,0:T(8,128)(2,1)}, bf16[4,256,384]{1,2,0:T(8,128)(2,1)S(1)}, u32[]{:S(2)}, u32[]{:S(2)}) collective-permute-start(bf16[4,256,384]{1,2,0:T(8,128)(2,1)} %get-tuple-element.538), channel_id=1, source_target_pairs={{248,0},{0,8},{8,16},{16,24},{24,32},{32,40},{40,48},{48,56},{56,6... | collective-permute-start | bytes 2359304 | tf_op jit(solution)/shard_map/while/body/eval_jaxpr/ppermute | solution.py:15
  547.8 1.5 copy-start.4
  549.4 18.8 %collective-permute-start = (bf16[4,256,384]{1,2,0:T(8,128)(2,1)}, bf16[4,256,384]{1,2,0:T(8,128)(2,1)S(1)}, u32[]{:S(2)}, u32[]{:S(2)}) collective-permute-start(bf16[4,256,384]{1,2,0:T(8,128)(2,1)} %get-tuple-element.538), channel_id=1, source_target_pairs={{248,0},{0,8},{8,16},{16,24},{24,32},{32,40},{40,48},{48,56},{56,6... | collective-permute-start | bytes 2359304 | tf_op jit(solution)/shard_map/while/body/eval_jaxpr/ppermute | solution.py:15
  570.5 1.5 copy-start.4
  572.1 17.8 %collective-permute-start = (bf16[4,256,384]{1,2,0:T(8,128)(2,1)}, bf16[4,256,384]{1,2,0:T(8,128)(2,1)S(1)}, u32[]{:S(2)}, u32[]{:S(2)}) collective-permute-start(bf16[4,256,384]{1,2,0:T(8,128)(2,1)} %get-tuple-element.538), channel_id=1, source_target_pairs={{248,0},{0,8},{8,16},{16,24},{24,32},{32,40},{40,48},{48,56},{56,6... | collective-permute-start | bytes 2359304 | tf_op jit(solution)/shard_map/while/body/eval_jaxpr/ppermute | solution.py:15
  592.3 1.5 copy-start.4
  593.9 16.9 %collective-permute-start = (bf16[4,256,384]{1,2,0:T(8,128)(2,1)}, bf16[4,256,384]{1,2,0:T(8,128)(2,1)S(1)}, u32[]{:S(2)}, u32[]{:S(2)}) collective-permute-start(bf16[4,256,384]{1,2,0:T(8,128)(2,1)} %get-tuple-element.538), channel_id=1, source_target_pairs={{248,0},{0,8},{8,16},{16,24},{24,32},{32,40},{40,48},{48,56},{56,6... | collective-permute-start | bytes 2359304 | tf_op jit(solution)/shard_map/while/body/eval_jaxpr/ppermute | solution.py:15
  614.8 16.0 %collective-permute-start = (bf16[4,256,384]{1,2,0:T(8,128)(2,1)}, bf16[4,256,384]{1,2,0:T(8,128)(2,1)S(1)}, u32[]{:S(2)}, u32[]{:S(2)}) collective-permute-start(bf16[4,256,384]{1,2,0:T(8,128)(2,1)} %get-tuple-element.538), channel_id=1, source_target_pairs={{248,0},{0,8},{8,16},{16,24},{24,32},{32,40},{40,48},{48,56},{56,6... | collective-permute-start | bytes 2359304 | tf_op jit(solution)/shard_map/while/body/eval_jaxpr/ppermute | solution.py:15
  633.1 1.5 copy-start.4
  634.8 15.1 %collective-permute-start = (bf16[4,256,384]{1,2,0:T(8,128)(2,1)}, bf16[4,256,384]{1,2,0:T(8,128)(2,1)S(1)}, u32[]{:S(2)}, u32[]{:S(2)}) collective-permute-start(bf16[4,256,384]{1,2,0:T(8,128)(2,1)} %get-tuple-element.538), channel_id=1, source_target_pairs={{248,0},{0,8},{8,16},{16,24},{24,32},{32,40},{40,48},{48,56},{56,6... | collective-permute-start | bytes 2359304 | tf_op jit(solution)/shard_map/while/body/eval_jaxpr/ppermute | solution.py:15
  652.2 1.5 copy-start.4
  653.8 14.4 %collective-permute-start = (bf16[4,256,384]{1,2,0:T(8,128)(2,1)}, bf16[4,256,384]{1,2,0:T(8,128)(2,1)S(1)}, u32[]{:S(2)}, u32[]{:S(2)}) collective-permute-start(bf16[4,256,384]{1,2,0:T(8,128)(2,1)} %get-tuple-element.538), channel_id=1, source_target_pairs={{248,0},{0,8},{8,16},{16,24},{24,32},{32,40},{40,48},{48,56},{56,6... | collective-permute-start | bytes 2359304 | tf_op jit(solution)/shard_map/while/body/eval_jaxpr/ppermute | solution.py:15
  670.5 1.5 copy-start.4
  672.1 14.4 %collective-permute-start = (bf16[4,256,384]{1,2,0:T(8,128)(2,1)}, bf16[4,256,384]{1,2,0:T(8,128)(2,1)S(1)}, u32[]{:S(2)}, u32[]{:S(2)}) collective-permute-start(bf16[4,256,384]{1,2,0:T(8,128)(2,1)} %get-tuple-element.538), channel_id=1, source_target_pairs={{248,0},{0,8},{8,16},{16,24},{24,32},{32,40},{40,48},{48,56},{56,6... | collective-permute-start | bytes 2359304 | tf_op jit(solution)/shard_map/while/body/eval_jaxpr/ppermute | solution.py:15
  688.8 1.5 copy-start.4
  690.4 14.5 %collective-permute-start = (bf16[4,256,384]{1,2,0:T(8,128)(2,1)}, bf16[4,256,384]{1,2,0:T(8,128)(2,1)S(1)}, u32[]{:S(2)}, u32[]{:S(2)}) collective-permute-start(bf16[4,256,384]{1,2,0:T(8,128)(2,1)} %get-tuple-element.538), channel_id=1, source_target_pairs={{248,0},{0,8},{8,16},{16,24},{24,32},{32,40},{40,48},{48,56},{56,6... | collective-permute-start | bytes 2359304 | tf_op jit(solution)/shard_map/while/body/eval_jaxpr/ppermute | solution.py:15
  707.3 1.5 copy-start.4
  (97 other events, 103.9 us)
Sparse Core Ops, SparseCore 0:
  715.4 60.0 reduce-scatter.1
where the time goes:
time: 788 us; the launch traced here: 784 us
  waiting for transfers between devices  578 us (73%)
  matrix products  107 us (14%)
  local copies, waits for them, and re-layouts  61.6 us (8%)
  other arithmetic  16.9 us (2%)
  between operations  14.9 us (2%)
    ppermute x31, waiting for transfers between devices, passed_along(): return lax.ppermute(block, axis, route)  517 us
    reduce_scatter x1, waiting for transfers between devices, body(): lax.psum_scatter(jnp.concatenate((jnp.dot(mixed, out_weight, preferred_el...  60.2 us
    while x310, local copies, waits for them, and re-layouts  35.4 us
    dot_general x32, matrix products, live_tiles_for(): return jnp.einsum('hrt,kt->hrk', row_mask, one_hot) > 0.5  24.8 us
    dot_general x32, matrix products, accumulate(): jnp.einsum('qhd,khd->hqk', qtan_heads, key_heads, preferred_element_type=...  16.3 us
    dot_general x32, matrix products, accumulate(): jnp.einsum('hqk,khd->qhd', weights_low, value_heads, preferred_element_ty...  16.1 us
  transfers between devices with their start and end apart: 32, of which 32 were waited for; matrix products, arithmetic and copies ran while one was open for 5% of the time, Pallas kernels for 0%

commit v1 on v0

v1 whole, which is shorter than its diff:
```python
import functools
import math

import jax
import jax.numpy as jnp
from jax import lax
from jax.experimental import pallas as pl
from jax.experimental.pallas import tpu as pltpu
from jax.sharding import Mesh
from jax.sharding import PartitionSpec as P

NX, NZ, NY, NC = 4, 8, 4, 2
HEADS_HERE = 3
HEAD_DIM = 128
PAIR = 2 * HEAD_DIM
TILE = 128
TOK = 256
TILES_HERE = TOK // TILE
FRAME_TILES = NX * NZ * TILES_HERE
WIDE = HEADS_HERE * PAIR
PACKED = WIDE + 128
PIECES = 3
SLOT_TOK = TOK // NY
DM = 3072
SCALING = HEAD_DIM ** (-0.5)
EXP_SCALE = SCALING * math.log2(math.e)
VERY_LOW = -1e30
VERY_HIGH = 1e30
VMEM_LIMIT = 56 * 1024 * 1024
NT = (((1,), (1,)), ((), ()))


def params():
    return pltpu.CompilerParams(vmem_limit_bytes=VMEM_LIMIT)


def prepare_kernel(q_ref, qt_ref, k_ref, kt_ref, v_ref, vt_ref, qq_ref, kv_ref):
    for h in range(HEADS_HERE):
        cols = pl.ds(h * HEAD_DIM, HEAD_DIM)
        qq_ref[:, pl.ds(h * PAIR, HEAD_DIM)] = qt_ref[:, cols]
        qq_ref[:, pl.ds(h * PAIR + HEAD_DIM, HEAD_DIM)] = q_ref[:, cols]
        kv_ref[h, :, 0:HEAD_DIM] = k_ref[:, cols]
        kv_ref[h, :, HEAD_DIM:PAIR] = kt_ref[:, cols]
        kv_ref[HEADS_HERE + h, 0:HEAD_DIM, :] = v_ref[:, cols].T
        kv_ref[HEADS_HERE + h, HEAD_DIM:PAIR, :] = vt_ref[:, cols].T


def prepare(queries, query_tangent, keys, key_tangent, values, value_tangent):
    return pl.pallas_call(
        prepare_kernel,
        out_shape=(
            jax.ShapeDtypeStruct((TOK, WIDE), jnp.bfloat16),
            jax.ShapeDtypeStruct((2 * HEADS_HERE, TOK, PAIR), jnp.bfloat16),
        ),
        compiler_params=params(),
        name="prepare",
    )(queries, query_tangent, keys, key_tangent, values, value_tangent)


def attend_slot(h, slot, key_blocks, q2, mask_ref, frame_ref, place_ref, kks, vvs, old):
    x, z = place_ref[0], place_ref[1]
    query_frame = frame_ref[((x + slot) % NX) * NZ + z]
    lanes = lax.broadcasted_iota(jnp.int32, (1, TOK), 1)
    first = lanes < TILE
    m_old, l_old, d_old, acc_old = old
    scores, lives = [], []
    m_new = m_old
    for at, offset in enumerate(key_blocks):
        key_frame = frame_ref[x * NZ + (z + offset + NZ) % NZ]
        s = lax.dot_general(
            kks[at][:, 0:HEAD_DIM], q2[:, HEAD_DIM:PAIR], NT, preferred_element_type=jnp.float32
        )
        for j in range(TILES_HERE):
            row = (h * FRAME_TILES + query_frame * TILES_HERE) * FRAME_TILES
            col = key_frame * TILES_HERE + j
            live = jnp.where(first, mask_ref[row + col], mask_ref[row + FRAME_TILES + col]) == 1
            s_tile = s[j * TILE : (j + 1) * TILE]
            top = jnp.max(s_tile, axis=0, keepdims=True) * EXP_SCALE
            m_new = jnp.maximum(m_new, jnp.where(live, top, VERY_LOW))
            scores.append(s_tile)
            lives.append(live)
    fade = jnp.exp2(m_old - m_new)
    l_new, d_sum = l_old * fade, jnp.zeros_like(d_old)
    main, side = None, None
    for at in range(len(key_blocks)):
        t = lax.dot_general(kks[at][...], q2, NT, preferred_element_type=jnp.float32)
        weights, scaled = [], []
        for j in range(TILES_HERE):
            less = jnp.where(lives[TILES_HERE * at + j], m_new, VERY_HIGH)
            w = jnp.exp2(scores[TILES_HERE * at + j] * EXP_SCALE - less)
            ws = w * t[j * TILE : (j + 1) * TILE]
            l_new = l_new + jnp.sum(w, axis=0, keepdims=True)
            d_sum = d_sum + jnp.sum(ws, axis=0, keepdims=True)
            weights.append(w.astype(jnp.bfloat16))
            scaled.append(ws.astype(jnp.bfloat16))
        weights = jnp.concatenate(weights, axis=0)
        scaled = jnp.concatenate(scaled, axis=0)
        o = jnp.dot(vvs[at][...], weights, preferred_element_type=jnp.float32)
        o2 = jnp.dot(vvs[at][0:HEAD_DIM, :], scaled, preferred_element_type=jnp.float32)
        main = o if main is None else main + o
        side = o2 if side is None else side + o2
    d_new = d_old * fade + SCALING * d_sum
    top = acc_old[0:HEAD_DIM] * fade + main[0:HEAD_DIM]
    bottom = acc_old[HEAD_DIM:PAIR] * fade + main[HEAD_DIM:PAIR] + SCALING * side
    return m_new, l_new, d_new, top, bottom


def attend_kernel(key_blocks, is_first, is_last, *refs):
    count = len(key_blocks)
    mask_ref, frame_ref, place_ref = refs[:3]
    q_refs = refs[3 : 3 + NX]
    rest = refs[3 + NX :]
    kk_refs = [r.at[0] for r in rest[:count]]
    vv_refs = [r.at[0] for r in rest[count : 2 * count]]
    rest = rest[2 * count :]
    if not is_first:
        acc_in, stat_in = rest[:2]
        rest = rest[2:]
    h = pl.program_id(0)
    if is_last:
        side_ref = rest[1]

        @pl.when(h == 0)
        def _():
            side_ref[...] = jnp.zeros_like(side_ref)

    for slot in range(NX):
        cols = pl.ds(slot * TOK, TOK)
        if is_first:
            zero = jnp.zeros((1, TOK), jnp.float32)
            old = (zero + VERY_LOW, zero, zero, jnp.zeros((PAIR, TOK), jnp.float32))
        else:
            old = (
                stat_in[0, 0:1, cols],
                stat_in[0, 1:2, cols],
                stat_in[0, 2:3, cols],
                acc_in[0, :, cols],
            )
        m, l, d, top, bottom = attend_slot(
            h, slot, key_blocks, q_refs[slot][...], mask_ref, frame_ref, place_ref, kk_refs, vv_refs, old
        )
        if not is_last:
            acc_out, stat_out = rest
            stat_out[0, 0:1, cols] = m
            stat_out[0, 1:2, cols] = l
            stat_out[0, 2:3, cols] = d
            acc_out[0, 0:HEAD_DIM, cols] = top
            acc_out[0, HEAD_DIM:PAIR, cols] = bottom
        else:
            out_ref = rest[0]
            some = l > 0.0
            inverse = jnp.where(some, 1.0 / jnp.where(some, l, 1.0), 0.0)
            level = jnp.where(some, m + jnp.log2(jnp.where(some, l, 1.0)), VERY_LOW)
            drift = d * inverse
            attn = top * inverse
            tangent = bottom * inverse - drift * attn
            target = (place_ref[0] + slot) % NX
            columns = pl.multiple_of(h * PAIR, PAIR)
            out_ref[target, :, pl.ds(columns, HEAD_DIM)] = attn.astype(jnp.bfloat16).T
            out_ref[target, :, pl.ds(columns + HEAD_DIM, HEAD_DIM)] = tangent.astype(jnp.bfloat16).T
            for at, value in enumerate((level, drift)):
                left = value
                for p in range(PIECES):
                    piece = left.astype(jnp.bfloat16).astype(jnp.float32)
                    side_ref[slot, pl.ds(8 * p + HEADS_HERE * at + h, 1), :] = piece
                    left = left - piece

            @pl.when(h == HEADS_HERE - 1)
            def _():
                out_ref[target, :, pl.ds(WIDE, 128)] = side_ref[slot].T.astype(jnp.bfloat16)


def attend(key_blocks, mask, frames, place, slots, kks, vvs, state, is_last):
    count = len(key_blocks)
    is_first = state is None
    smem = pl.BlockSpec(memory_space=pltpu.SMEM)
    acc_spec = pl.BlockSpec((1, PAIR, NX * TOK), lambda h: (h, 0, 0))
    stat_spec = pl.BlockSpec((1, 8, NX * TOK), lambda h: (h, 0, 0))
    in_specs = [smem] * 3
    in_specs += [pl.BlockSpec((TOK, PAIR), lambda h: (0, h))] * NX
    in_specs += [pl.BlockSpec((1, TOK, PAIR), lambda h: (h, 0, 0))] * count
    for vv in vvs:
        skip = vv.shape[0] - HEADS_HERE
        in_specs.append(pl.BlockSpec((1, PAIR, TOK), lambda h, skip=skip: (skip + h, 0, 0)))
    operands = [mask, frames, place, *slots, *kks, *vvs]
    if not is_first:
        in_specs += [acc_spec, stat_spec]
        operands += list(state)
    scratch = []
    if is_last:
        out_shape = jax.ShapeDtypeStruct((NX, TOK, PACKED), jnp.bfloat16)
        out_specs = pl.BlockSpec((NX, TOK, PACKED), lambda h: (0, 0, 0))
        scratch = [pltpu.VMEM((NX, 128, TOK), jnp.float32)]
    else:
        out_shape = (
            jax.ShapeDtypeStruct((HEADS_HERE, PAIR, NX * TOK), jnp.float32),
            jax.ShapeDtypeStruct((HEADS_HERE, 8, NX * TOK), jnp.float32),
        )
        out_specs = (acc_spec, stat_spec)
    return pl.pallas_call(
        functools.partial(attend_kernel, key_blocks, is_first, is_last),
        grid=(HEADS_HERE,),
        in_specs=in_specs,
        out_specs=out_specs,
        out_shape=out_shape,
        scratch_shapes=scratch,
        compiler_params=params(),
        name="attend_last" if is_last else "attend",
    )(*operands)


COLS = 512


def project_kernel(place_ref, r_ref, w_ref, main_ref, tangent_ref, other_ref, mixed):
    c = place_ref[3]

    @pl.when(pl.program_id(0) == 0)
    def _():
        for group in range(NY):
            sides = []
            for x in range(NX):
                side = r_ref[x * NY + group, :, pl.ds(WIDE, 128)].astype(jnp.float32)
                sides.append(side + (pltpu.roll(side, 128 - 8, 1) + pltpu.roll(side, 128 - 16, 1)))
            top = functools.reduce(jnp.maximum, sides)
            shares = [jnp.exp2(side - top) for side in sides]
            inverse = 1.0 / sum(shares)
            shares = [share * inverse for share in shares]
            drifts = [pltpu.roll(side, 128 - HEADS_HERE, 1) for side in sides]
            drift = sum(s * d for s, d in zip(shares, drifts))
            moves = [s * (d - drift) for s, d in zip(shares, drifts)]
            for h in range(HEADS_HERE):
                attn, tangent = 0.0, 0.0
                for x in range(NX):
                    a = r_ref[x * NY + group, :, pl.ds(h * PAIR, HEAD_DIM)].astype(jnp.float32)
                    t = r_ref[x * NY + group, :, pl.ds(h * PAIR + HEAD_DIM, HEAD_DIM)].astype(jnp.float32)
                    share = shares[x][:, h : h + 1]
                    attn = attn + share * a
                    tangent = tangent + share * t + moves[x][:, h : h + 1] * a
                cols = pl.ds((group * HEADS_HERE + h) * HEAD_DIM, HEAD_DIM)
                mixed[0:SLOT_TOK, cols] = attn.astype(jnp.bfloat16)
                mixed[SLOT_TOK : 2 * SLOT_TOK, cols] = tangent.astype(jnp.bfloat16)

    total = jnp.dot(mixed[...], w_ref[...], preferred_element_type=jnp.float32)
    half = SLOT_TOK // NC
    mine = c == 0
    for which, own_ref in enumerate((main_ref, tangent_ref)):
        low = total[which * SLOT_TOK : which * SLOT_TOK + half]
        high = total[which * SLOT_TOK + half : (which + 1) * SLOT_TOK]
        own_ref[...] = jnp.where(mine, low, high)
        other_ref[which] = jnp.where(mine, high, low).astype(jnp.bfloat16)


def project(place, received, weight):
    half = SLOT_TOK // NC
    rows = NY * HEADS_HERE * HEAD_DIM
    own_spec = pl.BlockSpec((half, COLS), lambda i: (0, i))
    own_shape = jax.ShapeDtypeStruct((half, DM), jnp.float32)
    return pl.pallas_call(
        project_kernel,
        grid=(DM // COLS,),
        in_specs=[
            pl.BlockSpec(memory_space=pltpu.SMEM),
            pl.BlockSpec((NX * NY, SLOT_TOK, PACKED), lambda i: (0, 0, 0)),
            pl.BlockSpec((rows, COLS), lambda i: (0, i)),
        ],
        out_specs=(own_spec, own_spec, pl.BlockSpec((2, half, COLS), lambda i: (0, 0, i))),
        out_shape=(own_shape, own_shape, jax.ShapeDtypeStruct((2, half, DM), jnp.bfloat16)),
        scratch_shapes=[pltpu.VMEM((2 * SLOT_TOK, rows), jnp.bfloat16)],
        compiler_params=params(),
        name="project",
    )(place, received, weight)


def finish_kernel(main_ref, tangent_ref, arrived_ref, out_ref, tout_ref):
    out_ref[...] = (main_ref[...] + arrived_ref[0].astype(jnp.float32)).astype(jnp.bfloat16)
    tout_ref[...] = (tangent_ref[...] + arrived_ref[1].astype(jnp.float32)).astype(jnp.bfloat16)


def finish(main, tangent, arrived):
    shape = jax.ShapeDtypeStruct(main.shape, jnp.bfloat16)
    return pl.pallas_call(
        finish_kernel, out_shape=(shape, shape), compiler_params=params(), name="finish"
    )(main, tangent, arrived)


def shifted(block, axis, distance):
    size = lax.axis_size(axis)
    return lax.ppermute(block, axis, [(i, (i + distance) % size) for i in range(size)])


def body(
    queries,
    keys,
    values,
    query_tangent,
    key_tangent,
    value_tangent,
    tile_mask,
    block_frame,
    out_weight,
):
    place = jnp.stack([lax.axis_index(a) for a in ("x", "z", "y", "c")]).astype(jnp.int32)
    mask = tile_mask.reshape(-1)
    qq, bundle = prepare(queries, query_tangent, keys, key_tangent, values, value_tangent)

    weight = lax.all_gather(out_weight, "y", tiled=True)

    slots = [qq, shifted(qq, "x", -1), shifted(qq, "x", 2), shifted(qq, "x", 1)]
    from_left = shifted(bundle, "z", 1)
    from_right = shifted(bundle, "z", -1)
    from_left, from_right, slots, mask = lax.optimization_barrier(
        (from_left, from_right, slots, mask)
    )

    def run(key_blocks, kks, vvs, state, is_last=False):
        return attend(key_blocks, mask, block_frame, place, slots, kks, vvs, state, is_last)

    blocks = (bundle, from_left, from_right)
    offsets = (0, -1, 1)
    state = None
    for distance in (2, 3):
        next_left = shifted(from_left, "z", 1)
        next_right = shifted(from_right, "z", -1)
        state = run(offsets, blocks, blocks, state)
        from_left, from_right, state = lax.optimization_barrier((next_left, next_right, state))
        blocks = (from_left, from_right)
        offsets = (-distance, distance)
    far_keys = shifted(from_left[:HEADS_HERE], "z", 1)
    far_values = shifted(from_right[HEADS_HERE:], "z", -1)
    state = run(offsets, blocks, blocks, state)
    far_keys, far_values, state = lax.optimization_barrier((far_keys, far_values, state))
    packed = run((4,), (far_keys,), (far_values,), state, is_last=True)
    received = lax.all_to_all(
        packed.reshape(NX * NY, SLOT_TOK, PACKED), ("x", "y"), 0, 0, tiled=True
    )
    main, tangent, other = project(place, received, weight)
    arrived = lax.ppermute(other, "c", [(0, 1), (1, 0)])
    return finish(main, tangent, arrived)


def solution(mesh):
    inner = Mesh(mesh.devices.reshape(NX, NZ, NY, NC), ("x", "z", "y", "c"))
    blk, head = ("x", "z"), ("y", "c")
    in_specs = (
        P(blk, head),
        P(blk, head),
        P(blk, head),
        P(blk, head),
        P(blk, head),
        P(blk, head),
        P(head, None, None),
        P(),
        P(head, None),
    )
    out_specs = (P(blk + head, None), P(blk + head, None))
    return jax.shard_map(body, mesh=inner, in_specs=in_specs, out_specs=out_specs, check_vma=False)
```

time: 788 us -> 155 us (0.20)
  waiting for transfers between devices: 578 us -> 33.9 us
  matrix products: 107 us -> 0 us
  local copies, waits for them, and re-layouts: 61.6 us -> 2.28 us
  Pallas kernels: 0 us -> 54.8 us
  blocking collectives: 0 us -> 26.2 us
  starting transfers between devices: 2.58 us -> 22.9 us
  other arithmetic: 16.9 us -> 0.58 us
    ppermute x31 -> x12, waiting for transfers between devices: 517 us -> 33.2 us  [the longest x11 31.6 us: shifted(): lax.ppermute(block, axis, [(i, (i + distance) % size) for i in range(size)])]
    dot_general x226 -> x0, matrix products: 107 us -> none  [the longest x32 24.8 us: live_tiles_for(): return jnp.einsum('hrt,kt->hrk', row_mask, one_hot) > 0.5]
    reduce_scatter x1 -> x0, waiting for transfers between devices: 60.2 us -> none  [body(): lax.psum_scatter(jnp.concatenate((jnp.dot(mixed, out_weight, preferred_el...]
    pallas_call x0 -> x7, Pallas kernels: none -> 54.8 us  [the longest x4 40.7 us: attend(): pl.pallas_call(functools.partial(attend_kernel, key_blocks, is_first, is_...]
    while x314 -> x0, local copies, waits for them, and re-layouts: 39 us -> none
    all_to_all x0 -> x1, blocking collectives: none -> 26.2 us  [body(): lax.all_to_all(packed.reshape(NX * NY, SLOT_TOK, PACKED), ('x', 'y'), 0,...]
    ppermute x31 -> x12, starting transfers between devices: 2.54 us -> 22.8 us  [the longest x11 18.2 us: shifted(): lax.ppermute(block, axis, [(i, (i + distance) % size) for i in range(size)])]
    reduce_sum x65 -> x0, other arithmetic: 11.5 us -> none  [the longest x32 6.43 us: accumulate(): totals = totals * fading + jnp.sum(weights, axis=2)]
  transfers between devices with their start and end apart: 32 -> 13, of which waited for: 32 -> 7; matrix products, arithmetic and copies ran while one was open for 5% -> 1% of each run, Pallas kernels for 0% -> 28%
where the time goes in v1:
time: 155 us
  Pallas kernels  54.8 us (35%)
  waiting for transfers between devices  33.9 us (22%)
  blocking collectives  26.2 us (17%)
  starting transfers between devices  22.9 us (15%)
  between operations  14.1 us (9%)
  local copies, waits for them, and re-layouts  2.28 us (1%)
    pallas_call x4, Pallas kernels, attend(): pl.pallas_call(functools.partial(attend_kernel, key_blocks, is_first, is_...  40.7 us
    ppermute x11, waiting for transfers between devices, shifted(): lax.ppermute(block, axis, [(i, (i + distance) % size) for i in range(size)])  31.6 us
    all_to_all x1, blocking collectives, body(): lax.all_to_all(packed.reshape(NX * NY, SLOT_TOK, PACKED), ('x', 'y'), 0,...  26.2 us
    ppermute x11, starting transfers between devices, shifted(): lax.ppermute(block, axis, [(i, (i + distance) % size) for i in range(size)])  18.2 us
    pallas_call x1, Pallas kernels, project(): pl.pallas_call(project_kernel, grid=(DM // COLS,), in_specs=[pl.BlockSpec...  9.56 us
    ppermute x1, starting transfers between devices, body(): arrived = lax.ppermute(other, 'c', [(0, 1), (1, 0)])  4.59 us
  transfers between devices with their start and end apart: 13, of which 7 were waited for; matrix products, arithmetic and copies ran while one was open for 1% of the time, Pallas kernels for 28%

profile of v1, /device:TPU:1, one launch (start us, length us, event | category | flops | bytes accessed | tf_op | source)
XLA Modules:
  0.0 154.7 jit_solution(13613895850592590179)
XLA Ops:
  7.2 0.0 copy-start.11
  7.2 0.0 all-gather.2.cloned.1.call-start
  7.2 0.7 all-gather.2.cloned.1.call-update
  7.9 2.5 %prepare.1 = (bf16[256,768]{1,0:T(8,128)(2,1)}, bf16[6,256,256]{2,1,0:T(8,128)(2,1)}) custom-call(bf16[256,384]{1,0:T(8,128)(2,1)} %q_ref.1, bf16[256,384]{1,0:T(8,128)(2,1)} %qt_ref.1, bf16[256,384]{1,0:T(8,128)(2,1)} %k_ref.1, bf16[256,384]{1,0:T(8,128)(2,1)} %kt_ref.1, bf16[256,384]{1,0:T(8,128)(2,1)} %v_ref.1, bf16[256,384]{1,0:T(8,128)(2,1)} %vt_ref.1), custom_call_target="tpu_custom_call" | custom-call | tf_op jit(solution)/shard_map/prepare/pallas_call | solution.py:49
  10.4 2.5 %collective-permute-start = (bf16[6,256,256]{2,1,0:T(8,128)(2,1)}, bf16[6,256,256]{2,1,0:T(8,128)(2,1)S(1)}, u32[]{:S(2)}, u32[]{:S(2)}) collective-permute-start(bf16[6,256,256]{2,1,0:T(8,128)(2,1)} %get-tuple-element.32.refs_7_.refs_10_), channel_id=1, source_target_pairs={{0,8},{8,16},{16,24},{24,32},{32,40},{40,48},{48,56},{56,0},{1,9},... | collective-permute-start | bytes 2359304 | tf_op jit(solution)/shard_map/ppermute | solution.py:289
  12.9 4.0 %collective-permute-start.1 = (bf16[6,256,256]{2,1,0:T(8,128)(2,1)}, bf16[6,256,256]{2,1,0:T(8,128)(2,1)}, u32[]{:S(2)}, u32[]{:S(2)}) collective-permute-start(bf16[6,256,256]{2,1,0:T(8,128)(2,1)} %get-tuple-element.32.refs_7_.refs_10_), channel_id=1, source_target_pairs={{0,56},{8,0},{16,8},{24,16},{32,24},{40,32},{48,40},{56,48},{1,57}... | collective-permute-start | bytes 2359304 | tf_op jit(solution)/shard_map/ppermute | solution.py:289
  16.9 2.4 %collective-permute-start.2 = (bf16[256,768]{1,0:T(8,128)(2,1)}, bf16[256,768]{1,0:T(8,128)(2,1)S(1)}, u32[]{:S(2)}, u32[]{:S(2)}) collective-permute-start(bf16[256,768]{1,0:T(8,128)(2,1)} %get-tuple-element.35.refs_3_), channel_id=1, source_target_pairs={{0,192},{64,0},{128,64},{192,128},{1,193},{65,1},{129,65},{193,129... | collective-permute-start | bytes 1179656 | tf_op jit(solution)/shard_map/ppermute | solution.py:289
  19.3 0.5 collective-permute-start.3
  19.8 0.6 collective-permute-start.4
  20.4 0.0 copy-done.11
  20.4 0.7 reshape.10.refs_0_
  21.1 6.7 %collective-permute-done.2.refs_4_ = bf16[256,768]{1,0:T(8,128)(2,1)S(1)} collective-permute-done((bf16[256,768]{1,0:T(8,128)(2,1)}, bf16[256,768]{1,0:T(8,128)(2,1)S(1)}, u32[]{:S(2)}, u32[]{:S(2)}) %collective-permute-start.2) | collective-permute-done | bytes 393248 | tf_op jit(solution)/shard_map/ppermute | solution.py:289
  27.8 0.0 copy-start
  27.8 2.6 %collective-permute-done.3.refs_5_ = bf16[256,768]{1,0:T(8,128)(2,1)S(1)} collective-permute-done((bf16[256,768]{1,0:T(8,128)(2,1)}, bf16[256,768]{1,0:T(8,128)(2,1)S(1)}, u32[]{:S(2)}, u32[]{:S(2)}) %collective-permute-start.3) | collective-permute-done | bytes 393248 | tf_op jit(solution)/shard_map/ppermute | solution.py:289
  30.4 0.0 copy-start.1
  30.4 10.2 %collective-permute-done.4.refs_6_ = bf16[256,768]{1,0:T(8,128)(2,1)S(1)} collective-permute-done((bf16[256,768]{1,0:T(8,128)(2,1)}, bf16[256,768]{1,0:T(8,128)(2,1)S(1)}, u32[]{:S(2)}, u32[]{:S(2)}) %collective-permute-start.4) | collective-permute-done | bytes 393248 | tf_op jit(solution)/shard_map/ppermute | solution.py:289
  40.6 0.0 copy-start.2
  40.6 0.0 collective-permute-done.refs_8_.refs_11_
  40.6 0.0 copy-start.7
  40.6 0.0 collective-permute-done.1.refs_9_.refs_12_
  40.6 0.1 collective-permute-start.5
  40.7 2.7 %collective-permute-start.6 = (bf16[6,256,256]{2,1,0:T(8,128)(2,1)}, bf16[6,256,256]{2,1,0:T(8,128)(2,1)S(1)}, u32[]{:S(2)}, u32[]{:S(2)}) collective-permute-start(bf16[6,256,256]{2,1,0:T(8,128)(2,1)} %collective-permute-done.1.refs_9_.refs_12_), channel_id=1, source_target_pairs={{0,56},{8,0},{16,8},{24,16},{32,24},{40,32},{48,40},{56,48},{1,57}... | collective-permute-start | bytes 2359304 | tf_op jit(solution)/shard_map/ppermute | solution.py:289
  43.4 0.6 pad_add_fusion.refs_2_.place_ref
  44.0 0.0 copy-done
  44.0 0.0 copy-done.1
  44.0 0.0 copy-done.2
  44.0 0.0 copy-done.7
  44.0 12.4 %attend.3 = (f32[3,256,1024]{2,1,0:T(8,128)}, f32[3,8,1024]{2,1,0:T(8,128)}) custom-call(s32[12288]{0:T(1024)} %reshape.10.refs_0_, s32[32]{0:T(128)} %refs_1_.7, s32[4]{0:T(128)} %pad_add_fusion.refs_2_.place_ref, bf16[256,768]{1,0:T(8,128)(2,1)} %get-tuple-element.35.refs_3_, bf16[256,768]{1,0:T(8,128)(2,1)} %copy-done, bf16[256,768]{1,0:T(8,128)(2,1)} %copy-done.1, ...), custom_call_target="tpu_custom_call" | custom-call | tf_op jit(solution)/shard_map/attend/pallas_call | solution.py:200
  56.4 4.4 %collective-permute-done.5.refs_7_.refs_9_ = bf16[6,256,256]{2,1,0:T(8,128)(2,1)S(1)} collective-permute-done((bf16[6,256,256]{2,1,0:T(8,128)(2,1)S(1)}, bf16[6,256,256]{2,1,0:T(8,128)(2,1)S(1)}, u32[]{:S(2)}, u32[]{:S(2)}) %collective-permute-start.5) | collective-permute-done | bytes 786464 | tf_op jit(solution)/shard_map/ppermute | solution.py:289
  60.7 0.0 copy-start.5
  60.7 0.0 collective-permute-done.6.refs_8_.refs_10_
  60.7 0.0 copy-start.6
  60.8 0.1 collective-permute-start.7
  60.8 2.7 %collective-permute-start.8 = (bf16[6,256,256]{2,1,0:T(8,128)(2,1)S(1)}, bf16[6,256,256]{2,1,0:T(8,128)(2,1)S(1)}, u32[]{:S(2)}, u32[]{:S(2)}) collective-permute-start(bf16[6,256,256]{2,1,0:T(8,128)(2,1)S(1)} %collective-permute-done.6.refs_8_.refs_10_), channel_id=1, source_target_pairs={{0,56},{8,0},{16,8},{24,16},{32,24},{40,32},{48,40},{56,48},{1,57}... | collective-permute-start | bytes 2359304 | tf_op jit(solution)/shard_map/ppermute | solution.py:289
  63.5 0.0 copy-done.5
  63.5 0.0 copy-done.6
  63.5 9.1 %attend.4 = (f32[3,256,1024]{2,1,0:T(8,128)}, f32[3,8,1024]{2,1,0:T(8,128)}) custom-call(s32[12288]{0:T(1024)} %reshape.10.refs_0_, s32[32]{0:T(128)} %refs_1_.7, s32[4]{0:T(128)} %pad_add_fusion.refs_2_.place_ref, bf16[256,768]{1,0:T(8,128)(2,1)} %get-tuple-element.35.refs_3_, bf16[256,768]{1,0:T(8,128)(2,1)} %copy-done, bf16[256,768]{1,0:T(8,128)(2,1)} %copy-done.1, ...), custom_call_target="tpu_custom_call" | custom-call | tf_op jit(solution)/shard_map/attend/pallas_call | solution.py:200
  72.6 7.5 %collective-permute-done.7.refs_7_.refs_9_ = bf16[6,256,256]{2,1,0:T(8,128)(2,1)S(1)} collective-permute-done((bf16[6,256,256]{2,1,0:T(8,128)(2,1)S(1)}, bf16[6,256,256]{2,1,0:T(8,128)(2,1)S(1)}, u32[]{:S(2)}, u32[]{:S(2)}) %collective-permute-start.7) | collective-permute-done | bytes 786464 | tf_op jit(solution)/shard_map/ppermute | solution.py:289
  80.1 0.0 copy-start.3
  80.1 0.0 collective-permute-done.8.refs_8_.refs_10_
  80.1 0.0 copy-start.4
  80.1 2.6 %collective-permute-start.10 = (bf16[3,256,256]{2,1,0:T(8,128)(2,1)S(1)}, bf16[3,256,256]{2,1,0:T(8,128)(2,1)S(1)}, u32[]{:S(2)}, u32[]{:S(2)}) collective-permute-start(bf16[3,256,256]{2,1,0:T(8,128)(2,1)S(1)} %slice.7), channel_id=1, source_target_pairs={{0,56},{8,0},{16,8},{24,16},{32,24},{40,32},{48,40},{56,48},{1,57}... | collective-permute-start | bytes 1179656 | tf_op jit(solution)/shard_map/ppermute | solution.py:289
  82.8 0.1 collective-permute-start.9
  82.9 0.0 copy-done.3
  82.9 0.0 copy-done.4
  82.9 9.1 %attend.5 = (f32[3,256,1024]{2,1,0:T(8,128)}, f32[3,8,1024]{2,1,0:T(8,128)}) custom-call(s32[12288]{0:T(1024)} %reshape.10.refs_0_, s32[32]{0:T(128)} %refs_1_.7, s32[4]{0:T(128)} %pad_add_fusion.refs_2_.place_ref, bf16[256,768]{1,0:T(8,128)(2,1)} %get-tuple-element.35.refs_3_, bf16[256,768]{1,0:T(8,128)(2,1)} %copy-done, bf16[256,768]{1,0:T(8,128)(2,1)} %copy-done.1, ...), custom_call_target="tpu_custom_call" | custom-call | tf_op jit(solution)/shard_map/attend/pallas_call | solution.py:200
  92.0 0.0 collective-permute-done.10.refs_8_
  92.0 0.0 copy-start.8
  92.0 0.3 collective-permute-done.9.refs_7_
  92.3 0.0 copy-start.9
  92.3 0.5 copy-done.8
  92.7 0.3 copy-done.9
  93.0 10.1 %attend_last.1 = bf16[4,256,896]{2,1,0:T(8,128)(2,1)} custom-call(s32[12288]{0:T(1024)} %reshape.10.refs_0_, s32[32]{0:T(128)} %refs_1_.7, s32[4]{0:T(128)} %pad_add_fusion.refs_2_.place_ref, bf16[256,768]{1,0:T(8,128)(2,1)} %get-tuple-element.35.refs_3_, bf16[256,768]{1,0:T(8,128)(2,1)} %copy-done, bf16[256,768]{1,0:T(8,128)(2,1)} %copy-done.1, ...), custom_call_target="tpu_custom_call" | custom-call | tf_op jit(solution)/shard_map/attend_last/pallas_call | solution.py:200
  103.2 26.2 %all_to_all.5.r_ref = bf16[16,64,896]{2,1,0:T(8,128)(2,1)} all-to-all(bf16[16,64,896]{2,1,0:T(8,128)(2,1)} %bitcast.5), channel_id=1, replica_groups=mesh['x'=4,'z'=8,'y'=4,'c'=2] {'x','y'}, dimensions={0} | all-to-all | bytes 3670016 | tf_op jit(solution)/shard_map/all_to_all | solution.py:334
  129.3 0.0 all-gather.2.cloned.1.call-done.w_ref
  129.4 9.6 %project.1 = (f32[32,3072]{1,0:T(8,128)}, f32[32,3072]{1,0:T(8,128)}, bf16[2,32,3072]{2,1,0:T(8,128)(2,1)}) custom-call(s32[4]{0:T(128)} %pad_add_fusion.refs_2_.place_ref, bf16[16,64,896]{2,1,0:T(8,128)(2,1)} %all_to_all.5.r_ref, bf16[1536,3072]{1,0:T(8,128)(2,1)} %all-gather.2.cloned.1.call-done.w_ref), custom_call_target="tpu_custom_call" | custom-call | tf_op jit(solution)/shard_map/project/pallas_call | solution.py:259
  138.9 4.6 %collective-permute-start.11 = (bf16[2,32,3072]{2,1,0:T(8,128)(2,1)}, bf16[2,32,3072]{2,1,0:T(8,128)(2,1)S(1)}, u32[]{:S(2)}, u32[]{:S(2)}) collective-permute-start(bf16[2,32,3072]{2,1,0:T(8,128)(2,1)} %get-tuple-element.61), channel_id=1, source_target_pairs={{0,1},{1,0},{2,3},{3,2},{4,5},{5,4},{6,7},{7,6},{8,9},{9,8},{10,11... | collective-permute-start | bytes 1179656 | tf_op jit(solution)/shard_map/ppermute | solution.py:338
  143.5 1.6 %collective-permute-done.11.arrived_ref = bf16[2,32,3072]{2,1,0:T(8,128)(2,1)S(1)} collective-permute-done((bf16[2,32,3072]{2,1,0:T(8,128)(2,1)}, bf16[2,32,3072]{2,1,0:T(8,128)(2,1)S(1)}, u32[]{:S(2)}, u32[]{:S(2)}) %collective-permute-start.11) | collective-permute-done | bytes 393248 | tf_op jit(solution)/shard_map/ppermute | solution.py:338
  145.1 0.0 copy-start.10
  145.1 0.8 copy-done.10
  145.8 2.0 %finish.1 = (bf16[32,3072]{1,0:T(8,128)(2,1)}, bf16[32,3072]{1,0:T(8,128)(2,1)}) custom-call(f32[32,3072]{1,0:T(8,128)} %get-tuple-element.59.main_ref, f32[32,3072]{1,0:T(8,128)} %get-tuple-element.60.tangent_ref, bf16[2,32,3072]{2,1,0:T(8,128)(2,1)} %copy-done.10), custom_call_target="tpu_custom_call" | custom-call | tf_op jit(solution)/shard_map/finish/pallas_call | solution.py:282
  (2 shorter events, 0.1 us)
Async XLA Ops:
  7.2 13.3 %copy-start.11 = (s32[3,64,64]{2,1,0:T(8,128)S(1)}, s32[3,64,64]{2,1,0:T(8,128)}, u32[]{:S(2)}) copy-start(s32[3,64,64]{2,1,0:T(8,128)} %param.15) | copy-start | bytes 147460
  7.2 122.2 %all-gather.2.cloned.1.call-start = ((), (), s32[]{:S(2)}) async-start(), calls=%async_computation.1 | async-start | bytes 11796480 | tf_op jit(solution)/shard_map/all_gather | solution.py:307
  10.4 30.2 %collective-permute-start = (bf16[6,256,256]{2,1,0:T(8,128)(2,1)}, bf16[6,256,256]{2,1,0:T(8,128)(2,1)S(1)}, u32[]{:S(2)}, u32[]{:S(2)}) collective-permute-start(bf16[6,256,256]{2,1,0:T(8,128)(2,1)} %get-tuple-element.32.refs_7_.refs_10_), channel_id=1, source_target_pairs={{0,8},{8,16},{16,24},{24,32},{32,40},{40,48},{48,56},{56,0},{1,9},... | collective-permute-start | bytes 2359304 | tf_op jit(solution)/shard_map/ppermute | solution.py:289
  12.9 27.7 %collective-permute-start.1 = (bf16[6,256,256]{2,1,0:T(8,128)(2,1)}, bf16[6,256,256]{2,1,0:T(8,128)(2,1)}, u32[]{:S(2)}, u32[]{:S(2)}) collective-permute-start(bf16[6,256,256]{2,1,0:T(8,128)(2,1)} %get-tuple-element.32.refs_7_.refs_10_), channel_id=1, source_target_pairs={{0,56},{8,0},{16,8},{24,16},{32,24},{40,32},{48,40},{56,48},{1,57}... | collective-permute-start | bytes 2359304 | tf_op jit(solution)/shard_map/ppermute | solution.py:289
  16.9 10.9 %collective-permute-start.2 = (bf16[256,768]{1,0:T(8,128)(2,1)}, bf16[256,768]{1,0:T(8,128)(2,1)S(1)}, u32[]{:S(2)}, u32[]{:S(2)}) collective-permute-start(bf16[256,768]{1,0:T(8,128)(2,1)} %get-tuple-element.35.refs_3_), channel_id=1, source_target_pairs={{0,192},{64,0},{128,64},{192,128},{1,193},{65,1},{129,65},{193,129... | collective-permute-start | bytes 1179656 | tf_op jit(solution)/shard_map/ppermute | solution.py:289
  19.3 11.1 %collective-permute-start.3 = (bf16[256,768]{1,0:T(8,128)(2,1)}, bf16[256,768]{1,0:T(8,128)(2,1)S(1)}, u32[]{:S(2)}, u32[]{:S(2)}) collective-permute-start(bf16[256,768]{1,0:T(8,128)(2,1)} %get-tuple-element.35.refs_3_), channel_id=1, source_target_pairs={{0,128},{64,192},{128,0},{192,64},{1,129},{65,193},{129,1},{193,65... | collective-permute-start | bytes 1179656 | tf_op jit(solution)/shard_map/ppermute | solution.py:289
  19.8 20.8 %collective-permute-start.4 = (bf16[256,768]{1,0:T(8,128)(2,1)}, bf16[256,768]{1,0:T(8,128)(2,1)S(1)}, u32[]{:S(2)}, u32[]{:S(2)}) collective-permute-start(bf16[256,768]{1,0:T(8,128)(2,1)} %get-tuple-element.35.refs_3_), channel_id=1, source_target_pairs={{0,64},{64,128},{128,192},{192,0},{1,65},{65,129},{129,193},{193,1... | collective-permute-start | bytes 1179656 | tf_op jit(solution)/shard_map/ppermute | solution.py:289
  27.8 16.1 %copy-start = (bf16[256,768]{1,0:T(8,128)(2,1)}, bf16[256,768]{1,0:T(8,128)(2,1)S(1)}, u32[]{:S(2)}) copy-start(bf16[256,768]{1,0:T(8,128)(2,1)S(1)} %collective-permute-done.2.refs_4_) | copy-start | bytes 1179652
  30.4 13.5 %copy-start.1 = (bf16[256,768]{1,0:T(8,128)(2,1)}, bf16[256,768]{1,0:T(8,128)(2,1)S(1)}, u32[]{:S(2)}) copy-start(bf16[256,768]{1,0:T(8,128)(2,1)S(1)} %collective-permute-done.3.refs_5_) | copy-start | bytes 1179652
  40.6 3.4 %copy-start.2 = (bf16[256,768]{1,0:T(8,128)(2,1)}, bf16[256,768]{1,0:T(8,128)(2,1)S(1)}, u32[]{:S(2)}) copy-start(bf16[256,768]{1,0:T(8,128)(2,1)S(1)} %collective-permute-done.4.refs_6_) | copy-start | bytes 1179652
  40.6 3.4 %copy-start.7 = (bf16[6,256,256]{2,1,0:T(8,128)(2,1)}, bf16[6,256,256]{2,1,0:T(8,128)(2,1)S(1)}, u32[]{:S(2)}) copy-start(bf16[6,256,256]{2,1,0:T(8,128)(2,1)S(1)} %collective-permute-done.refs_8_.refs_11_) | copy-start | bytes 2359300
  40.6 20.1 %collective-permute-start.5 = (bf16[6,256,256]{2,1,0:T(8,128)(2,1)S(1)}, bf16[6,256,256]{2,1,0:T(8,128)(2,1)S(1)}, u32[]{:S(2)}, u32[]{:S(2)}) collective-permute-start(bf16[6,256,256]{2,1,0:T(8,128)(2,1)S(1)} %collective-permute-done.refs_8_.refs_11_), channel_id=1, source_target_pairs={{0,8},{8,16},{16,24},{24,32},{32,40},{40,48},{48,56},{56,0},{1,9},... | collective-permute-start | bytes 2359304 | tf_op jit(solution)/shard_map/ppermute | solution.py:289
  40.7 20.0 %collective-permute-start.6 = (bf16[6,256,256]{2,1,0:T(8,128)(2,1)}, bf16[6,256,256]{2,1,0:T(8,128)(2,1)S(1)}, u32[]{:S(2)}, u32[]{:S(2)}) collective-permute-start(bf16[6,256,256]{2,1,0:T(8,128)(2,1)} %collective-permute-done.1.refs_9_.refs_12_), channel_id=1, source_target_pairs={{0,56},{8,0},{16,8},{24,16},{32,24},{40,32},{48,40},{56,48},{1,57}... | collective-permute-start | bytes 2359304 | tf_op jit(solution)/shard_map/ppermute | solution.py:289
  60.7 2.8 %copy-start.5 = (bf16[6,256,256]{2,1,0:T(8,128)(2,1)}, bf16[6,256,256]{2,1,0:T(8,128)(2,1)S(1)}, u32[]{:S(2)}) copy-start(bf16[6,256,256]{2,1,0:T(8,128)(2,1)S(1)} %collective-permute-done.5.refs_7_.refs_9_) | copy-start | bytes 2359300
  60.7 2.8 %copy-start.6 = (bf16[6,256,256]{2,1,0:T(8,128)(2,1)}, bf16[6,256,256]{2,1,0:T(8,128)(2,1)S(1)}, u32[]{:S(2)}) copy-start(bf16[6,256,256]{2,1,0:T(8,128)(2,1)S(1)} %collective-permute-done.6.refs_8_.refs_10_) | copy-start | bytes 2359300
  60.8 19.3 %collective-permute-start.7 = (bf16[6,256,256]{2,1,0:T(8,128)(2,1)S(1)}, bf16[6,256,256]{2,1,0:T(8,128)(2,1)S(1)}, u32[]{:S(2)}, u32[]{:S(2)}) collective-permute-start(bf16[6,256,256]{2,1,0:T(8,128)(2,1)S(1)} %collective-permute-done.5.refs_7_.refs_9_), channel_id=1, source_target_pairs={{0,8},{8,16},{16,24},{24,32},{32,40},{40,48},{48,56},{56,0},{1,9},... | collective-permute-start | bytes 2359304 | tf_op jit(solution)/shard_map/ppermute | solution.py:289
  60.8 19.2 %collective-permute-start.8 = (bf16[6,256,256]{2,1,0:T(8,128)(2,1)S(1)}, bf16[6,256,256]{2,1,0:T(8,128)(2,1)S(1)}, u32[]{:S(2)}, u32[]{:S(2)}) collective-permute-start(bf16[6,256,256]{2,1,0:T(8,128)(2,1)S(1)} %collective-permute-done.6.refs_8_.refs_10_), channel_id=1, source_target_pairs={{0,56},{8,0},{16,8},{24,16},{32,24},{40,32},{48,40},{56,48},{1,57}... | collective-permute-start | bytes 2359304 | tf_op jit(solution)/shard_map/ppermute | solution.py:289
  80.1 2.8 %copy-start.3 = (bf16[6,256,256]{2,1,0:T(8,128)(2,1)}, bf16[6,256,256]{2,1,0:T(8,128)(2,1)S(1)}, u32[]{:S(2)}) copy-start(bf16[6,256,256]{2,1,0:T(8,128)(2,1)S(1)} %collective-permute-done.7.refs_7_.refs_9_) | copy-start | bytes 2359300
  80.1 2.8 %copy-start.4 = (bf16[6,256,256]{2,1,0:T(8,128)(2,1)}, bf16[6,256,256]{2,1,0:T(8,128)(2,1)S(1)}, u32[]{:S(2)}) copy-start(bf16[6,256,256]{2,1,0:T(8,128)(2,1)S(1)} %collective-permute-done.8.refs_8_.refs_10_) | copy-start | bytes 2359300
  80.1 11.9 %collective-permute-start.10 = (bf16[3,256,256]{2,1,0:T(8,128)(2,1)S(1)}, bf16[3,256,256]{2,1,0:T(8,128)(2,1)S(1)}, u32[]{:S(2)}, u32[]{:S(2)}) collective-permute-start(bf16[3,256,256]{2,1,0:T(8,128)(2,1)S(1)} %slice.7), channel_id=1, source_target_pairs={{0,56},{8,0},{16,8},{24,16},{32,24},{40,32},{48,40},{56,48},{1,57}... | collective-permute-start | bytes 1179656 | tf_op jit(solution)/shard_map/ppermute | solution.py:289
  82.8 9.5 %collective-permute-start.9 = (bf16[3,256,256]{2,1,0:T(8,128)(2,1)S(1)}, bf16[3,256,256]{2,1,0:T(8,128)(2,1)S(1)}, u32[]{:S(2)}, u32[]{:S(2)}) collective-permute-start(bf16[3,256,256]{2,1,0:T(8,128)(2,1)S(1)} %slice.6), channel_id=1, source_target_pairs={{0,8},{8,16},{16,24},{24,32},{32,40},{40,48},{48,56},{56,0},{1,9},... | collective-permute-start | bytes 1179656 | tf_op jit(solution)/shard_map/ppermute | solution.py:289
  92.0 0.8 copy-start.8
  92.3 0.7 copy-start.9
  138.9 6.1 %collective-permute-start.11 = (bf16[2,32,3072]{2,1,0:T(8,128)(2,1)}, bf16[2,32,3072]{2,1,0:T(8,128)(2,1)S(1)}, u32[]{:S(2)}, u32[]{:S(2)}) collective-permute-start(bf16[2,32,3072]{2,1,0:T(8,128)(2,1)} %get-tuple-element.61), channel_id=1, source_target_pairs={{0,1},{1,0},{2,3},{3,2},{4,5},{5,4},{6,7},{7,6},{8,9},{9,8},{10,11... | collective-permute-start | bytes 1179656 | tf_op jit(solution)/shard_map/ppermute | solution.py:338
  145.1 0.8 copy-start.10
Sparse Core Ops, SparseCore 0:
  9.8 98.3 all-gather.1

commit v2 on v1

v2 whole, which is shorter than its diff:
```python
import functools
import math

import jax
import jax.numpy as jnp
from jax import lax
from jax.experimental import pallas as pl
from jax.experimental.pallas import tpu as pltpu
from jax.sharding import Mesh
from jax.sharding import PartitionSpec as P

NX, NZ, NY, NC = 4, 8, 4, 2
HEADS_HERE = 3
HEAD_DIM = 128
PAIR = 2 * HEAD_DIM
TILE = 128
TOK = 256
TILES_HERE = TOK // TILE
FRAME_TILES = NX * NZ * TILES_HERE
WIDE = HEADS_HERE * PAIR
PACKED = WIDE + 128
PIECES = 3
WITH_ONES = HEAD_DIM + 16
SLOT_TOK = TOK // NY
DM = 3072
SCALING = HEAD_DIM ** (-0.5)
EXP_SCALE = SCALING * math.log2(math.e)
VERY_LOW = -1e30
VERY_HIGH = 1e30
VMEM_LIMIT = 56 * 1024 * 1024
NT = (((1,), (1,)), ((), ()))


def params():
    return pltpu.CompilerParams(vmem_limit_bytes=VMEM_LIMIT)


def prepare_kernel(q_ref, qt_ref, k_ref, kt_ref, v_ref, vt_ref, qq_ref, kv_ref):
    for h in range(HEADS_HERE):
        cols = pl.ds(h * HEAD_DIM, HEAD_DIM)
        qq_ref[:, pl.ds(h * PAIR, HEAD_DIM)] = qt_ref[:, cols]
        qq_ref[:, pl.ds(h * PAIR + HEAD_DIM, HEAD_DIM)] = q_ref[:, cols]
        kv_ref[h, :, 0:HEAD_DIM] = k_ref[:, cols]
        kv_ref[h, :, HEAD_DIM:PAIR] = kt_ref[:, cols]
        kv_ref[HEADS_HERE + h, 0:HEAD_DIM, :] = v_ref[:, cols].T
        kv_ref[HEADS_HERE + h, HEAD_DIM:PAIR, :] = vt_ref[:, cols].T


def prepare(queries, query_tangent, keys, key_tangent, values, value_tangent):
    return pl.pallas_call(
        prepare_kernel,
        out_shape=(
            jax.ShapeDtypeStruct((TOK, WIDE), jnp.bfloat16),
            jax.ShapeDtypeStruct((2 * HEADS_HERE, TOK, PAIR), jnp.bfloat16),
        ),
        compiler_params=params(),
        name="prepare",
    )(queries, query_tangent, keys, key_tangent, values, value_tangent)


def turned(array):
    size = array.shape[1]
    row = lax.broadcasted_iota(jnp.int32, (size, size), 0)
    col = lax.broadcasted_iota(jnp.int32, (size, size), 1)
    identity = jnp.where(row == col, 1.0, 0.0).astype(jnp.bfloat16)
    return lax.dot_general(identity, array, NT, preferred_element_type=jnp.float32).astype(jnp.bfloat16)


def products(kk, q2):
    s = lax.dot_general(
        kk[:, 0:HEAD_DIM], q2[:, HEAD_DIM:PAIR], NT, preferred_element_type=jnp.float32
    )
    return s, lax.dot_general(kk, q2, NT, preferred_element_type=jnp.float32)


def attend_slot(h, slot, key_blocks, s, t, mask_ref, frame_ref, place_ref, vv_ref, old):
    x, z = place_ref[0], place_ref[1]
    query_frame = frame_ref[((x + slot) & (NX - 1)) * NZ + z]
    lanes = lax.broadcasted_iota(jnp.int32, (1, TOK), 1)
    first = lanes < TILE
    m_old, l_old, d_old, acc_old = old
    lives = []
    m_new = m_old
    for at, offset in enumerate(key_blocks):
        key_frame = frame_ref[x * NZ + ((z + offset) & (NZ - 1))]
        for j in range(TILES_HERE):
            row = (h * FRAME_TILES + query_frame * TILES_HERE) * FRAME_TILES
            col = key_frame * TILES_HERE + j
            live = jnp.where(first, mask_ref[row + col], mask_ref[row + FRAME_TILES + col]) == 1
            tile = at * TILES_HERE + j
            top = jnp.max(s[tile * TILE : (tile + 1) * TILE], axis=0, keepdims=True) * EXP_SCALE
            m_new = jnp.maximum(m_new, jnp.where(live, top, VERY_LOW))
            lives.append(live)
    fade = jnp.exp2(m_old - m_new)
    weights, scaled = [], []
    for tile, live in enumerate(lives):
        rows = slice(tile * TILE, (tile + 1) * TILE)
        w = jnp.exp2(s[rows] * EXP_SCALE - jnp.where(live, m_new, VERY_HIGH))
        weights.append(w.astype(jnp.bfloat16))
        scaled.append((w * t[rows]).astype(jnp.bfloat16))
    o = jnp.dot(vv_ref[...], jnp.concatenate(weights, axis=0), preferred_element_type=jnp.float32)
    o2 = jnp.dot(
        vv_ref[0:WITH_ONES, :], jnp.concatenate(scaled, axis=0), preferred_element_type=jnp.float32
    )
    l_new = l_old * fade + o[HEAD_DIM : HEAD_DIM + 1]
    d_new = d_old * fade + SCALING * o2[HEAD_DIM : HEAD_DIM + 1]
    top = acc_old[0:HEAD_DIM] * fade + o[0:HEAD_DIM]
    bottom = acc_old[HEAD_DIM:PAIR] * fade + (o[WITH_ONES:] + SCALING * o2[0:HEAD_DIM])
    return m_new, l_new, d_new, top, bottom


def attend_kernel(key_blocks, is_first, is_last, *refs):
    count = len(key_blocks)
    mask_ref, frame_ref, place_ref = refs[:3]
    q_refs = refs[3 : 3 + NX]
    rest = refs[3 + NX :]
    kk_refs = [r.at[0] for r in rest[:count]]
    vv_refs = [r.at[0] for r in rest[count : 2 * count]]
    rest = rest[2 * count :]
    if not is_first:
        acc_in, stat_in = rest[:2]
        rest = rest[2:]
    rest, vv_ref = rest[:-1], rest[-1]
    h = pl.program_id(0)
    kk = jnp.concatenate([r[...] for r in kk_refs], axis=0)
    for at in range(count):
        cols = pl.ds(at * TOK, TOK)
        vv_ref[0:HEAD_DIM, cols] = vv_refs[at][0:HEAD_DIM, :]
        vv_ref[HEAD_DIM:WITH_ONES, cols] = jnp.ones((WITH_ONES - HEAD_DIM, TOK), jnp.bfloat16)
        vv_ref[WITH_ONES:, cols] = vv_refs[at][HEAD_DIM:PAIR, :]
    if is_last:
        side_ref = rest[1]

        @pl.when(h == 0)
        def _():
            side_ref[...] = jnp.zeros_like(side_ref)

    ahead = [products(kk, q_refs[slot][...]) for slot in range(NX)]
    for slot in range(NX):
        cols = pl.ds(slot * TOK, TOK)
        if is_first:
            zero = jnp.zeros((1, TOK), jnp.float32)
            old = (zero + VERY_LOW, zero, zero, jnp.zeros((PAIR, TOK), jnp.float32))
        else:
            old = (
                stat_in[0, 0:1, cols],
                stat_in[0, 1:2, cols],
                stat_in[0, 2:3, cols],
                acc_in[0, :, cols],
            )
        m, l, d, top, bottom = attend_slot(
            h, slot, key_blocks, *ahead[slot], mask_ref, frame_ref, place_ref, vv_ref, old
        )
        if not is_last:
            acc_out, stat_out = rest
            stat_out[0, 0:1, cols] = m
            stat_out[0, 1:2, cols] = l
            stat_out[0, 2:3, cols] = d
            acc_out[0, 0:HEAD_DIM, cols] = top
            acc_out[0, HEAD_DIM:PAIR, cols] = bottom
        else:
            out_ref = rest[0]
            some = l > 0.0
            inverse = jnp.where(some, 1.0 / jnp.where(some, l, 1.0), 0.0)
            level = jnp.where(some, m + jnp.log2(jnp.where(some, l, 1.0)), VERY_LOW)
            drift = d * inverse
            attn = top * inverse
            tangent = bottom * inverse - drift * attn
            target = (place_ref[0] + slot) & (NX - 1)
            columns = pl.multiple_of(h * PAIR, PAIR)
            both = jnp.concatenate((attn, tangent), axis=0).astype(jnp.bfloat16)
            out_ref[target, :, pl.ds(columns, PAIR)] = both.T
            for at, value in enumerate((level, drift)):
                left = value
                for p in range(PIECES):
                    piece = left.astype(jnp.bfloat16).astype(jnp.float32)
                    side_ref[slot, pl.ds(8 * p + HEADS_HERE * at + h, 1), :] = piece
                    left = left - piece

    if is_last:

        @pl.when(h == HEADS_HERE - 1)
        def _():
            for slot in range(NX):
                target = (place_ref[0] + slot) & (NX - 1)
                out_ref[target, :, pl.ds(WIDE, 128)] = side_ref[slot].astype(jnp.bfloat16).T


def attend(key_blocks, mask, frames, place, slots, kks, vvs, state, is_last):
    count = len(key_blocks)
    is_first = state is None
    smem = pl.BlockSpec(memory_space=pltpu.SMEM)
    acc_spec = pl.BlockSpec((1, PAIR, NX * TOK), lambda h: (h, 0, 0))
    stat_spec = pl.BlockSpec((1, 8, NX * TOK), lambda h: (h, 0, 0))
    in_specs = [smem] * 3
    in_specs += [pl.BlockSpec((TOK, PAIR), lambda h: (0, h))] * NX
    in_specs += [pl.BlockSpec((1, TOK, PAIR), lambda h: (h, 0, 0))] * count
    for vv in vvs:
        skip = vv.shape[0] - HEADS_HERE
        in_specs.append(pl.BlockSpec((1, PAIR, TOK), lambda h, skip=skip: (skip + h, 0, 0)))
    operands = [mask, frames, place, *slots, *kks, *vvs]
    if not is_first:
        in_specs += [acc_spec, stat_spec]
        operands += list(state)
    scratch = [pltpu.VMEM((WITH_ONES + HEAD_DIM, count * TOK), jnp.bfloat16)]
    if is_last:
        out_shape = jax.ShapeDtypeStruct((NX, TOK, PACKED), jnp.bfloat16)
        out_specs = pl.BlockSpec((NX, TOK, PACKED), lambda h: (0, 0, 0))
        scratch = [pltpu.VMEM((NX, 128, TOK), jnp.float32)] + scratch
    else:
        out_shape = (
            jax.ShapeDtypeStruct((HEADS_HERE, PAIR, NX * TOK), jnp.float32),
            jax.ShapeDtypeStruct((HEADS_HERE, 8, NX * TOK), jnp.float32),
        )
        out_specs = (acc_spec, stat_spec)
    return pl.pallas_call(
        functools.partial(attend_kernel, key_blocks, is_first, is_last),
        grid=(HEADS_HERE,),
        in_specs=in_specs,
        out_specs=out_specs,
        out_shape=out_shape,
        scratch_shapes=scratch,
        compiler_params=params(),
        cost_estimate=pl.CostEstimate(
            flops=count * NX * HEADS_HERE * 12 * TOK * TOK * HEAD_DIM,
            transcendentals=count * NX * HEADS_HERE * TOK * TOK,
            bytes_accessed=8 * 1024 * 1024,
        ),
        name="attend_last" if is_last else "attend",
    )(*operands)


COLS = 512


def project_kernel(place_ref, *refs):
    sources, (main_ref, tangent_ref, other_ref, mixed, r_ref) = refs[:6], refs[6:11]
    targets, sems = (r_ref,) + refs[11:16], refs[16]
    copies = [
        pltpu.make_async_copy(source, target, sems.at[i])
        for i, (source, target) in enumerate(zip(sources, targets))
    ]
    for copy in copies:
        copy.start()
    y, c = place_ref[2], place_ref[3]
    copies[0].wait()
    for rel, shift in enumerate((0, NY - 1, 1, 2)):
        group = (y + shift) & (NY - 1)
        sides = []
        for x in range(NX):
            side = r_ref[x * NY + group, :, pl.ds(WIDE, 128)].astype(jnp.float32)
            sides.append(side + (pltpu.roll(side, 128 - 8, 1) + pltpu.roll(side, 128 - 16, 1)))
        top = functools.reduce(jnp.maximum, sides)
        shares = [jnp.exp2(side - top) for side in sides]
        inverse = 1.0 / sum(shares)
        shares = [share * inverse for share in shares]
        drifts = [pltpu.roll(side, 128 - HEADS_HERE, 1) for side in sides]
        drift = sum(s * d for s, d in zip(shares, drifts))
        moves = [s * (d - drift) for s, d in zip(shares, drifts)]
        for h in range(HEADS_HERE):
            attn, tangent = 0.0, 0.0
            for x in range(NX):
                a = r_ref[x * NY + group, :, pl.ds(h * PAIR, HEAD_DIM)].astype(jnp.float32)
                t = r_ref[x * NY + group, :, pl.ds(h * PAIR + HEAD_DIM, HEAD_DIM)].astype(jnp.float32)
                share = shares[x][:, h : h + 1]
                attn = attn + share * a
                tangent = tangent + share * t + moves[x][:, h : h + 1] * a
            cols = pl.ds((rel * HEADS_HERE + h) * HEAD_DIM, HEAD_DIM)
            mixed[0:SLOT_TOK, cols] = attn.astype(jnp.bfloat16)
            mixed[SLOT_TOK : 2 * SLOT_TOK, cols] = tangent.astype(jnp.bfloat16)

    for copy in copies[1:]:
        copy.wait()
    half = SLOT_TOK // NC
    mine = c == 0
    for column in range(0, DM, COLS):
        cols = pl.ds(column, COLS)
        total, start = 0.0, 0
        for ref in targets[1:]:
            rows = pl.ds(start, ref.shape[0])
            start += ref.shape[0]
            total = total + jnp.dot(mixed[:, rows], ref[:, cols], preferred_element_type=jnp.float32)
        for which, own_ref in enumerate((main_ref, tangent_ref)):
            low = total[which * SLOT_TOK : which * SLOT_TOK + half]
            high = total[which * SLOT_TOK + half : (which + 1) * SLOT_TOK]
            own_ref[:, cols] = jnp.where(mine, low, high)
            other_ref[which, :, cols] = jnp.where(mine, high, low).astype(jnp.bfloat16)


def project(place, received, weights):
    half = SLOT_TOK // NC
    own_shape = jax.ShapeDtypeStruct((half, DM), jnp.float32)
    anywhere = pl.BlockSpec(memory_space=pltpu.HBM)
    operands = (received, *weights)
    return pl.pallas_call(
        project_kernel,
        in_specs=[pl.BlockSpec(memory_space=pltpu.SMEM)] + [anywhere] * len(operands),
        out_shape=(own_shape, own_shape, jax.ShapeDtypeStruct((2, half, DM), jnp.bfloat16)),
        scratch_shapes=[
            pltpu.VMEM((2 * SLOT_TOK, NY * HEADS_HERE * HEAD_DIM), jnp.bfloat16),
            *[pltpu.VMEM(operand.shape, operand.dtype) for operand in operands],
            pltpu.SemaphoreType.DMA((len(operands),)),
        ],
        compiler_params=params(),
        name="project",
    )(place, *operands)


def finish_kernel(main_ref, tangent_ref, arrived_ref, out_ref, tout_ref):
    out_ref[...] = (main_ref[...] + arrived_ref[0].astype(jnp.float32)).astype(jnp.bfloat16)
    tout_ref[...] = (tangent_ref[...] + arrived_ref[1].astype(jnp.float32)).astype(jnp.bfloat16)


def finish(main, tangent, arrived):
    shape = jax.ShapeDtypeStruct(main.shape, jnp.bfloat16)
    return pl.pallas_call(
        finish_kernel, out_shape=(shape, shape), compiler_params=params(), name="finish"
    )(main, tangent, arrived)


def shifted(block, axis, distance):
    size = lax.axis_size(axis)
    return lax.ppermute(block, axis, [(i, (i + distance) % size) for i in range(size)])


def after(array, *others):
    return lax.optimization_barrier((array, *others))[0]


def body(
    queries,
    keys,
    values,
    query_tangent,
    key_tangent,
    value_tangent,
    tile_mask,
    block_frame,
    out_weight,
):
    place = jnp.stack([lax.axis_index(a) for a in ("x", "z", "y", "c")]).astype(jnp.int32)
    mask = tile_mask.reshape(-1)
    qq, bundle = prepare(queries, query_tangent, keys, key_tangent, values, value_tangent)

    left_1 = shifted(bundle, "z", 1)
    right_1 = shifted(bundle, "z", -1)
    slot_1 = shifted(qq, "x", -1)
    slot_3 = shifted(after(qq, slot_1), "x", 1)
    slot_2 = shifted(after(qq, slot_3), "x", 2)
    slots = [qq, slot_1, slot_2, slot_3]
    weight_left = shifted(out_weight, "y", 1)
    weight_right = shifted(out_weight, "y", -1)

    def run(key_blocks, kks, vvs, state, is_last=False):
        return attend(key_blocks, mask, block_frame, place, slots, kks, vvs, state, is_last)

    left_2 = shifted(left_1, "z", 1)
    right_2 = shifted(right_1, "z", -1)
    left_3 = shifted(left_2, "z", 1)
    right_3 = shifted(right_2, "z", -1)
    blocks = (bundle, left_1, right_1)
    state = run((0, -1, 1), blocks, blocks, None)

    weight_left, weight_right, _ = lax.optimization_barrier((weight_left, weight_right, state[1]))
    half = out_weight.shape[0] // 2
    far_a = shifted(weight_left[:half], "y", 1)
    far_b = shifted(weight_right[half:], "y", -1)

    held_left, held_right, _ = lax.optimization_barrier((left_3, right_3, state[1]))
    far_keys = shifted(held_left[:HEADS_HERE], "z", 1)
    far_values = shifted(held_right[HEADS_HERE:], "z", -1)
    blocks = (left_2, right_2, left_3, right_3)
    state = run((-2, 2, -3, 3), blocks, blocks, state)

    packed = run((4,), (far_keys,), (far_values,), state, is_last=True)
    packed, far_a, far_b = lax.optimization_barrier((packed, far_a, far_b))
    received = lax.all_to_all(
        packed.reshape(NX * NY, SLOT_TOK, PACKED), ("x", "y"), 0, 0, tiled=True
    )
    weights = (out_weight, weight_left, weight_right, far_a, far_b)
    main, tangent, other = project(place, received, weights)
    arrived = lax.ppermute(other, "c", [(0, 1), (1, 0)])
    return finish(main, tangent, arrived)


def solution(mesh):
    inner = Mesh(mesh.devices.reshape(NX, NZ, NY, NC), ("x", "z", "y", "c"))
    blk, head = ("x", "z"), ("y", "c")
    in_specs = (
        P(blk, head),
        P(blk, head),
        P(blk, head),
        P(blk, head),
        P(blk, head),
        P(blk, head),
        P(head, None, None),
        P(),
        P(head, None),
    )
    out_specs = (P(blk + head, None), P(blk + head, None))
    return jax.shard_map(body, mesh=inner, in_specs=in_specs, out_specs=out_specs, check_vma=False)
```

time: 155 us -> 134 us (0.86)
  Pallas kernels: 54.8 us -> 38.3 us
  between operations: 14.1 us -> 0.8 us
  starting transfers between devices: 22.9 us -> 30.3 us
  local copies, waits for them, and re-layouts: 2.28 us -> 8.23 us
  waiting for transfers between devices: 33.9 us -> 29.8 us
    pallas_call x4 -> x3, Pallas kernels: 40.7 us -> 26 us  [attend(): pl.pallas_call(functools.partial(attend_kernel, key_blocks, is_first, is_...]
    ppermute x11 -> x15, starting transfers between devices: 18.2 us -> 24.2 us  [shifted(): lax.ppermute(block, axis, [(i, (i + distance) % size) for i in range(size)])]
    slice x2 -> x4, local copies, waits for them, and re-layouts: 0.05 us -> 4.23 us  [the longest x1 2.11 us: body(): far_b = shifted(weight_right[half:], 'y', -1)]
    ppermute x11 -> x15, waiting for transfers between devices: 31.6 us -> 28.3 us  [shifted(): lax.ppermute(block, axis, [(i, (i + distance) % size) for i in range(size)])]
    pallas_call x1, Pallas kernels: 9.56 us -> 7.77 us  [project(): pl.pallas_call(project_kernel, in_specs=[pl.BlockSpec(memory_space=pltpu....]
    ppermute x1, starting transfers between devices: 4.59 us -> 6.17 us  [body(): arrived = lax.ppermute(other, 'c', [(0, 1), (1, 0)])]
  transfers between devices with their start and end apart: 13 -> 16, of which waited for: 7 -> 7; matrix products, arithmetic and copies ran while one was open for 1% -> 5% of each run, Pallas kernels for 28% -> 21%
where the time goes in v2:
time: 134 us; the launch traced here: 133 us
  Pallas kernels  38.3 us (29%)
  starting transfers between devices  30.3 us (23%)
  waiting for transfers between devices  29.8 us (22%)
  blocking collectives  25.3 us (19%)
  local copies, waits for them, and re-layouts  8.23 us (6%)
    ppermute x15, waiting for transfers between devices, shifted(): lax.ppermute(block, axis, [(i, (i + distance) % size) for i in range(size)])  28.3 us
    pallas_call x3, Pallas kernels, attend(): pl.pallas_call(functools.partial(attend_kernel, key_blocks, is_first, is_...  26 us
    all_to_all x1, blocking collectives, body(): lax.all_to_all(packed.reshape(NX * NY, SLOT_TOK, PACKED), ('x', 'y'), 0,...  25.3 us
    ppermute x15, starting transfers between devices, shifted(): lax.ppermute(block, axis, [(i, (i + distance) % size) for i in range(size)])  24.2 us
    pallas_call x1, Pallas kernels, project(): pl.pallas_call(project_kernel, in_specs=[pl.BlockSpec(memory_space=pltpu....  7.77 us
    ppermute x1, starting transfers between devices, body(): arrived = lax.ppermute(other, 'c', [(0, 1), (1, 0)])  6.17 us
  transfers between devices with their start and end apart: 16, of which 7 were waited for; matrix products, arithmetic and copies ran while one was open for 5% of the time, Pallas kernels for 21%

profile of v2, /device:TPU:1, one launch (start us, length us, event | category | flops | bytes accessed | tf_op | source)
XLA Modules:
  0.0 133.3 jit_solution(14073210635923976537)
XLA Ops:
  0.6 2.2 %collective-permute-start.11 = (bf16[384,3072]{1,0:T(8,128)(2,1)}, bf16[384,3072]{1,0:T(8,128)(2,1)S(1)}, u32[]{:S(2)}, u32[]{:S(2)}) collective-permute-start(bf16[384,3072]{1,0:T(8,128)(2,1)} %refs_1_.7), channel_id=1, source_target_pairs={{0,2},{2,4},{4,6},{6,0},{1,3},{3,5},{5,7},{7,1},{8,10},{10,12},{12... | collective-permute-start | bytes 7077896 | tf_op jit(solution)/shard_map/ppermute | solution.py:323
  2.8 1.5 %collective-permute-start.12 = (bf16[384,3072]{1,0:T(8,128)(2,1)}, bf16[384,3072]{1,0:T(8,128)(2,1)}, u32[]{:S(2)}, u32[]{:S(2)}) collective-permute-start(bf16[384,3072]{1,0:T(8,128)(2,1)} %refs_1_.7), channel_id=1, source_target_pairs={{0,6},{2,0},{4,2},{6,4},{1,7},{3,1},{5,3},{7,5},{8,14},{10,8},{12,... | collective-permute-start | bytes 7077896 | tf_op jit(solution)/shard_map/ppermute | solution.py:323
  4.4 2.5 %prepare.1 = (bf16[256,768]{1,0:T(8,128)(2,1)}, bf16[6,256,256]{2,1,0:T(8,128)(2,1)}) custom-call(bf16[256,384]{1,0:T(8,128)(2,1)} %q_ref.1, bf16[256,384]{1,0:T(8,128)(2,1)} %qt_ref.1, bf16[256,384]{1,0:T(8,128)(2,1)} %k_ref.1, bf16[256,384]{1,0:T(8,128)(2,1)} %kt_ref.1, bf16[256,384]{1,0:T(8,128)(2,1)} %v_ref.1, bf16[256,384]{1,0:T(8,128)(2,1)} %vt_ref.1), custom_call_target="tpu_custom_call" | custom-call | tf_op jit(solution)/shard_map/prepare/pallas_call | solution.py:50
  6.9 5.6 %collective-permute-start.6 = (bf16[6,256,256]{2,1,0:T(8,128)(2,1)}, bf16[6,256,256]{2,1,0:T(8,128)(2,1)}, u32[]{:S(2)}, u32[]{:S(2)}) collective-permute-start(bf16[6,256,256]{2,1,0:T(8,128)(2,1)} %get-tuple-element.23.refs_7_.refs_10_), channel_id=1, source_target_pairs={{0,56},{8,0},{16,8},{24,16},{32,24},{40,32},{48,40},{56,48},{1,57}... | collective-permute-start | bytes 2359304 | tf_op jit(solution)/shard_map/ppermute | solution.py:323
  12.5 0.0 collective-permute-start.3
  12.5 2.5 %collective-permute-start = (bf16[256,768]{1,0:T(8,128)(2,1)}, bf16[256,768]{1,0:T(8,128)(2,1)S(1)}, u32[]{:S(2)}, u32[]{:S(2)}) collective-permute-start(bf16[256,768]{1,0:T(8,128)(2,1)} %get-tuple-element.22.refs_3_), channel_id=1, source_target_pairs={{0,192},{64,0},{128,64},{192,128},{1,193},{65,1},{129,65},{193,129... | collective-permute-start | bytes 1179656 | tf_op jit(solution)/shard_map/ppermute | solution.py:323
  14.9 7.4 %collective-permute-done.refs_4_ = bf16[256,768]{1,0:T(8,128)(2,1)S(1)} collective-permute-done((bf16[256,768]{1,0:T(8,128)(2,1)}, bf16[256,768]{1,0:T(8,128)(2,1)S(1)}, u32[]{:S(2)}, u32[]{:S(2)}) %collective-permute-start) | collective-permute-done | bytes 393248 | tf_op jit(solution)/shard_map/ppermute | solution.py:323
  22.3 0.0 copy-start.3
  22.3 0.9 collective-permute-start.1
  23.2 5.3 %collective-permute-done.6.refs_9_.refs_12_ = bf16[6,256,256]{2,1,0:T(8,128)(2,1)} collective-permute-done((bf16[6,256,256]{2,1,0:T(8,128)(2,1)}, bf16[6,256,256]{2,1,0:T(8,128)(2,1)}, u32[]{:S(2)}, u32[]{:S(2)}) %collective-permute-start.6) | collective-permute-done | bytes 786464 | tf_op jit(solution)/shard_map/ppermute | solution.py:323
  28.5 3.4 %collective-permute-start.7 = (bf16[6,256,256]{2,1,0:T(8,128)(2,1)}, bf16[6,256,256]{2,1,0:T(8,128)(2,1)}, u32[]{:S(2)}, u32[]{:S(2)}) collective-permute-start(bf16[6,256,256]{2,1,0:T(8,128)(2,1)} %collective-permute-done.6.refs_9_.refs_12_), channel_id=1, source_target_pairs={{0,56},{8,0},{16,8},{24,16},{32,24},{40,32},{48,40},{56,48},{1,57}... | collective-permute-start | bytes 2359304 | tf_op jit(solution)/shard_map/ppermute | solution.py:323
  31.9 0.0 collective-permute-done.3.refs_8_.refs_11_
  31.9 0.0 collective-permute-start.4
  31.9 1.3 collective-permute-done.1.refs_6_
  33.3 0.0 copy-start.4
  33.3 1.5 %collective-permute-start.2 = (bf16[256,768]{1,0:T(8,128)(2,1)}, bf16[256,768]{1,0:T(8,128)(2,1)S(1)}, u32[]{:S(2)}, u32[]{:S(2)}) collective-permute-start(bf16[256,768]{1,0:T(8,128)(2,1)} %get-tuple-element.22.refs_3_), channel_id=1, source_target_pairs={{0,128},{64,192},{128,0},{192,64},{1,129},{65,193},{129,1},{193,65... | collective-permute-start | bytes 1179656 | tf_op jit(solution)/shard_map/ppermute | solution.py:323
  34.8 1.6 %reshape.10.refs_0_ = s32[12288]{0:T(1024)} reshape(s32[3,64,64]{2,1,0:T(8,128)} %param.15) | data formatting | bytes 98304 | tf_op jit(solution)/shard_map/reshape | solution.py:342
  36.4 0.6 pad_add_fusion.refs_2_.place_ref
  37.0 10.1 %collective-permute-done.7.refs_8_.refs_12_ = bf16[6,256,256]{2,1,0:T(8,128)(2,1)} collective-permute-done((bf16[6,256,256]{2,1,0:T(8,128)(2,1)}, bf16[6,256,256]{2,1,0:T(8,128)(2,1)}, u32[]{:S(2)}, u32[]{:S(2)}) %collective-permute-start.7) | collective-permute-done | bytes 786464 | tf_op jit(solution)/shard_map/ppermute | solution.py:323
  47.1 3.4 %collective-permute-start.8 = (bf16[6,256,256]{2,1,0:T(8,128)(2,1)}, bf16[6,256,256]{2,1,0:T(8,128)(2,1)}, u32[]{:S(2)}, u32[]{:S(2)}) collective-permute-start(bf16[6,256,256]{2,1,0:T(8,128)(2,1)} %collective-permute-done.7.refs_8_.refs_12_), channel_id=1, source_target_pairs={{0,56},{8,0},{16,8},{24,16},{32,24},{40,32},{48,40},{56,48},{1,57}... | collective-permute-start | bytes 2359304 | tf_op jit(solution)/shard_map/ppermute | solution.py:323
  50.5 0.0 collective-permute-done.4.refs_7_.refs_11_
  50.5 0.0 collective-permute-start.5
  50.5 0.0 collective-permute-done.2.refs_5_
  50.5 0.0 copy-done.3
  50.5 0.0 copy-done.4
  50.5 0.0 copy-start.5
  50.5 0.7 copy-done.5
  51.3 8.6 %attend.2 = (f32[3,256,1024]{2,1,0:T(8,128)}, f32[3,8,1024]{2,1,0:T(8,128)}) custom-call(s32[12288]{0:T(1024)} %reshape.10.refs_0_, s32[32]{0:T(128)} %refs_1_.6, s32[4]{0:T(128)} %pad_add_fusion.refs_2_.place_ref, bf16[256,768]{1,0:T(8,128)(2,1)} %get-tuple-element.22.refs_3_, bf16[256,768]{1,0:T(8,128)(2,1)} %copy-done.3, bf16[256,768]{1,0:T(8,128)(2,1)} %copy-done.5, ...), custom_call_target="tpu_custom_call" | custom-call | flops 3623878656 | bytes 8388608 | tf_op jit(solution)/shard_map/attend/pallas_call | solution.py:216
  59.9 0.0 collective-permute-done.11.refs_2_
  59.9 0.0 copy-start
  59.9 0.0 collective-permute-done.12.refs_3_
  59.9 0.1 slice.14
  60.0 2.1 %slice.15 = bf16[192,3072]{1,0:T(8,128)(2,1)S(1)} slice(bf16[384,3072]{1,0:T(8,128)(2,1)} %collective-permute-done.12.refs_3_), slice={[192:384], [0:3072]} | slice | bytes 2359296 | tf_op jit(solution)/shard_map/slice | solution.py:367
  62.1 0.0 copy-done
  62.1 1.1 collective-permute-start.14
  63.3 0.4 collective-permute-start.13
  63.7 1.0 collective-permute-done.8.refs_10_.refs_14_
  64.7 3.1 %collective-permute-done.5.refs_9_.refs_13_ = bf16[6,256,256]{2,1,0:T(8,128)(2,1)} collective-permute-done((bf16[6,256,256]{2,1,0:T(8,128)(2,1)}, bf16[6,256,256]{2,1,0:T(8,128)(2,1)}, u32[]{:S(2)}, u32[]{:S(2)}) %collective-permute-start.5) | collective-permute-done | bytes 786464 | tf_op jit(solution)/shard_map/ppermute | solution.py:323
  67.8 1.0 slice.12
  68.9 1.0 slice.13
  69.9 0.4 collective-permute-start.10
  70.2 1.2 collective-permute-start.9
  71.4 10.8 %attend.3 = (f32[3,256,1024]{2,1,0:T(8,128)}, f32[3,8,1024]{2,1,0:T(8,128)}) custom-call(s32[12288]{0:T(1024)} %reshape.10.refs_0_, s32[32]{0:T(128)} %refs_1_.6, s32[4]{0:T(128)} %pad_add_fusion.refs_2_.place_ref, bf16[256,768]{1,0:T(8,128)(2,1)} %get-tuple-element.22.refs_3_, bf16[256,768]{1,0:T(8,128)(2,1)} %copy-done.3, bf16[256,768]{1,0:T(8,128)(2,1)} %copy-done.5, ...), custom_call_target="tpu_custom_call" | custom-call | flops 4831838208 | bytes 8388608 | tf_op jit(solution)/shard_map/attend/pallas_call | solution.py:216
  82.2 0.0 collective-permute-done.10.refs_8_
  82.3 0.0 copy-start.6
  82.3 0.0 collective-permute-done.9.refs_7_
  82.3 0.0 copy-start.7
  82.3 0.7 copy-done.6
  83.0 0.2 copy-done.7
  83.2 6.6 %attend_last.1 = bf16[4,256,896]{2,1,0:T(8,128)(2,1)} custom-call(s32[12288]{0:T(1024)} %reshape.10.refs_0_, s32[32]{0:T(128)} %refs_1_.6, s32[4]{0:T(128)} %pad_add_fusion.refs_2_.place_ref, bf16[256,768]{1,0:T(8,128)(2,1)} %get-tuple-element.22.refs_3_, bf16[256,768]{1,0:T(8,128)(2,1)} %copy-done.3, bf16[256,768]{1,0:T(8,128)(2,1)} %copy-done.5, ...), custom_call_target="tpu_custom_call" | custom-call | flops 1207959552 | bytes 8388608 | tf_op jit(solution)/shard_map/attend_last/pallas_call | solution.py:216
  89.7 0.0 collective-permute-done.14.refs_5_
  89.7 0.0 copy-start.1
  89.8 0.0 collective-permute-done.13.refs_4_
  89.8 0.0 copy-start.2
  89.8 25.3 %all_to_all.5.refs_0_ = bf16[16,64,896]{2,1,0:T(8,128)(2,1)} all-to-all(bf16[16,64,896]{2,1,0:T(8,128)(2,1)} %bitcast.5), channel_id=1, replica_groups=mesh['x'=4,'z'=8,'y'=4,'c'=2] {'x','y'}, dimensions={0} | all-to-all | bytes 3670016 | tf_op jit(solution)/shard_map/all_to_all | solution.py:377
  115.0 0.0 copy-done.1
  115.0 0.0 copy-done.2
  115.0 7.8 %project.1 = (f32[32,3072]{1,0:T(8,128)}, f32[32,3072]{1,0:T(8,128)}, bf16[2,32,3072]{2,1,0:T(8,128)(2,1)}) custom-call(s32[4]{0:T(128)} %pad_add_fusion.refs_2_.place_ref, bf16[16,64,896]{2,1,0:T(8,128)(2,1)} %all_to_all.5.refs_0_, bf16[384,3072]{1,0:T(8,128)(2,1)} %refs_1_.7, bf16[384,3072]{1,0:T(8,128)(2,1)} %copy-done, ...), custom_call_target="tpu_custom_call" | custom-call | tf_op jit(solution)/shard_map/project/pallas_call | solution.py:295
  122.8 6.2 %collective-permute-start.15 = (bf16[2,32,3072]{2,1,0:T(8,128)(2,1)}, bf16[2,32,3072]{2,1,0:T(8,128)(2,1)S(1)}, u32[]{:S(2)}, u32[]{:S(2)}) collective-permute-start(bf16[2,32,3072]{2,1,0:T(8,128)(2,1)} %get-tuple-element.37), channel_id=1, source_target_pairs={{0,1},{1,0},{2,3},{3,2},{4,5},{5,4},{6,7},{7,6},{8,9},{9,8},{10,11... | collective-permute-start | bytes 1179656 | tf_op jit(solution)/shard_map/ppermute | solution.py:382
  129.0 1.6 %collective-permute-done.15.arrived_ref = bf16[2,32,3072]{2,1,0:T(8,128)(2,1)S(1)} collective-permute-done((bf16[2,32,3072]{2,1,0:T(8,128)(2,1)}, bf16[2,32,3072]{2,1,0:T(8,128)(2,1)S(1)}, u32[]{:S(2)}, u32[]{:S(2)}) %collective-permute-start.15) | collective-permute-done | bytes 393248 | tf_op jit(solution)/shard_map/ppermute | solution.py:382
  130.6 0.0 copy-start.8
  130.6 0.8 copy-done.8
  131.3 2.0 %finish.1 = (bf16[32,3072]{1,0:T(8,128)(2,1)}, bf16[32,3072]{1,0:T(8,128)(2,1)}) custom-call(f32[32,3072]{1,0:T(8,128)} %get-tuple-element.35.main_ref, f32[32,3072]{1,0:T(8,128)} %get-tuple-element.36.tangent_ref, bf16[2,32,3072]{2,1,0:T(8,128)(2,1)} %copy-done.8), custom_call_target="tpu_custom_call" | custom-call | tf_op jit(solution)/shard_map/finish/pallas_call | solution.py:316
Async XLA Ops:
  0.6 59.3 %collective-permute-start.11 = (bf16[384,3072]{1,0:T(8,128)(2,1)}, bf16[384,3072]{1,0:T(8,128)(2,1)S(1)}, u32[]{:S(2)}, u32[]{:S(2)}) collective-permute-start(bf16[384,3072]{1,0:T(8,128)(2,1)} %refs_1_.7), channel_id=1, source_target_pairs={{0,2},{2,4},{4,6},{6,0},{1,3},{3,5},{5,7},{7,1},{8,10},{10,12},{12... | collective-permute-start | bytes 7077896 | tf_op jit(solution)/shard_map/ppermute | solution.py:323
  2.8 57.1 %collective-permute-start.12 = (bf16[384,3072]{1,0:T(8,128)(2,1)}, bf16[384,3072]{1,0:T(8,128)(2,1)}, u32[]{:S(2)}, u32[]{:S(2)}) collective-permute-start(bf16[384,3072]{1,0:T(8,128)(2,1)} %refs_1_.7), channel_id=1, source_target_pairs={{0,6},{2,0},{4,2},{6,4},{1,7},{3,1},{5,3},{7,5},{8,14},{10,8},{12,... | collective-permute-start | bytes 7077896 | tf_op jit(solution)/shard_map/ppermute | solution.py:323
  6.9 21.6 %collective-permute-start.6 = (bf16[6,256,256]{2,1,0:T(8,128)(2,1)}, bf16[6,256,256]{2,1,0:T(8,128)(2,1)}, u32[]{:S(2)}, u32[]{:S(2)}) collective-permute-start(bf16[6,256,256]{2,1,0:T(8,128)(2,1)} %get-tuple-element.23.refs_7_.refs_10_), channel_id=1, source_target_pairs={{0,56},{8,0},{16,8},{24,16},{32,24},{40,32},{48,40},{56,48},{1,57}... | collective-permute-start | bytes 2359304 | tf_op jit(solution)/shard_map/ppermute | solution.py:323
  12.5 19.5 %collective-permute-start.3 = (bf16[6,256,256]{2,1,0:T(8,128)(2,1)}, bf16[6,256,256]{2,1,0:T(8,128)(2,1)}, u32[]{:S(2)}, u32[]{:S(2)}) collective-permute-start(bf16[6,256,256]{2,1,0:T(8,128)(2,1)} %get-tuple-element.23.refs_7_.refs_10_), channel_id=1, source_target_pairs={{0,8},{8,16},{16,24},{24,32},{32,40},{40,48},{48,56},{56,0},{1,9},... | collective-permute-start | bytes 2359304 | tf_op jit(solution)/shard_map/ppermute | solution.py:323
  12.5 9.8 %collective-permute-start = (bf16[256,768]{1,0:T(8,128)(2,1)}, bf16[256,768]{1,0:T(8,128)(2,1)S(1)}, u32[]{:S(2)}, u32[]{:S(2)}) collective-permute-start(bf16[256,768]{1,0:T(8,128)(2,1)} %get-tuple-element.22.refs_3_), channel_id=1, source_target_pairs={{0,192},{64,0},{128,64},{192,128},{1,193},{65,1},{129,65},{193,129... | collective-permute-start | bytes 1179656 | tf_op jit(solution)/shard_map/ppermute | solution.py:323
  22.3 28.2 %copy-start.3 = (bf16[256,768]{1,0:T(8,128)(2,1)}, bf16[256,768]{1,0:T(8,128)(2,1)S(1)}, u32[]{:S(2)}) copy-start(bf16[256,768]{1,0:T(8,128)(2,1)S(1)} %collective-permute-done.refs_4_) | copy-start | bytes 1179652
  22.3 11.0 %collective-permute-start.1 = (bf16[256,768]{1,0:T(8,128)(2,1)}, bf16[256,768]{1,0:T(8,128)(2,1)S(1)}, u32[]{:S(2)}, u32[]{:S(2)}) collective-permute-start(bf16[256,768]{1,0:T(8,128)(2,1)} %get-tuple-element.22.refs_3_), channel_id=1, source_target_pairs={{0,64},{64,128},{128,192},{192,0},{1,65},{65,129},{129,193},{193,1... | collective-permute-start | bytes 1179656 | tf_op jit(solution)/shard_map/ppermute | solution.py:323
  28.5 18.6 %collective-permute-start.7 = (bf16[6,256,256]{2,1,0:T(8,128)(2,1)}, bf16[6,256,256]{2,1,0:T(8,128)(2,1)}, u32[]{:S(2)}, u32[]{:S(2)}) collective-permute-start(bf16[6,256,256]{2,1,0:T(8,128)(2,1)} %collective-permute-done.6.refs_9_.refs_12_), channel_id=1, source_target_pairs={{0,56},{8,0},{16,8},{24,16},{32,24},{40,32},{48,40},{56,48},{1,57}... | collective-permute-start | bytes 2359304 | tf_op jit(solution)/shard_map/ppermute | solution.py:323
  31.9 18.6 %collective-permute-start.4 = (bf16[6,256,256]{2,1,0:T(8,128)(2,1)}, bf16[6,256,256]{2,1,0:T(8,128)(2,1)}, u32[]{:S(2)}, u32[]{:S(2)}) collective-permute-start(bf16[6,256,256]{2,1,0:T(8,128)(2,1)} %collective-permute-done.3.refs_8_.refs_11_), channel_id=1, source_target_pairs={{0,8},{8,16},{16,24},{24,32},{32,40},{40,48},{48,56},{56,0},{1,9},... | collective-permute-start | bytes 2359304 | tf_op jit(solution)/shard_map/ppermute | solution.py:323
  33.3 17.2 %copy-start.4 = (bf16[256,768]{1,0:T(8,128)(2,1)}, bf16[256,768]{1,0:T(8,128)(2,1)S(1)}, u32[]{:S(2)}) copy-start(bf16[256,768]{1,0:T(8,128)(2,1)S(1)} %collective-permute-done.1.refs_6_) | copy-start | bytes 1179652
  33.3 17.2 %collective-permute-start.2 = (bf16[256,768]{1,0:T(8,128)(2,1)}, bf16[256,768]{1,0:T(8,128)(2,1)S(1)}, u32[]{:S(2)}, u32[]{:S(2)}) collective-permute-start(bf16[256,768]{1,0:T(8,128)(2,1)} %get-tuple-element.22.refs_3_), channel_id=1, source_target_pairs={{0,128},{64,192},{128,0},{192,64},{1,129},{65,193},{129,1},{193,65... | collective-permute-start | bytes 1179656 | tf_op jit(solution)/shard_map/ppermute | solution.py:323
  47.1 17.6 %collective-permute-start.8 = (bf16[6,256,256]{2,1,0:T(8,128)(2,1)}, bf16[6,256,256]{2,1,0:T(8,128)(2,1)}, u32[]{:S(2)}, u32[]{:S(2)}) collective-permute-start(bf16[6,256,256]{2,1,0:T(8,128)(2,1)} %collective-permute-done.7.refs_8_.refs_12_), channel_id=1, source_target_pairs={{0,56},{8,0},{16,8},{24,16},{32,24},{40,32},{48,40},{56,48},{1,57}... | collective-permute-start | bytes 2359304 | tf_op jit(solution)/shard_map/ppermute | solution.py:323
  50.5 17.4 %collective-permute-start.5 = (bf16[6,256,256]{2,1,0:T(8,128)(2,1)}, bf16[6,256,256]{2,1,0:T(8,128)(2,1)}, u32[]{:S(2)}, u32[]{:S(2)}) collective-permute-start(bf16[6,256,256]{2,1,0:T(8,128)(2,1)} %collective-permute-done.4.refs_7_.refs_11_), channel_id=1, source_target_pairs={{0,8},{8,16},{16,24},{24,32},{32,40},{40,48},{48,56},{56,0},{1,9},... | collective-permute-start | bytes 2359304 | tf_op jit(solution)/shard_map/ppermute | solution.py:323
  50.5 0.7 copy-start.5
  59.9 2.2 %copy-start = (bf16[384,3072]{1,0:T(8,128)(2,1)}, bf16[384,3072]{1,0:T(8,128)(2,1)S(1)}, u32[]{:S(2)}) copy-start(bf16[384,3072]{1,0:T(8,128)(2,1)S(1)} %collective-permute-done.11.refs_2_) | copy-start | bytes 7077892
  62.1 27.6 %collective-permute-start.14 = (bf16[192,3072]{1,0:T(8,128)(2,1)S(1)}, bf16[192,3072]{1,0:T(8,128)(2,1)S(1)}, u32[]{:S(2)}, u32[]{:S(2)}) collective-permute-start(bf16[192,3072]{1,0:T(8,128)(2,1)S(1)} %slice.15), channel_id=1, source_target_pairs={{0,6},{2,0},{4,2},{6,4},{1,7},{3,1},{5,3},{7,5},{8,14},{10,8},{12,... | collective-permute-start | bytes 3538952 | tf_op jit(solution)/shard_map/ppermute | solution.py:323
  63.3 26.5 %collective-permute-start.13 = (bf16[192,3072]{1,0:T(8,128)(2,1)S(1)}, bf16[192,3072]{1,0:T(8,128)(2,1)S(1)}, u32[]{:S(2)}, u32[]{:S(2)}) collective-permute-start(bf16[192,3072]{1,0:T(8,128)(2,1)S(1)} %slice.14), channel_id=1, source_target_pairs={{0,2},{2,4},{4,6},{6,0},{1,3},{3,5},{5,7},{7,1},{8,10},{10,12},{12... | collective-permute-start | bytes 3538952 | tf_op jit(solution)/shard_map/ppermute | solution.py:323
  69.9 12.4 %collective-permute-start.10 = (bf16[3,256,256]{2,1,0:T(8,128)(2,1)S(1)}, bf16[3,256,256]{2,1,0:T(8,128)(2,1)S(1)}, u32[]{:S(2)}, u32[]{:S(2)}) collective-permute-start(bf16[3,256,256]{2,1,0:T(8,128)(2,1)S(1)} %slice.13), channel_id=1, source_target_pairs={{0,56},{8,0},{16,8},{24,16},{32,24},{40,32},{48,40},{56,48},{1,57}... | collective-permute-start | bytes 1179656 | tf_op jit(solution)/shard_map/ppermute | solution.py:323
  70.2 12.0 %collective-permute-start.9 = (bf16[3,256,256]{2,1,0:T(8,128)(2,1)S(1)}, bf16[3,256,256]{2,1,0:T(8,128)(2,1)S(1)}, u32[]{:S(2)}, u32[]{:S(2)}) collective-permute-start(bf16[3,256,256]{2,1,0:T(8,128)(2,1)S(1)} %slice.12), channel_id=1, source_target_pairs={{0,8},{8,16},{16,24},{24,32},{32,40},{40,48},{48,56},{56,0},{1,9},... | collective-permute-start | bytes 1179656 | tf_op jit(solution)/shard_map/ppermute | solution.py:323
  82.3 0.8 copy-start.6
  82.3 0.9 copy-start.7
  89.7 25.3 %copy-start.1 = (bf16[192,3072]{1,0:T(8,128)(2,1)}, bf16[192,3072]{1,0:T(8,128)(2,1)S(1)}, u32[]{:S(2)}) copy-start(bf16[192,3072]{1,0:T(8,128)(2,1)S(1)} %collective-permute-done.14.refs_5_) | copy-start | bytes 3538948
  89.8 25.3 %copy-start.2 = (bf16[192,3072]{1,0:T(8,128)(2,1)}, bf16[192,3072]{1,0:T(8,128)(2,1)S(1)}, u32[]{:S(2)}) copy-start(bf16[192,3072]{1,0:T(8,128)(2,1)S(1)} %collective-permute-done.13.refs_4_) | copy-start | bytes 3538948
  122.8 7.7 %collective-permute-start.15 = (bf16[2,32,3072]{2,1,0:T(8,128)(2,1)}, bf16[2,32,3072]{2,1,0:T(8,128)(2,1)S(1)}, u32[]{:S(2)}, u32[]{:S(2)}) collective-permute-start(bf16[2,32,3072]{2,1,0:T(8,128)(2,1)} %get-tuple-element.37), channel_id=1, source_target_pairs={{0,1},{1,0},{2,3},{3,2},{4,5},{5,4},{6,7},{7,6},{8,9},{9,8},{10,11... | collective-permute-start | bytes 1179656 | tf_op jit(solution)/shard_map/ppermute | solution.py:382
  130.6 0.8 copy-start.8

commit v3 on v2

--- a/solution.py
+++ b/solution.py
@@ -234,12 +234,13 @@
 
 
 def project_kernel(place_ref, *refs):
-    sources, (main_ref, tangent_ref, other_ref, mixed, r_ref) = refs[:6], refs[6:11]
-    targets, sems = (r_ref,) + refs[11:16], refs[16]
-    copies = [
-        pltpu.make_async_copy(source, target, sems.at[i])
-        for i, (source, target) in enumerate(zip(sources, targets))
-    ]
+    sources, (main_ref, tangent_ref, other_ref, mixed, r_ref, w_ref, sems) = refs[:6], refs[6:]
+    copies = [pltpu.make_async_copy(sources[0], r_ref, sems.at[0])]
+    start = 0
+    for i, source in enumerate(sources[1:], 1):
+        rows = pl.ds(start, source.shape[0])
+        copies.append(pltpu.make_async_copy(source, w_ref.at[rows], sems.at[i]))
+        start += source.shape[0]
     for copy in copies:
         copy.start()
     y, c = place_ref[2], place_ref[3]
@@ -275,11 +276,7 @@
     mine = c == 0
     for column in range(0, DM, COLS):
         cols = pl.ds(column, COLS)
-        total, start = 0.0, 0
-        for ref in targets[1:]:
-            rows = pl.ds(start, ref.shape[0])
-            start += ref.shape[0]
-            total = total + jnp.dot(mixed[:, rows], ref[:, cols], preferred_element_type=jnp.float32)
+        total = jnp.dot(mixed[...], w_ref[:, cols], preferred_element_type=jnp.float32)
         for which, own_ref in enumerate((main_ref, tangent_ref)):
             low = total[which * SLOT_TOK : which * SLOT_TOK + half]
             high = total[which * SLOT_TOK + half : (which + 1) * SLOT_TOK]
@@ -298,24 +295,13 @@
         out_shape=(own_shape, own_shape, jax.ShapeDtypeStruct((2, half, DM), jnp.bfloat16)),
         scratch_shapes=[
             pltpu.VMEM((2 * SLOT_TOK, NY * HEADS_HERE * HEAD_DIM), jnp.bfloat16),
-            *[pltpu.VMEM(operand.shape, operand.dtype) for operand in operands],
+            pltpu.VMEM(received.shape, received.dtype),
+            pltpu.VMEM((NY * HEADS_HERE * HEAD_DIM, DM), jnp.bfloat16),
             pltpu.SemaphoreType.DMA((len(operands),)),
         ],
         compiler_params=params(),
         name="project",
     )(place, *operands)
-
-
-def finish_kernel(main_ref, tangent_ref, arrived_ref, out_ref, tout_ref):
-    out_ref[...] = (main_ref[...] + arrived_ref[0].astype(jnp.float32)).astype(jnp.bfloat16)
-    tout_ref[...] = (tangent_ref[...] + arrived_ref[1].astype(jnp.float32)).astype(jnp.bfloat16)
-
-
-def finish(main, tangent, arrived):
-    shape = jax.ShapeDtypeStruct(main.shape, jnp.bfloat16)
-    return pl.pallas_call(
-        finish_kernel, out_shape=(shape, shape), compiler_params=params(), name="finish"
-    )(main, tangent, arrived)
 
 
 def shifted(block, axis, distance):
@@ -380,7 +366,10 @@
     weights = (out_weight, weight_left, weight_right, far_a, far_b)
     main, tangent, other = project(place, received, weights)
     arrived = lax.ppermute(other, "c", [(0, 1), (1, 0)])
-    return finish(main, tangent, arrived)
+    return tuple(
+        (own + part.astype(jnp.float32)).astype(jnp.bfloat16)
+        for own, part in ((main, arrived[0]), (tangent, arrived[1]))
+    )
 
 
 def solution(mesh):

time: 134 us -> 133 us (level)
  Pallas kernels: 38.3 us -> 35.9 us
  other arithmetic: 0.6 us -> 2.52 us
    pallas_call x1 -> x0, Pallas kernels: 2.01 us -> none  [finish(): pl.pallas_call(finish_kernel, out_shape=(shape, shape), compiler_params=p...]
    convert_element_type x0 -> x1, other arithmetic: none -> 1.92 us  [body(): (own + part.astype(jnp.float32)).astype(jnp.bfloat16)]
  transfers between devices with their start and end apart: 16 -> 16, of which waited for: 7 -> 7; matrix products, arithmetic and copies ran while one was open for 5% -> 5% of each run, Pallas kernels for 21% -> 22%
where the time goes in v3:
time: 133 us; the launch traced here: 132 us
  Pallas kernels  35.9 us (27%)
  starting transfers between devices  30.4 us (23%)
  waiting for transfers between devices  29.8 us (22%)
  blocking collectives  25.3 us (19%)
  local copies, waits for them, and re-layouts  7.47 us (6%)
  other arithmetic  2.52 us (2%)
    ppermute x15, waiting for transfers between devices, shifted(): lax.ppermute(block, axis, [(i, (i + distance) % size) for i in range(size)])  28.3 us
    pallas_call x3, Pallas kernels, attend(): pl.pallas_call(functools.partial(attend_kernel, key_blocks, is_first, is_...  26 us
    all_to_all x1, blocking collectives, body(): lax.all_to_all(packed.reshape(NX * NY, SLOT_TOK, PACKED), ('x', 'y'), 0,...  25.3 us
    ppermute x15, starting transfers between devices, shifted(): lax.ppermute(block, axis, [(i, (i + distance) % size) for i in range(size)])  24.1 us
    pallas_call x1, Pallas kernels, project(): pl.pallas_call(project_kernel, in_specs=[pl.BlockSpec(memory_space=pltpu....  7.35 us
    ppermute x1, starting transfers between devices, body(): arrived = lax.ppermute(other, 'c', [(0, 1), (1, 0)])  6.2 us
  transfers between devices with their start and end apart: 16, of which 7 were waited for; matrix products, arithmetic and copies ran while one was open for 5% of the time, Pallas kernels for 22%

profile of v3, /device:TPU:1, one launch (start us, length us, event | category | flops | bytes accessed | tf_op | source)
XLA Modules:
  0.0 132.1 jit_solution(10395716682642352102)
XLA Ops:
  0.6 2.2 %collective-permute-start.11 = (bf16[384,3072]{1,0:T(8,128)(2,1)}, bf16[384,3072]{1,0:T(8,128)(2,1)S(1)}, u32[]{:S(2)}, u32[]{:S(2)}) collective-permute-start(bf16[384,3072]{1,0:T(8,128)(2,1)} %refs_1_.7), channel_id=1, source_target_pairs={{0,2},{2,4},{4,6},{6,0},{1,3},{3,5},{5,7},{7,1},{8,10},{10,12},{12... | collective-permute-start | bytes 7077896 | tf_op jit(solution)/shard_map/ppermute | solution.py:309
  2.8 1.5 %collective-permute-start.12 = (bf16[384,3072]{1,0:T(8,128)(2,1)}, bf16[384,3072]{1,0:T(8,128)(2,1)}, u32[]{:S(2)}, u32[]{:S(2)}) collective-permute-start(bf16[384,3072]{1,0:T(8,128)(2,1)} %refs_1_.7), channel_id=1, source_target_pairs={{0,6},{2,0},{4,2},{6,4},{1,7},{3,1},{5,3},{7,5},{8,14},{10,8},{12,... | collective-permute-start | bytes 7077896 | tf_op jit(solution)/shard_map/ppermute | solution.py:309
  4.4 2.5 %prepare.1 = (bf16[256,768]{1,0:T(8,128)(2,1)}, bf16[6,256,256]{2,1,0:T(8,128)(2,1)}) custom-call(bf16[256,384]{1,0:T(8,128)(2,1)} %q_ref.1, bf16[256,384]{1,0:T(8,128)(2,1)} %qt_ref.1, bf16[256,384]{1,0:T(8,128)(2,1)} %k_ref.1, bf16[256,384]{1,0:T(8,128)(2,1)} %kt_ref.1, bf16[256,384]{1,0:T(8,128)(2,1)} %v_ref.1, bf16[256,384]{1,0:T(8,128)(2,1)} %vt_ref.1), custom_call_target="tpu_custom_call" | custom-call | tf_op jit(solution)/shard_map/prepare/pallas_call | solution.py:50
  6.9 5.6 %collective-permute-start.6 = (bf16[6,256,256]{2,1,0:T(8,128)(2,1)}, bf16[6,256,256]{2,1,0:T(8,128)(2,1)}, u32[]{:S(2)}, u32[]{:S(2)}) collective-permute-start(bf16[6,256,256]{2,1,0:T(8,128)(2,1)} %get-tuple-element.23.refs_7_.refs_10_), channel_id=1, source_target_pairs={{0,56},{8,0},{16,8},{24,16},{32,24},{40,32},{48,40},{56,48},{1,57}... | collective-permute-start | bytes 2359304 | tf_op jit(solution)/shard_map/ppermute | solution.py:309
  12.5 0.0 collective-permute-start.3
  12.5 2.5 %collective-permute-start = (bf16[256,768]{1,0:T(8,128)(2,1)}, bf16[256,768]{1,0:T(8,128)(2,1)S(1)}, u32[]{:S(2)}, u32[]{:S(2)}) collective-permute-start(bf16[256,768]{1,0:T(8,128)(2,1)} %get-tuple-element.22.refs_3_), channel_id=1, source_target_pairs={{0,192},{64,0},{128,64},{192,128},{1,193},{65,1},{129,65},{193,129... | collective-permute-start | bytes 1179656 | tf_op jit(solution)/shard_map/ppermute | solution.py:309
  14.9 7.4 %collective-permute-done.refs_4_ = bf16[256,768]{1,0:T(8,128)(2,1)S(1)} collective-permute-done((bf16[256,768]{1,0:T(8,128)(2,1)}, bf16[256,768]{1,0:T(8,128)(2,1)S(1)}, u32[]{:S(2)}, u32[]{:S(2)}) %collective-permute-start) | collective-permute-done | bytes 393248 | tf_op jit(solution)/shard_map/ppermute | solution.py:309
  22.3 0.0 copy-start.3
  22.3 0.9 collective-permute-start.1
  23.2 5.3 %collective-permute-done.6.refs_9_.refs_12_ = bf16[6,256,256]{2,1,0:T(8,128)(2,1)} collective-permute-done((bf16[6,256,256]{2,1,0:T(8,128)(2,1)}, bf16[6,256,256]{2,1,0:T(8,128)(2,1)}, u32[]{:S(2)}, u32[]{:S(2)}) %collective-permute-start.6) | collective-permute-done | bytes 786464 | tf_op jit(solution)/shard_map/ppermute | solution.py:309
  28.5 3.4 %collective-permute-start.7 = (bf16[6,256,256]{2,1,0:T(8,128)(2,1)}, bf16[6,256,256]{2,1,0:T(8,128)(2,1)}, u32[]{:S(2)}, u32[]{:S(2)}) collective-permute-start(bf16[6,256,256]{2,1,0:T(8,128)(2,1)} %collective-permute-done.6.refs_9_.refs_12_), channel_id=1, source_target_pairs={{0,56},{8,0},{16,8},{24,16},{32,24},{40,32},{48,40},{56,48},{1,57}... | collective-permute-start | bytes 2359304 | tf_op jit(solution)/shard_map/ppermute | solution.py:309
  31.9 0.0 collective-permute-done.3.refs_8_.refs_11_
  31.9 0.0 collective-permute-start.4
  31.9 1.3 %collective-permute-done.1.refs_6_ = bf16[256,768]{1,0:T(8,128)(2,1)S(1)} collective-permute-done((bf16[256,768]{1,0:T(8,128)(2,1)}, bf16[256,768]{1,0:T(8,128)(2,1)S(1)}, u32[]{:S(2)}, u32[]{:S(2)}) %collective-permute-start.1) | collective-permute-done | bytes 393248 | tf_op jit(solution)/shard_map/ppermute | solution.py:309
  33.3 0.0 copy-start.4
  33.3 1.5 %collective-permute-start.2 = (bf16[256,768]{1,0:T(8,128)(2,1)}, bf16[256,768]{1,0:T(8,128)(2,1)S(1)}, u32[]{:S(2)}, u32[]{:S(2)}) collective-permute-start(bf16[256,768]{1,0:T(8,128)(2,1)} %get-tuple-element.22.refs_3_), channel_id=1, source_target_pairs={{0,128},{64,192},{128,0},{192,64},{1,129},{65,193},{129,1},{193,65... | collective-permute-start | bytes 1179656 | tf_op jit(solution)/shard_map/ppermute | solution.py:309
  34.8 1.6 %reshape.14.refs_0_ = s32[12288]{0:T(1024)} reshape(s32[3,64,64]{2,1,0:T(8,128)} %param.15) | data formatting | bytes 98304 | tf_op jit(solution)/shard_map/reshape | solution.py:328
  36.4 0.6 pad_add_fusion.refs_2_.place_ref
  37.0 10.1 %collective-permute-done.7.refs_8_.refs_12_ = bf16[6,256,256]{2,1,0:T(8,128)(2,1)} collective-permute-done((bf16[6,256,256]{2,1,0:T(8,128)(2,1)}, bf16[6,256,256]{2,1,0:T(8,128)(2,1)}, u32[]{:S(2)}, u32[]{:S(2)}) %collective-permute-start.7) | collective-permute-done | bytes 786464 | tf_op jit(solution)/shard_map/ppermute | solution.py:309
  47.1 3.4 %collective-permute-start.8 = (bf16[6,256,256]{2,1,0:T(8,128)(2,1)}, bf16[6,256,256]{2,1,0:T(8,128)(2,1)}, u32[]{:S(2)}, u32[]{:S(2)}) collective-permute-start(bf16[6,256,256]{2,1,0:T(8,128)(2,1)} %collective-permute-done.7.refs_8_.refs_12_), channel_id=1, source_target_pairs={{0,56},{8,0},{16,8},{24,16},{32,24},{40,32},{48,40},{56,48},{1,57}... | collective-permute-start | bytes 2359304 | tf_op jit(solution)/shard_map/ppermute | solution.py:309
  50.5 0.0 collective-permute-done.4.refs_7_.refs_11_
  50.5 0.0 collective-permute-start.5
  50.5 0.0 collective-permute-done.2.refs_5_
  50.5 0.0 copy-done.3
  50.5 0.0 copy-done.4
  50.5 0.0 copy-start.5
  50.5 0.7 copy-done.5
  51.3 8.6 %attend.2 = (f32[3,256,1024]{2,1,0:T(8,128)}, f32[3,8,1024]{2,1,0:T(8,128)}) custom-call(s32[12288]{0:T(1024)} %reshape.14.refs_0_, s32[32]{0:T(128)} %refs_1_.6, s32[4]{0:T(128)} %pad_add_fusion.refs_2_.place_ref, bf16[256,768]{1,0:T(8,128)(2,1)} %get-tuple-element.22.refs_3_, bf16[256,768]{1,0:T(8,128)(2,1)} %copy-done.3, bf16[256,768]{1,0:T(8,128)(2,1)} %copy-done.5, ...), custom_call_target="tpu_custom_call" | custom-call | flops 3623878656 | bytes 8388608 | tf_op jit(solution)/shard_map/attend/pallas_call | solution.py:216
  59.9 0.0 collective-permute-done.11.refs_2_
  59.9 0.0 copy-start
  59.9 0.0 collective-permute-done.12.refs_3_
  59.9 0.1 slice.20
  60.0 2.1 %slice.21 = bf16[192,3072]{1,0:T(8,128)(2,1)S(1)} slice(bf16[384,3072]{1,0:T(8,128)(2,1)} %collective-permute-done.12.refs_3_), slice={[192:384], [0:3072]} | slice | bytes 2359296 | tf_op jit(solution)/shard_map/slice | solution.py:353
  62.1 0.0 copy-done
  62.1 1.1 collective-permute-start.14
  63.3 0.4 collective-permute-start.13
  63.7 1.0 collective-permute-done.8.refs_10_.refs_14_
  64.7 3.1 %collective-permute-done.5.refs_9_.refs_13_ = bf16[6,256,256]{2,1,0:T(8,128)(2,1)} collective-permute-done((bf16[6,256,256]{2,1,0:T(8,128)(2,1)}, bf16[6,256,256]{2,1,0:T(8,128)(2,1)}, u32[]{:S(2)}, u32[]{:S(2)}) %collective-permute-start.5) | collective-permute-done | bytes 786464 | tf_op jit(solution)/shard_map/ppermute | solution.py:309
  67.8 1.0 slice.18
  68.9 1.0 slice.19
  69.9 0.4 collective-permute-start.10
  70.2 1.2 collective-permute-start.9
  71.4 10.8 %attend.3 = (f32[3,256,1024]{2,1,0:T(8,128)}, f32[3,8,1024]{2,1,0:T(8,128)}) custom-call(s32[12288]{0:T(1024)} %reshape.14.refs_0_, s32[32]{0:T(128)} %refs_1_.6, s32[4]{0:T(128)} %pad_add_fusion.refs_2_.place_ref, bf16[256,768]{1,0:T(8,128)(2,1)} %get-tuple-element.22.refs_3_, bf16[256,768]{1,0:T(8,128)(2,1)} %copy-done.3, bf16[256,768]{1,0:T(8,128)(2,1)} %copy-done.5, ...), custom_call_target="tpu_custom_call" | custom-call | flops 4831838208 | bytes 8388608 | tf_op jit(solution)/shard_map/attend/pallas_call | solution.py:216
  82.2 0.0 collective-permute-done.10.refs_8_
  82.3 0.0 copy-start.6
  82.3 0.0 collective-permute-done.9.refs_7_
  82.3 0.0 copy-start.7
  82.3 0.7 copy-done.6
  83.0 0.2 copy-done.7
  83.2 6.6 %attend_last.1 = bf16[4,256,896]{2,1,0:T(8,128)(2,1)} custom-call(s32[12288]{0:T(1024)} %reshape.14.refs_0_, s32[32]{0:T(128)} %refs_1_.6, s32[4]{0:T(128)} %pad_add_fusion.refs_2_.place_ref, bf16[256,768]{1,0:T(8,128)(2,1)} %get-tuple-element.22.refs_3_, bf16[256,768]{1,0:T(8,128)(2,1)} %copy-done.3, bf16[256,768]{1,0:T(8,128)(2,1)} %copy-done.5, ...), custom_call_target="tpu_custom_call" | custom-call | flops 1207959552 | bytes 8388608 | tf_op jit(solution)/shard_map/attend_last/pallas_call | solution.py:216
  89.7 0.0 collective-permute-done.14.refs_5_
  89.7 0.0 copy-start.1
  89.8 0.0 collective-permute-done.13.refs_4_
  89.8 0.0 copy-start.2
  89.8 25.3 %all_to_all.5.refs_0_ = bf16[16,64,896]{2,1,0:T(8,128)(2,1)} all-to-all(bf16[16,64,896]{2,1,0:T(8,128)(2,1)} %bitcast.15), channel_id=1, replica_groups=mesh['x'=4,'z'=8,'y'=4,'c'=2] {'x','y'}, dimensions={0} | all-to-all | bytes 3670016 | tf_op jit(solution)/shard_map/all_to_all | solution.py:363
  115.0 0.0 copy-done.1
  115.0 0.0 copy-done.2
  115.0 7.4 %project.1 = (f32[32,3072]{1,0:T(8,128)}, f32[32,3072]{1,0:T(8,128)}, bf16[2,32,3072]{2,1,0:T(8,128)(2,1)}) custom-call(s32[4]{0:T(128)} %pad_add_fusion.refs_2_.place_ref, bf16[16,64,896]{2,1,0:T(8,128)(2,1)} %all_to_all.5.refs_0_, bf16[384,3072]{1,0:T(8,128)(2,1)} %refs_1_.7, bf16[384,3072]{1,0:T(8,128)(2,1)} %copy-done, ...), custom_call_target="tpu_custom_call" | custom-call | tf_op jit(solution)/shard_map/project/pallas_call | solution.py:292
  122.4 6.2 %collective-permute-start.15 = (bf16[2,32,3072]{2,1,0:T(8,128)(2,1)}, bf16[2,32,3072]{2,1,0:T(8,128)(2,1)S(1)}, u32[]{:S(2)}, u32[]{:S(2)}) collective-permute-start(bf16[2,32,3072]{2,1,0:T(8,128)(2,1)} %get-tuple-element.36), channel_id=1, source_target_pairs={{0,1},{1,0},{2,3},{3,2},{4,5},{5,4},{6,7},{7,6},{8,9},{9,8},{10,11... | collective-permute-start | bytes 1179656 | tf_op jit(solution)/shard_map/ppermute | solution.py:368
  128.6 1.6 %collective-permute-done.15 = bf16[2,32,3072]{2,1,0:T(8,128)(2,1)S(1)} collective-permute-done((bf16[2,32,3072]{2,1,0:T(8,128)(2,1)}, bf16[2,32,3072]{2,1,0:T(8,128)(2,1)S(1)}, u32[]{:S(2)}, u32[]{:S(2)}) %collective-permute-start.15) | collective-permute-done | bytes 393248 | tf_op jit(solution)/shard_map/ppermute | solution.py:368
  130.2 1.9 %fusion = (bf16[32,3072]{1,0:T(8,128)(2,1)}, bf16[32,3072]{1,0:T(8,128)(2,1)}) fusion(f32[32,3072]{1,0:T(8,128)} %get-tuple-element.37, bf16[2,32,3072]{2,1,0:T(8,128)(2,1)S(1)} %collective-permute-done.15, f32[32,3072]{1,0:T(8,128)} %get-tuple-element.35), kind=kLoop, calls=%fused_computation.1 | loop fusion | flops 589824 | bytes 1572864 | tf_op jit(solution)/shard_map/convert_element_type | solution.py:370
Async XLA Ops:
  0.6 59.3 %collective-permute-start.11 = (bf16[384,3072]{1,0:T(8,128)(2,1)}, bf16[384,3072]{1,0:T(8,128)(2,1)S(1)}, u32[]{:S(2)}, u32[]{:S(2)}) collective-permute-start(bf16[384,3072]{1,0:T(8,128)(2,1)} %refs_1_.7), channel_id=1, source_target_pairs={{0,2},{2,4},{4,6},{6,0},{1,3},{3,5},{5,7},{7,1},{8,10},{10,12},{12... | collective-permute-start | bytes 7077896 | tf_op jit(solution)/shard_map/ppermute | solution.py:309
  2.8 57.1 %collective-permute-start.12 = (bf16[384,3072]{1,0:T(8,128)(2,1)}, bf16[384,3072]{1,0:T(8,128)(2,1)}, u32[]{:S(2)}, u32[]{:S(2)}) collective-permute-start(bf16[384,3072]{1,0:T(8,128)(2,1)} %refs_1_.7), channel_id=1, source_target_pairs={{0,6},{2,0},{4,2},{6,4},{1,7},{3,1},{5,3},{7,5},{8,14},{10,8},{12,... | collective-permute-start | bytes 7077896 | tf_op jit(solution)/shard_map/ppermute | solution.py:309
  6.9 21.6 %collective-permute-start.6 = (bf16[6,256,256]{2,1,0:T(8,128)(2,1)}, bf16[6,256,256]{2,1,0:T(8,128)(2,1)}, u32[]{:S(2)}, u32[]{:S(2)}) collective-permute-start(bf16[6,256,256]{2,1,0:T(8,128)(2,1)} %get-tuple-element.23.refs_7_.refs_10_), channel_id=1, source_target_pairs={{0,56},{8,0},{16,8},{24,16},{32,24},{40,32},{48,40},{56,48},{1,57}... | collective-permute-start | bytes 2359304 | tf_op jit(solution)/shard_map/ppermute | solution.py:309
  12.5 19.5 %collective-permute-start.3 = (bf16[6,256,256]{2,1,0:T(8,128)(2,1)}, bf16[6,256,256]{2,1,0:T(8,128)(2,1)}, u32[]{:S(2)}, u32[]{:S(2)}) collective-permute-start(bf16[6,256,256]{2,1,0:T(8,128)(2,1)} %get-tuple-element.23.refs_7_.refs_10_), channel_id=1, source_target_pairs={{0,8},{8,16},{16,24},{24,32},{32,40},{40,48},{48,56},{56,0},{1,9},... | collective-permute-start | bytes 2359304 | tf_op jit(solution)/shard_map/ppermute | solution.py:309
  12.5 9.8 %collective-permute-start = (bf16[256,768]{1,0:T(8,128)(2,1)}, bf16[256,768]{1,0:T(8,128)(2,1)S(1)}, u32[]{:S(2)}, u32[]{:S(2)}) collective-permute-start(bf16[256,768]{1,0:T(8,128)(2,1)} %get-tuple-element.22.refs_3_), channel_id=1, source_target_pairs={{0,192},{64,0},{128,64},{192,128},{1,193},{65,1},{129,65},{193,129... | collective-permute-start | bytes 1179656 | tf_op jit(solution)/shard_map/ppermute | solution.py:309
  22.3 28.2 %copy-start.3 = (bf16[256,768]{1,0:T(8,128)(2,1)}, bf16[256,768]{1,0:T(8,128)(2,1)S(1)}, u32[]{:S(2)}) copy-start(bf16[256,768]{1,0:T(8,128)(2,1)S(1)} %collective-permute-done.refs_4_) | copy-start | bytes 1179652
  22.3 11.0 %collective-permute-start.1 = (bf16[256,768]{1,0:T(8,128)(2,1)}, bf16[256,768]{1,0:T(8,128)(2,1)S(1)}, u32[]{:S(2)}, u32[]{:S(2)}) collective-permute-start(bf16[256,768]{1,0:T(8,128)(2,1)} %get-tuple-element.22.refs_3_), channel_id=1, source_target_pairs={{0,64},{64,128},{128,192},{192,0},{1,65},{65,129},{129,193},{193,1... | collective-permute-start | bytes 1179656 | tf_op jit(solution)/shard_map/ppermute | solution.py:309
  28.5 18.6 %collective-permute-start.7 = (bf16[6,256,256]{2,1,0:T(8,128)(2,1)}, bf16[6,256,256]{2,1,0:T(8,128)(2,1)}, u32[]{:S(2)}, u32[]{:S(2)}) collective-permute-start(bf16[6,256,256]{2,1,0:T(8,128)(2,1)} %collective-permute-done.6.refs_9_.refs_12_), channel_id=1, source_target_pairs={{0,56},{8,0},{16,8},{24,16},{32,24},{40,32},{48,40},{56,48},{1,57}... | collective-permute-start | bytes 2359304 | tf_op jit(solution)/shard_map/ppermute | solution.py:309
  31.9 18.6 %collective-permute-start.4 = (bf16[6,256,256]{2,1,0:T(8,128)(2,1)}, bf16[6,256,256]{2,1,0:T(8,128)(2,1)}, u32[]{:S(2)}, u32[]{:S(2)}) collective-permute-start(bf16[6,256,256]{2,1,0:T(8,128)(2,1)} %collective-permute-done.3.refs_8_.refs_11_), channel_id=1, source_target_pairs={{0,8},{8,16},{16,24},{24,32},{32,40},{40,48},{48,56},{56,0},{1,9},... | collective-permute-start | bytes 2359304 | tf_op jit(solution)/shard_map/ppermute | solution.py:309
  33.3 17.2 %copy-start.4 = (bf16[256,768]{1,0:T(8,128)(2,1)}, bf16[256,768]{1,0:T(8,128)(2,1)S(1)}, u32[]{:S(2)}) copy-start(bf16[256,768]{1,0:T(8,128)(2,1)S(1)} %collective-permute-done.1.refs_6_) | copy-start | bytes 1179652
  33.3 17.2 %collective-permute-start.2 = (bf16[256,768]{1,0:T(8,128)(2,1)}, bf16[256,768]{1,0:T(8,128)(2,1)S(1)}, u32[]{:S(2)}, u32[]{:S(2)}) collective-permute-start(bf16[256,768]{1,0:T(8,128)(2,1)} %get-tuple-element.22.refs_3_), channel_id=1, source_target_pairs={{0,128},{64,192},{128,0},{192,64},{1,129},{65,193},{129,1},{193,65... | collective-permute-start | bytes 1179656 | tf_op jit(solution)/shard_map/ppermute | solution.py:309
  47.1 17.6 %collective-permute-start.8 = (bf16[6,256,256]{2,1,0:T(8,128)(2,1)}, bf16[6,256,256]{2,1,0:T(8,128)(2,1)}, u32[]{:S(2)}, u32[]{:S(2)}) collective-permute-start(bf16[6,256,256]{2,1,0:T(8,128)(2,1)} %collective-permute-done.7.refs_8_.refs_12_), channel_id=1, source_target_pairs={{0,56},{8,0},{16,8},{24,16},{32,24},{40,32},{48,40},{56,48},{1,57}... | collective-permute-start | bytes 2359304 | tf_op jit(solution)/shard_map/ppermute | solution.py:309
  50.5 17.4 %collective-permute-start.5 = (bf16[6,256,256]{2,1,0:T(8,128)(2,1)}, bf16[6,256,256]{2,1,0:T(8,128)(2,1)}, u32[]{:S(2)}, u32[]{:S(2)}) collective-permute-start(bf16[6,256,256]{2,1,0:T(8,128)(2,1)} %collective-permute-done.4.refs_7_.refs_11_), channel_id=1, source_target_pairs={{0,8},{8,16},{16,24},{24,32},{32,40},{40,48},{48,56},{56,0},{1,9},... | collective-permute-start | bytes 2359304 | tf_op jit(solution)/shard_map/ppermute | solution.py:309
  50.5 0.7 copy-start.5
  59.9 2.2 %copy-start = (bf16[384,3072]{1,0:T(8,128)(2,1)}, bf16[384,3072]{1,0:T(8,128)(2,1)S(1)}, u32[]{:S(2)}) copy-start(bf16[384,3072]{1,0:T(8,128)(2,1)S(1)} %collective-permute-done.11.refs_2_) | copy-start | bytes 7077892
  62.1 27.6 %collective-permute-start.14 = (bf16[192,3072]{1,0:T(8,128)(2,1)S(1)}, bf16[192,3072]{1,0:T(8,128)(2,1)S(1)}, u32[]{:S(2)}, u32[]{:S(2)}) collective-permute-start(bf16[192,3072]{1,0:T(8,128)(2,1)S(1)} %slice.21), channel_id=1, source_target_pairs={{0,6},{2,0},{4,2},{6,4},{1,7},{3,1},{5,3},{7,5},{8,14},{10,8},{12,... | collective-permute-start | bytes 3538952 | tf_op jit(solution)/shard_map/ppermute | solution.py:309
  63.3 26.5 %collective-permute-start.13 = (bf16[192,3072]{1,0:T(8,128)(2,1)S(1)}, bf16[192,3072]{1,0:T(8,128)(2,1)S(1)}, u32[]{:S(2)}, u32[]{:S(2)}) collective-permute-start(bf16[192,3072]{1,0:T(8,128)(2,1)S(1)} %slice.20), channel_id=1, source_target_pairs={{0,2},{2,4},{4,6},{6,0},{1,3},{3,5},{5,7},{7,1},{8,10},{10,12},{12... | collective-permute-start | bytes 3538952 | tf_op jit(solution)/shard_map/ppermute | solution.py:309
  69.9 12.4 %collective-permute-start.10 = (bf16[3,256,256]{2,1,0:T(8,128)(2,1)S(1)}, bf16[3,256,256]{2,1,0:T(8,128)(2,1)S(1)}, u32[]{:S(2)}, u32[]{:S(2)}) collective-permute-start(bf16[3,256,256]{2,1,0:T(8,128)(2,1)S(1)} %slice.19), channel_id=1, source_target_pairs={{0,56},{8,0},{16,8},{24,16},{32,24},{40,32},{48,40},{56,48},{1,57}... | collective-permute-start | bytes 1179656 | tf_op jit(solution)/shard_map/ppermute | solution.py:309
  70.2 12.0 %collective-permute-start.9 = (bf16[3,256,256]{2,1,0:T(8,128)(2,1)S(1)}, bf16[3,256,256]{2,1,0:T(8,128)(2,1)S(1)}, u32[]{:S(2)}, u32[]{:S(2)}) collective-permute-start(bf16[3,256,256]{2,1,0:T(8,128)(2,1)S(1)} %slice.18), channel_id=1, source_target_pairs={{0,8},{8,16},{16,24},{24,32},{32,40},{40,48},{48,56},{56,0},{1,9},... | collective-permute-start | bytes 1179656 | tf_op jit(solution)/shard_map/ppermute | solution.py:309
  82.3 0.8 copy-start.6
  82.3 0.9 copy-start.7
  89.7 25.3 %copy-start.1 = (bf16[192,3072]{1,0:T(8,128)(2,1)}, bf16[192,3072]{1,0:T(8,128)(2,1)S(1)}, u32[]{:S(2)}) copy-start(bf16[192,3072]{1,0:T(8,128)(2,1)S(1)} %collective-permute-done.14.refs_5_) | copy-start | bytes 3538948
  89.8 25.3 %copy-start.2 = (bf16[192,3072]{1,0:T(8,128)(2,1)}, bf16[192,3072]{1,0:T(8,128)(2,1)S(1)}, u32[]{:S(2)}) copy-start(bf16[192,3072]{1,0:T(8,128)(2,1)S(1)} %collective-permute-done.13.refs_4_) | copy-start | bytes 3538948
  122.4 7.8 %collective-permute-start.15 = (bf16[2,32,3072]{2,1,0:T(8,128)(2,1)}, bf16[2,32,3072]{2,1,0:T(8,128)(2,1)S(1)}, u32[]{:S(2)}, u32[]{:S(2)}) collective-permute-start(bf16[2,32,3072]{2,1,0:T(8,128)(2,1)} %get-tuple-element.36), channel_id=1, source_target_pairs={{0,1},{1,0},{2,3},{3,2},{4,5},{5,4},{6,7},{7,6},{8,9},{9,8},{10,11... | collective-permute-start | bytes 1179656 | tf_op jit(solution)/shard_map/ppermute | solution.py:368

commit v4 on v3

--- a/solution.py
+++ b/solution.py
@@ -231,20 +231,28 @@
 
 
 COLS = 512
+SPANS = 2
 
 
 def project_kernel(place_ref, *refs):
     sources, (main_ref, tangent_ref, other_ref, mixed, r_ref, w_ref, sems) = refs[:6], refs[6:]
-    copies = [pltpu.make_async_copy(sources[0], r_ref, sems.at[0])]
-    start = 0
-    for i, source in enumerate(sources[1:], 1):
-        rows = pl.ds(start, source.shape[0])
-        copies.append(pltpu.make_async_copy(source, w_ref.at[rows], sems.at[i]))
-        start += source.shape[0]
-    for copy in copies:
-        copy.start()
+    first = pltpu.make_async_copy(sources[0], r_ref, sems.at[0, 0])
+    first.start()
+    spans = []
+    for at in range(SPANS):
+        cols = pl.ds(at * (DM // SPANS), DM // SPANS)
+        start, copies = 0, []
+        for i, source in enumerate(sources[1:], 1):
+            rows = pl.ds(start, source.shape[0])
+            copies.append(
+                pltpu.make_async_copy(source.at[:, cols], w_ref.at[rows, cols], sems.at[i, at])
+            )
+            start += source.shape[0]
+        for copy in copies:
+            copy.start()
+        spans.append(copies)
     y, c = place_ref[2], place_ref[3]
-    copies[0].wait()
+    first.wait()
     for rel, shift in enumerate((0, NY - 1, 1, 2)):
         group = (y + shift) & (NY - 1)
         sides = []
@@ -270,11 +278,12 @@
             mixed[0:SLOT_TOK, cols] = attn.astype(jnp.bfloat16)
             mixed[SLOT_TOK : 2 * SLOT_TOK, cols] = tangent.astype(jnp.bfloat16)
 
-    for copy in copies[1:]:
-        copy.wait()
     half = SLOT_TOK // NC
     mine = c == 0
     for column in range(0, DM, COLS):
+        if column % (DM // SPANS) == 0:
+            for copy in spans[column // (DM // SPANS)]:
+                copy.wait()
         cols = pl.ds(column, COLS)
         total = jnp.dot(mixed[...], w_ref[:, cols], preferred_element_type=jnp.float32)
         for which, own_ref in enumerate((main_ref, tangent_ref)):
@@ -297,7 +306,7 @@
             pltpu.VMEM((2 * SLOT_TOK, NY * HEADS_HERE * HEAD_DIM), jnp.bfloat16),
             pltpu.VMEM(received.shape, received.dtype),
             pltpu.VMEM((NY * HEADS_HERE * HEAD_DIM, DM), jnp.bfloat16),
-            pltpu.SemaphoreType.DMA((len(operands),)),
+            pltpu.SemaphoreType.DMA((len(operands), SPANS)),
         ],
         compiler_params=params(),
         name="project",

time: 133 us -> 132 us (level)
  no operation moved by 1% of the time
where the time goes in v4:
time: 132 us
  Pallas kernels  35.3 us (27%)
  starting transfers between devices  30.4 us (23%)
  waiting for transfers between devices  29.8 us (23%)
  blocking collectives  25.3 us (19%)
  local copies, waits for them, and re-layouts  7.47 us (6%)
  other arithmetic  2.52 us (2%)
    ppermute x15, waiting for transfers between devices, shifted(): lax.ppermute(block, axis, [(i, (i + distance) % size) for i in range(size)])  28.3 us
    pallas_call x3, Pallas kernels, attend(): pl.pallas_call(functools.partial(attend_kernel, key_blocks, is_first, is_...  26 us
    all_to_all x1, blocking collectives, body(): lax.all_to_all(packed.reshape(NX * NY, SLOT_TOK, PACKED), ('x', 'y'), 0,...  25.3 us
    ppermute x15, starting transfers between devices, shifted(): lax.ppermute(block, axis, [(i, (i + distance) % size) for i in range(size)])  24.1 us
    pallas_call x1, Pallas kernels, project(): pl.pallas_call(project_kernel, in_specs=[pl.BlockSpec(memory_space=pltpu....  6.8 us
    ppermute x1, starting transfers between devices, body(): arrived = lax.ppermute(other, 'c', [(0, 1), (1, 0)])  6.21 us
  transfers between devices with their start and end apart: 16, of which 7 were waited for; matrix products, arithmetic and copies ran while one was open for 5% of the time, Pallas kernels for 22%

profile of v4, /device:TPU:1, one launch (start us, length us, event | category | flops | bytes accessed | tf_op | source)
XLA Modules:
  0.0 131.5 jit_solution(15001441315350606465)
XLA Ops:
  0.6 2.2 %collective-permute-start.11 = (bf16[384,3072]{1,0:T(8,128)(2,1)}, bf16[384,3072]{1,0:T(8,128)(2,1)S(1)}, u32[]{:S(2)}, u32[]{:S(2)}) collective-permute-start(bf16[384,3072]{1,0:T(8,128)(2,1)} %refs_1_.7), channel_id=1, source_target_pairs={{0,2},{2,4},{4,6},{6,0},{1,3},{3,5},{5,7},{7,1},{8,10},{10,12},{12... | collective-permute-start | bytes 7077896 | tf_op jit(solution)/shard_map/ppermute | solution.py:318
  2.8 1.5 %collective-permute-start.12 = (bf16[384,3072]{1,0:T(8,128)(2,1)}, bf16[384,3072]{1,0:T(8,128)(2,1)}, u32[]{:S(2)}, u32[]{:S(2)}) collective-permute-start(bf16[384,3072]{1,0:T(8,128)(2,1)} %refs_1_.7), channel_id=1, source_target_pairs={{0,6},{2,0},{4,2},{6,4},{1,7},{3,1},{5,3},{7,5},{8,14},{10,8},{12,... | collective-permute-start | bytes 7077896 | tf_op jit(solution)/shard_map/ppermute | solution.py:318
  4.4 2.5 %prepare.1 = (bf16[256,768]{1,0:T(8,128)(2,1)}, bf16[6,256,256]{2,1,0:T(8,128)(2,1)}) custom-call(bf16[256,384]{1,0:T(8,128)(2,1)} %q_ref.1, bf16[256,384]{1,0:T(8,128)(2,1)} %qt_ref.1, bf16[256,384]{1,0:T(8,128)(2,1)} %k_ref.1, bf16[256,384]{1,0:T(8,128)(2,1)} %kt_ref.1, bf16[256,384]{1,0:T(8,128)(2,1)} %v_ref.1, bf16[256,384]{1,0:T(8,128)(2,1)} %vt_ref.1), custom_call_target="tpu_custom_call" | custom-call | tf_op jit(solution)/shard_map/prepare/pallas_call | solution.py:50
  6.9 5.6 %collective-permute-start.6 = (bf16[6,256,256]{2,1,0:T(8,128)(2,1)}, bf16[6,256,256]{2,1,0:T(8,128)(2,1)}, u32[]{:S(2)}, u32[]{:S(2)}) collective-permute-start(bf16[6,256,256]{2,1,0:T(8,128)(2,1)} %get-tuple-element.23.refs_7_.refs_10_), channel_id=1, source_target_pairs={{0,56},{8,0},{16,8},{24,16},{32,24},{40,32},{48,40},{56,48},{1,57}... | collective-permute-start | bytes 2359304 | tf_op jit(solution)/shard_map/ppermute | solution.py:318
  12.5 0.0 collective-permute-start.3
  12.5 2.5 %collective-permute-start = (bf16[256,768]{1,0:T(8,128)(2,1)}, bf16[256,768]{1,0:T(8,128)(2,1)S(1)}, u32[]{:S(2)}, u32[]{:S(2)}) collective-permute-start(bf16[256,768]{1,0:T(8,128)(2,1)} %get-tuple-element.22.refs_3_), channel_id=1, source_target_pairs={{0,192},{64,0},{128,64},{192,128},{1,193},{65,1},{129,65},{193,129... | collective-permute-start | bytes 1179656 | tf_op jit(solution)/shard_map/ppermute | solution.py:318
  14.9 7.4 %collective-permute-done.refs_4_ = bf16[256,768]{1,0:T(8,128)(2,1)S(1)} collective-permute-done((bf16[256,768]{1,0:T(8,128)(2,1)}, bf16[256,768]{1,0:T(8,128)(2,1)S(1)}, u32[]{:S(2)}, u32[]{:S(2)}) %collective-permute-start) | collective-permute-done | bytes 393248 | tf_op jit(solution)/shard_map/ppermute | solution.py:318
  22.3 0.0 copy-start.3
  22.3 0.9 collective-permute-start.1
  23.2 5.3 %collective-permute-done.6.refs_9_.refs_12_ = bf16[6,256,256]{2,1,0:T(8,128)(2,1)} collective-permute-done((bf16[6,256,256]{2,1,0:T(8,128)(2,1)}, bf16[6,256,256]{2,1,0:T(8,128)(2,1)}, u32[]{:S(2)}, u32[]{:S(2)}) %collective-permute-start.6) | collective-permute-done | bytes 786464 | tf_op jit(solution)/shard_map/ppermute | solution.py:318
  28.5 3.4 %collective-permute-start.7 = (bf16[6,256,256]{2,1,0:T(8,128)(2,1)}, bf16[6,256,256]{2,1,0:T(8,128)(2,1)}, u32[]{:S(2)}, u32[]{:S(2)}) collective-permute-start(bf16[6,256,256]{2,1,0:T(8,128)(2,1)} %collective-permute-done.6.refs_9_.refs_12_), channel_id=1, source_target_pairs={{0,56},{8,0},{16,8},{24,16},{32,24},{40,32},{48,40},{56,48},{1,57}... | collective-permute-start | bytes 2359304 | tf_op jit(solution)/shard_map/ppermute | solution.py:318
  31.9 0.0 collective-permute-done.3.refs_8_.refs_11_
  31.9 0.0 collective-permute-start.4
  31.9 1.3 %collective-permute-done.1.refs_6_ = bf16[256,768]{1,0:T(8,128)(2,1)S(1)} collective-permute-done((bf16[256,768]{1,0:T(8,128)(2,1)}, bf16[256,768]{1,0:T(8,128)(2,1)S(1)}, u32[]{:S(2)}, u32[]{:S(2)}) %collective-permute-start.1) | collective-permute-done | bytes 393248 | tf_op jit(solution)/shard_map/ppermute | solution.py:318
  33.3 0.0 copy-start.4
  33.3 1.5 %collective-permute-start.2 = (bf16[256,768]{1,0:T(8,128)(2,1)}, bf16[256,768]{1,0:T(8,128)(2,1)S(1)}, u32[]{:S(2)}, u32[]{:S(2)}) collective-permute-start(bf16[256,768]{1,0:T(8,128)(2,1)} %get-tuple-element.22.refs_3_), channel_id=1, source_target_pairs={{0,128},{64,192},{128,0},{192,64},{1,129},{65,193},{129,1},{193,65... | collective-permute-start | bytes 1179656 | tf_op jit(solution)/shard_map/ppermute | solution.py:318
  34.8 1.6 %reshape.14.refs_0_ = s32[12288]{0:T(1024)} reshape(s32[3,64,64]{2,1,0:T(8,128)} %param.15) | data formatting | bytes 98304 | tf_op jit(solution)/shard_map/reshape | solution.py:337
  36.4 0.6 pad_add_fusion.refs_2_.place_ref
  37.0 10.1 %collective-permute-done.7.refs_8_.refs_12_ = bf16[6,256,256]{2,1,0:T(8,128)(2,1)} collective-permute-done((bf16[6,256,256]{2,1,0:T(8,128)(2,1)}, bf16[6,256,256]{2,1,0:T(8,128)(2,1)}, u32[]{:S(2)}, u32[]{:S(2)}) %collective-permute-start.7) | collective-permute-done | bytes 786464 | tf_op jit(solution)/shard_map/ppermute | solution.py:318
  47.1 3.4 %collective-permute-start.8 = (bf16[6,256,256]{2,1,0:T(8,128)(2,1)}, bf16[6,256,256]{2,1,0:T(8,128)(2,1)}, u32[]{:S(2)}, u32[]{:S(2)}) collective-permute-start(bf16[6,256,256]{2,1,0:T(8,128)(2,1)} %collective-permute-done.7.refs_8_.refs_12_), channel_id=1, source_target_pairs={{0,56},{8,0},{16,8},{24,16},{32,24},{40,32},{48,40},{56,48},{1,57}... | collective-permute-start | bytes 2359304 | tf_op jit(solution)/shard_map/ppermute | solution.py:318
  50.5 0.0 collective-permute-done.4.refs_7_.refs_11_
  50.5 0.0 collective-permute-start.5
  50.5 0.0 collective-permute-done.2.refs_5_
  50.5 0.0 copy-done.3
  50.5 0.0 copy-done.4
  50.5 0.0 copy-start.5
  50.5 0.7 copy-done.5
  51.3 8.6 %attend.2 = (f32[3,256,1024]{2,1,0:T(8,128)}, f32[3,8,1024]{2,1,0:T(8,128)}) custom-call(s32[12288]{0:T(1024)} %reshape.14.refs_0_, s32[32]{0:T(128)} %refs_1_.6, s32[4]{0:T(128)} %pad_add_fusion.refs_2_.place_ref, bf16[256,768]{1,0:T(8,128)(2,1)} %get-tuple-element.22.refs_3_, bf16[256,768]{1,0:T(8,128)(2,1)} %copy-done.3, bf16[256,768]{1,0:T(8,128)(2,1)} %copy-done.5, ...), custom_call_target="tpu_custom_call" | custom-call | flops 3623878656 | bytes 8388608 | tf_op jit(solution)/shard_map/attend/pallas_call | solution.py:216
  59.9 0.0 collective-permute-done.11.refs_2_
  59.9 0.0 copy-start
  59.9 0.0 collective-permute-done.12.refs_3_
  59.9 0.1 slice.20
  60.0 2.1 %slice.21 = bf16[192,3072]{1,0:T(8,128)(2,1)S(1)} slice(bf16[384,3072]{1,0:T(8,128)(2,1)} %collective-permute-done.12.refs_3_), slice={[192:384], [0:3072]} | slice | bytes 2359296 | tf_op jit(solution)/shard_map/slice | solution.py:362
  62.1 0.0 copy-done
  62.1 1.1 collective-permute-start.14
  63.3 0.4 collective-permute-start.13
  63.7 1.0 collective-permute-done.8.refs_10_.refs_14_
  64.7 3.1 %collective-permute-done.5.refs_9_.refs_13_ = bf16[6,256,256]{2,1,0:T(8,128)(2,1)} collective-permute-done((bf16[6,256,256]{2,1,0:T(8,128)(2,1)}, bf16[6,256,256]{2,1,0:T(8,128)(2,1)}, u32[]{:S(2)}, u32[]{:S(2)}) %collective-permute-start.5) | collective-permute-done | bytes 786464 | tf_op jit(solution)/shard_map/ppermute | solution.py:318
  67.8 1.0 slice.18
  68.9 1.0 slice.19
  69.9 0.4 collective-permute-start.10
  70.2 1.2 collective-permute-start.9
  71.4 10.8 %attend.3 = (f32[3,256,1024]{2,1,0:T(8,128)}, f32[3,8,1024]{2,1,0:T(8,128)}) custom-call(s32[12288]{0:T(1024)} %reshape.14.refs_0_, s32[32]{0:T(128)} %refs_1_.6, s32[4]{0:T(128)} %pad_add_fusion.refs_2_.place_ref, bf16[256,768]{1,0:T(8,128)(2,1)} %get-tuple-element.22.refs_3_, bf16[256,768]{1,0:T(8,128)(2,1)} %copy-done.3, bf16[256,768]{1,0:T(8,128)(2,1)} %copy-done.5, ...), custom_call_target="tpu_custom_call" | custom-call | flops 4831838208 | bytes 8388608 | tf_op jit(solution)/shard_map/attend/pallas_call | solution.py:216
  82.2 0.0 collective-permute-done.10.refs_8_
  82.3 0.0 copy-start.6
  82.3 0.0 collective-permute-done.9.refs_7_
  82.3 0.0 copy-start.7
  82.3 0.7 copy-done.6
  83.0 0.2 copy-done.7
  83.2 6.6 %attend_last.1 = bf16[4,256,896]{2,1,0:T(8,128)(2,1)} custom-call(s32[12288]{0:T(1024)} %reshape.14.refs_0_, s32[32]{0:T(128)} %refs_1_.6, s32[4]{0:T(128)} %pad_add_fusion.refs_2_.place_ref, bf16[256,768]{1,0:T(8,128)(2,1)} %get-tuple-element.22.refs_3_, bf16[256,768]{1,0:T(8,128)(2,1)} %copy-done.3, bf16[256,768]{1,0:T(8,128)(2,1)} %copy-done.5, ...), custom_call_target="tpu_custom_call" | custom-call | flops 1207959552 | bytes 8388608 | tf_op jit(solution)/shard_map/attend_last/pallas_call | solution.py:216
  89.7 0.0 collective-permute-done.14.refs_5_
  89.7 0.0 copy-start.1
  89.8 0.0 collective-permute-done.13.refs_4_
  89.8 0.0 copy-start.2
  89.8 25.3 %all_to_all.5.refs_0_ = bf16[16,64,896]{2,1,0:T(8,128)(2,1)} all-to-all(bf16[16,64,896]{2,1,0:T(8,128)(2,1)} %bitcast.15), channel_id=1, replica_groups=mesh['x'=4,'z'=8,'y'=4,'c'=2] {'x','y'}, dimensions={0} | all-to-all | bytes 3670016 | tf_op jit(solution)/shard_map/all_to_all | solution.py:372
  115.0 0.0 copy-done.1
  115.0 0.0 copy-done.2
  115.0 6.8 %project.1 = (f32[32,3072]{1,0:T(8,128)}, f32[32,3072]{1,0:T(8,128)}, bf16[2,32,3072]{2,1,0:T(8,128)(2,1)}) custom-call(s32[4]{0:T(128)} %pad_add_fusion.refs_2_.place_ref, bf16[16,64,896]{2,1,0:T(8,128)(2,1)} %all_to_all.5.refs_0_, bf16[384,3072]{1,0:T(8,128)(2,1)} %refs_1_.7, bf16[384,3072]{1,0:T(8,128)(2,1)} %copy-done, ...), custom_call_target="tpu_custom_call" | custom-call | tf_op jit(solution)/shard_map/project/pallas_call | solution.py:301
  121.8 6.2 %collective-permute-start.15 = (bf16[2,32,3072]{2,1,0:T(8,128)(2,1)}, bf16[2,32,3072]{2,1,0:T(8,128)(2,1)S(1)}, u32[]{:S(2)}, u32[]{:S(2)}) collective-permute-start(bf16[2,32,3072]{2,1,0:T(8,128)(2,1)} %get-tuple-element.36), channel_id=1, source_target_pairs={{0,1},{1,0},{2,3},{3,2},{4,5},{5,4},{6,7},{7,6},{8,9},{9,8},{10,11... | collective-permute-start | bytes 1179656 | tf_op jit(solution)/shard_map/ppermute | solution.py:377
  128.1 1.6 %collective-permute-done.15 = bf16[2,32,3072]{2,1,0:T(8,128)(2,1)S(1)} collective-permute-done((bf16[2,32,3072]{2,1,0:T(8,128)(2,1)}, bf16[2,32,3072]{2,1,0:T(8,128)(2,1)S(1)}, u32[]{:S(2)}, u32[]{:S(2)}) %collective-permute-start.15) | collective-permute-done | bytes 393248 | tf_op jit(solution)/shard_map/ppermute | solution.py:377
  129.6 1.9 %fusion = (bf16[32,3072]{1,0:T(8,128)(2,1)}, bf16[32,3072]{1,0:T(8,128)(2,1)}) fusion(f32[32,3072]{1,0:T(8,128)} %get-tuple-element.37, bf16[2,32,3072]{2,1,0:T(8,128)(2,1)S(1)} %collective-permute-done.15, f32[32,3072]{1,0:T(8,128)} %get-tuple-element.35), kind=kLoop, calls=%fused_computation.1 | loop fusion | flops 589824 | bytes 1572864 | tf_op jit(solution)/shard_map/convert_element_type | solution.py:379
Async XLA Ops:
  0.6 59.3 %collective-permute-start.11 = (bf16[384,3072]{1,0:T(8,128)(2,1)}, bf16[384,3072]{1,0:T(8,128)(2,1)S(1)}, u32[]{:S(2)}, u32[]{:S(2)}) collective-permute-start(bf16[384,3072]{1,0:T(8,128)(2,1)} %refs_1_.7), channel_id=1, source_target_pairs={{0,2},{2,4},{4,6},{6,0},{1,3},{3,5},{5,7},{7,1},{8,10},{10,12},{12... | collective-permute-start | bytes 7077896 | tf_op jit(solution)/shard_map/ppermute | solution.py:318
  2.8 57.1 %collective-permute-start.12 = (bf16[384,3072]{1,0:T(8,128)(2,1)}, bf16[384,3072]{1,0:T(8,128)(2,1)}, u32[]{:S(2)}, u32[]{:S(2)}) collective-permute-start(bf16[384,3072]{1,0:T(8,128)(2,1)} %refs_1_.7), channel_id=1, source_target_pairs={{0,6},{2,0},{4,2},{6,4},{1,7},{3,1},{5,3},{7,5},{8,14},{10,8},{12,... | collective-permute-start | bytes 7077896 | tf_op jit(solution)/shard_map/ppermute | solution.py:318
  6.9 21.6 %collective-permute-start.6 = (bf16[6,256,256]{2,1,0:T(8,128)(2,1)}, bf16[6,256,256]{2,1,0:T(8,128)(2,1)}, u32[]{:S(2)}, u32[]{:S(2)}) collective-permute-start(bf16[6,256,256]{2,1,0:T(8,128)(2,1)} %get-tuple-element.23.refs_7_.refs_10_), channel_id=1, source_target_pairs={{0,56},{8,0},{16,8},{24,16},{32,24},{40,32},{48,40},{56,48},{1,57}... | collective-permute-start | bytes 2359304 | tf_op jit(solution)/shard_map/ppermute | solution.py:318
  12.5 19.5 %collective-permute-start.3 = (bf16[6,256,256]{2,1,0:T(8,128)(2,1)}, bf16[6,256,256]{2,1,0:T(8,128)(2,1)}, u32[]{:S(2)}, u32[]{:S(2)}) collective-permute-start(bf16[6,256,256]{2,1,0:T(8,128)(2,1)} %get-tuple-element.23.refs_7_.refs_10_), channel_id=1, source_target_pairs={{0,8},{8,16},{16,24},{24,32},{32,40},{40,48},{48,56},{56,0},{1,9},... | collective-permute-start | bytes 2359304 | tf_op jit(solution)/shard_map/ppermute | solution.py:318
  12.5 9.8 %collective-permute-start = (bf16[256,768]{1,0:T(8,128)(2,1)}, bf16[256,768]{1,0:T(8,128)(2,1)S(1)}, u32[]{:S(2)}, u32[]{:S(2)}) collective-permute-start(bf16[256,768]{1,0:T(8,128)(2,1)} %get-tuple-element.22.refs_3_), channel_id=1, source_target_pairs={{0,192},{64,0},{128,64},{192,128},{1,193},{65,1},{129,65},{193,129... | collective-permute-start | bytes 1179656 | tf_op jit(solution)/shard_map/ppermute | solution.py:318
  22.3 28.2 %copy-start.3 = (bf16[256,768]{1,0:T(8,128)(2,1)}, bf16[256,768]{1,0:T(8,128)(2,1)S(1)}, u32[]{:S(2)}) copy-start(bf16[256,768]{1,0:T(8,128)(2,1)S(1)} %collective-permute-done.refs_4_) | copy-start | bytes 1179652
  22.3 11.0 %collective-permute-start.1 = (bf16[256,768]{1,0:T(8,128)(2,1)}, bf16[256,768]{1,0:T(8,128)(2,1)S(1)}, u32[]{:S(2)}, u32[]{:S(2)}) collective-permute-start(bf16[256,768]{1,0:T(8,128)(2,1)} %get-tuple-element.22.refs_3_), channel_id=1, source_target_pairs={{0,64},{64,128},{128,192},{192,0},{1,65},{65,129},{129,193},{193,1... | collective-permute-start | bytes 1179656 | tf_op jit(solution)/shard_map/ppermute | solution.py:318
  28.5 18.6 %collective-permute-start.7 = (bf16[6,256,256]{2,1,0:T(8,128)(2,1)}, bf16[6,256,256]{2,1,0:T(8,128)(2,1)}, u32[]{:S(2)}, u32[]{:S(2)}) collective-permute-start(bf16[6,256,256]{2,1,0:T(8,128)(2,1)} %collective-permute-done.6.refs_9_.refs_12_), channel_id=1, source_target_pairs={{0,56},{8,0},{16,8},{24,16},{32,24},{40,32},{48,40},{56,48},{1,57}... | collective-permute-start | bytes 2359304 | tf_op jit(solution)/shard_map/ppermute | solution.py:318
  31.9 18.6 %collective-permute-start.4 = (bf16[6,256,256]{2,1,0:T(8,128)(2,1)}, bf16[6,256,256]{2,1,0:T(8,128)(2,1)}, u32[]{:S(2)}, u32[]{:S(2)}) collective-permute-start(bf16[6,256,256]{2,1,0:T(8,128)(2,1)} %collective-permute-done.3.refs_8_.refs_11_), channel_id=1, source_target_pairs={{0,8},{8,16},{16,24},{24,32},{32,40},{40,48},{48,56},{56,0},{1,9},... | collective-permute-start | bytes 2359304 | tf_op jit(solution)/shard_map/ppermute | solution.py:318
  33.3 17.2 %copy-start.4 = (bf16[256,768]{1,0:T(8,128)(2,1)}, bf16[256,768]{1,0:T(8,128)(2,1)S(1)}, u32[]{:S(2)}) copy-start(bf16[256,768]{1,0:T(8,128)(2,1)S(1)} %collective-permute-done.1.refs_6_) | copy-start | bytes 1179652
  33.3 17.2 %collective-permute-start.2 = (bf16[256,768]{1,0:T(8,128)(2,1)}, bf16[256,768]{1,0:T(8,128)(2,1)S(1)}, u32[]{:S(2)}, u32[]{:S(2)}) collective-permute-start(bf16[256,768]{1,0:T(8,128)(2,1)} %get-tuple-element.22.refs_3_), channel_id=1, source_target_pairs={{0,128},{64,192},{128,0},{192,64},{1,129},{65,193},{129,1},{193,65... | collective-permute-start | bytes 1179656 | tf_op jit(solution)/shard_map/ppermute | solution.py:318
  47.1 17.6 %collective-permute-start.8 = (bf16[6,256,256]{2,1,0:T(8,128)(2,1)}, bf16[6,256,256]{2,1,0:T(8,128)(2,1)}, u32[]{:S(2)}, u32[]{:S(2)}) collective-permute-start(bf16[6,256,256]{2,1,0:T(8,128)(2,1)} %collective-permute-done.7.refs_8_.refs_12_), channel_id=1, source_target_pairs={{0,56},{8,0},{16,8},{24,16},{32,24},{40,32},{48,40},{56,48},{1,57}... | collective-permute-start | bytes 2359304 | tf_op jit(solution)/shard_map/ppermute | solution.py:318
  50.5 17.4 %collective-permute-start.5 = (bf16[6,256,256]{2,1,0:T(8,128)(2,1)}, bf16[6,256,256]{2,1,0:T(8,128)(2,1)}, u32[]{:S(2)}, u32[]{:S(2)}) collective-permute-start(bf16[6,256,256]{2,1,0:T(8,128)(2,1)} %collective-permute-done.4.refs_7_.refs_11_), channel_id=1, source_target_pairs={{0,8},{8,16},{16,24},{24,32},{32,40},{40,48},{48,56},{56,0},{1,9},... | collective-permute-start | bytes 2359304 | tf_op jit(solution)/shard_map/ppermute | solution.py:318
  50.5 0.7 copy-start.5
  59.9 2.2 %copy-start = (bf16[384,3072]{1,0:T(8,128)(2,1)}, bf16[384,3072]{1,0:T(8,128)(2,1)S(1)}, u32[]{:S(2)}) copy-start(bf16[384,3072]{1,0:T(8,128)(2,1)S(1)} %collective-permute-done.11.refs_2_) | copy-start | bytes 7077892
  62.1 27.6 %collective-permute-start.14 = (bf16[192,3072]{1,0:T(8,128)(2,1)S(1)}, bf16[192,3072]{1,0:T(8,128)(2,1)S(1)}, u32[]{:S(2)}, u32[]{:S(2)}) collective-permute-start(bf16[192,3072]{1,0:T(8,128)(2,1)S(1)} %slice.21), channel_id=1, source_target_pairs={{0,6},{2,0},{4,2},{6,4},{1,7},{3,1},{5,3},{7,5},{8,14},{10,8},{12,... | collective-permute-start | bytes 3538952 | tf_op jit(solution)/shard_map/ppermute | solution.py:318
  63.3 26.5 %collective-permute-start.13 = (bf16[192,3072]{1,0:T(8,128)(2,1)S(1)}, bf16[192,3072]{1,0:T(8,128)(2,1)S(1)}, u32[]{:S(2)}, u32[]{:S(2)}) collective-permute-start(bf16[192,3072]{1,0:T(8,128)(2,1)S(1)} %slice.20), channel_id=1, source_target_pairs={{0,2},{2,4},{4,6},{6,0},{1,3},{3,5},{5,7},{7,1},{8,10},{10,12},{12... | collective-permute-start | bytes 3538952 | tf_op jit(solution)/shard_map/ppermute | solution.py:318
  69.9 12.4 %collective-permute-start.10 = (bf16[3,256,256]{2,1,0:T(8,128)(2,1)S(1)}, bf16[3,256,256]{2,1,0:T(8,128)(2,1)S(1)}, u32[]{:S(2)}, u32[]{:S(2)}) collective-permute-start(bf16[3,256,256]{2,1,0:T(8,128)(2,1)S(1)} %slice.19), channel_id=1, source_target_pairs={{0,56},{8,0},{16,8},{24,16},{32,24},{40,32},{48,40},{56,48},{1,57}... | collective-permute-start | bytes 1179656 | tf_op jit(solution)/shard_map/ppermute | solution.py:318
  70.2 12.0 %collective-permute-start.9 = (bf16[3,256,256]{2,1,0:T(8,128)(2,1)S(1)}, bf16[3,256,256]{2,1,0:T(8,128)(2,1)S(1)}, u32[]{:S(2)}, u32[]{:S(2)}) collective-permute-start(bf16[3,256,256]{2,1,0:T(8,128)(2,1)S(1)} %slice.18), channel_id=1, source_target_pairs={{0,8},{8,16},{16,24},{24,32},{32,40},{40,48},{48,56},{56,0},{1,9},... | collective-permute-start | bytes 1179656 | tf_op jit(solution)/shard_map/ppermute | solution.py:318
  82.3 0.8 copy-start.6
  82.3 0.9 copy-start.7
  89.7 25.3 %copy-start.1 = (bf16[192,3072]{1,0:T(8,128)(2,1)}, bf16[192,3072]{1,0:T(8,128)(2,1)S(1)}, u32[]{:S(2)}) copy-start(bf16[192,3072]{1,0:T(8,128)(2,1)S(1)} %collective-permute-done.14.refs_5_) | copy-start | bytes 3538948
  89.8 25.3 %copy-start.2 = (bf16[192,3072]{1,0:T(8,128)(2,1)}, bf16[192,3072]{1,0:T(8,128)(2,1)S(1)}, u32[]{:S(2)}) copy-start(bf16[192,3072]{1,0:T(8,128)(2,1)S(1)} %collective-permute-done.13.refs_4_) | copy-start | bytes 3538948
  121.8 7.8 %collective-permute-start.15 = (bf16[2,32,3072]{2,1,0:T(8,128)(2,1)}, bf16[2,32,3072]{2,1,0:T(8,128)(2,1)S(1)}, u32[]{:S(2)}, u32[]{:S(2)}) collective-permute-start(bf16[2,32,3072]{2,1,0:T(8,128)(2,1)} %get-tuple-element.36), channel_id=1, source_target_pairs={{0,1},{1,0},{2,3},{3,2},{4,5},{5,4},{6,7},{7,6},{8,9},{9,8},{10,11... | collective-permute-start | bytes 1179656 | tf_op jit(solution)/shard_map/ppermute | solution.py:377
